TPU v7x, 32 devices: a whole 2x2x4 slice. The times are simulated.
32 devices in a mesh: row: 8 (over z, y), col: 4 (over x, core).
Axes of the slice: x: 2, y: 2, z: 4, core: 2. Of those that a mesh axis runs over, the one named last changes fastest.
Arguments:
- amplitudes: bfloat16 [1024, 32768], P('row', 'col'), may hold values from -6 to 6
- amp_mask: int32 [32, 128], P('row', 'col'), may hold values from 0 to 1, as said below
- integrals: bfloat16 [16384, 32768], P('row', 'col'), may hold values from -0.0625 to 0.0625
- int_mask: int32 [64, 128], P('row', 'col'), may hold values 0 or 1
- occ_energy: float32 [1024], P('col'), may hold values from -1.5 to -0.5
- vir_energy: float32 [16384], P('row'), may hold values from 0.5 to 1.5
Outputs:
- residual: bfloat16 [1024, 16384], P('col', 'row')
Inputs may be any that keep to these rules, and one draw needn't show every extreme that they name: In every row of amp_mask, each aligned group of 8 consecutive entries holds exactly 4 ones.
All inputs are finite; a program needn't handle non-finite values. No bound on the sum of `int_mask` on one device may be relied on, other than what follows from the above.
Results may differ from a plain program's by a relative error of at most 0.001.
Values may be sent and summed in bfloat16 or wider, within the bound.
No kernel may reach another device: no remote copies, remote signals or barrier semaphores. Data moves between devices by JAX's collectives and lax.ppermute only.
A program may use at most 192 MiB of HBM per device.

v0:
```python
import jax
import jax.numpy as jnp
from jax import lax
from jax.sharding import PartitionSpec as P

TILE = 256
IJ_BLK = 32


def expand_tiles(values, keep, rows_tile, cols_tile):
    nrow, ncol = keep.shape
    shaped = values.reshape(nrow, rows_tile, ncol, cols_tile)
    return (shaped * keep.astype(values.dtype)[:, None, :, None]).reshape(values.shape)


def contract(left, right):
    return lax.dot_general(
        left, right, (((1,), (1,)), ((), ())), preferred_element_type=jnp.float32
    )


def placement(mask, slots):
    rank = jnp.cumsum(mask, axis=1) - 1
    wanted = jnp.arange(slots, dtype=jnp.int32)[None, :, None]
    chosen = (mask[:, None, :] == 1) & (rank[:, None, :] == wanted)
    return chosen.astype(jnp.bfloat16)


def whole_sum(partial_value):
    return lax.psum_scatter(partial_value, "col", scatter_dimension=0, tiled=True)


def body(amplitudes, amp_mask, integrals, int_mask, occ_energy, vir_energy):
    int_used = expand_tiles(integrals, int_mask, TILE, TILE)
    nblock, ntile = amp_mask.shape
    slots = ntile // 2
    chosen = placement(amp_mask, slots)
    shaped = amplitudes.reshape(nblock, IJ_BLK, ntile, TILE)
    packed = jnp.einsum(
        "bitx,bkt->bikx", shaped, chosen, preferred_element_type=jnp.float32
    ).astype(jnp.bfloat16)
    packed = packed.reshape(nblock * IJ_BLK, slots * TILE)
    got_rows, got_place = (
        lax.all_gather(packed, "row", axis=0, tiled=True),
        lax.all_gather(chosen, "row", axis=0, tiled=True),
    )
    nall = got_place.shape[0]
    unpacked = jnp.einsum(
        "bikx,bkt->bitx",
        got_rows.reshape(nall, IJ_BLK, slots, TILE),
        got_place,
        preferred_element_type=jnp.float32,
    )
    gathered = unpacked.astype(jnp.bfloat16).reshape(nall * IJ_BLK, ntile * TILE)
    ladder = whole_sum(contract(gathered, int_used))
    denom = vir_energy[None, :] - occ_energy[:, None]
    return (ladder / denom).astype(jnp.bfloat16)


def solution(mesh):
    return jax.shard_map(
        body,
        mesh=mesh,
        in_specs=(
            P("row", "col"),
            P("row", "col"),
            P("row", "col"),
            P("row", "col"),
            P("col"),
            P("row"),
        ),
        out_specs=P("col", "row"),
        check_vma=False,
    )
```

profile of v0, /device:TPU:0, one launch (start us, length us, event | category | flops | bytes accessed | tf_op | source)
XLA Modules:
  0.0 304.8 jit_solution(13964555475023240197)
XLA Ops:
  6.5 0.0 all-gather.2.cloned.1.call-start
  6.5 0.7 broadcast_compare_fusion
  7.2 0.9 reduce_window_sum.11
  8.1 2.2 copy.9
  10.3 0.4 fusion.5
  10.7 1.4 copy.10
  12.1 0.0 all-gather.2.cloned.1.call-update
  12.2 0.0 reduce-scatter.2.cloned.1.call-start
  12.2 0.7 convert_element_type.26
  12.9 11.2 %mul.11 = bf16[8,256,32,256]{3,2,1,0:T(8,128)(2,1)} broadcast(bf16[8,32]{1,0:T(8,128)(2,1)S(1)} %convert_element_type.26), dimensions={0,2} | broadcast | bytes 33554944 | tf_op jit(solution)/shard_map/mul | solution.py:13
  24.1 31.3 %copy.13 = bf16[256,8,32,256]{3,1,2,0:T(8,128)(2,1)} copy(bf16[256,8,32,256]{3,2,1,0:T(8,128)(2,1)} %bitcast.38) | data formatting | bytes 67108864
  55.4 33.3 %all_gather.6 = bf16[32,16,32]{2,1,0:T(8,128)(2,1)S(1)} all-gather(bf16[4,16,32]{2,1,0:T(8,128)(2,1)S(1)} %fusion.11), channel_id=1, replica_groups=mesh['row'=8,'col'=4] {'row'}, dimensions={0}, use_global_device_ids=true | all-gather | bytes 36864 | tf_op jit(solution)/shard_map/all_gather | solution.py:45
  88.8 52.8 %all-gather.2.cloned.1.call-done = bf16[1024,4096]{1,0:T(8,128)(2,1)} async-done(((bf16[128,4096]{1,0:T(8,128)(2,1)}), bf16[1024,4096]{1,0:T(8,128)(2,1)}) %all-gather.2.cloned.1.call-update) | async-done | bytes 8388624 | tf_op jit(solution)/shard_map/all_gather | solution.py:44
  141.5 9.7 %copy.11 = bf16[128,8,16,256]{3,2,1,0:T(8,128)(2,1)} copy(bf16[128,8,16,256]{3,1,2,0:T(8,128)(2,1)} %bitcast.43) | data formatting | bytes 16777216
  151.2 10.3 %convolution_convert_fusion = bf16[32,32,32,256]{3,1,2,0:T(8,128)(2,1)} fusion(bf16[32,16,32]{2,1,0:T(8,128)(2,1)S(1)} %all_gather.6, bf16[32,32,16,256]{3,2,1,0:T(8,128)(2,1)} %bitcast.40), kind=kOutput, calls=%fused_computation.2 | convolution fusion | flops 276824064 | bytes 25198592 | tf_op jit(solution)/shard_map/bikx,bkt->bitx/dot_general | solution.py:48
  161.5 17.8 %copy.12 = bf16[128,8,32,256]{3,1,2,0:T(8,128)(2,1)} copy(bf16[128,8,32,256]{3,2,1,0:T(8,128)(2,1)} %bitcast.39) | data formatting | bytes 33554432
  179.3 0.0 copy-start
  179.3 0.0 copy-start.1
  179.3 45.7 %fusion = f32[1024,2048]{1,0:T(8,128)} fusion(bf16[1024,8192]{1,0:T(8,128)(2,1)} %bitcast.42, bf16[2048,8192]{1,0:T(8,128)(2,1)} %param.8, bf16[2048,8192]{1,0:T(8,128)(2,1)} %bitcast.41), kind=kOutput, calls=%fused_computation | convolution fusion | flops 34376515584 | bytes 92274688 | tf_op jit(solution)/shard_map/dot_general | solution.py:17
  225.0 0.0 reduce-scatter.2.cloned.1.call-update
  225.1 70.0 %reduce-scatter.2.cloned.1.call-done = f32[256,2048]{1,0:T(8,128)} async-done(((f32[1024,2048]{1,0:T(8,128)}), f32[256,2048]{1,0:T(8,128)}) %reduce-scatter.2.cloned.1.call-update) | async-done | bytes 2097168 | tf_op jit(solution)/shard_map/reduce_scatter | solution.py:30
  295.1 0.0 copy-done
  295.1 0.0 copy-done.1
  295.1 2.9 divide_convert_fusion
  (2 shorter events, 0.0 us)
Async XLA Ops:
  6.5 135.0 %all-gather.2.cloned.1.call-start = ((), (), s32[]{:S(2)}) async-start(), calls=%async_computation.1 | async-start | bytes 9437184 | tf_op jit(solution)/shard_map/all_gather | solution.py:44
  12.2 282.9 %reduce-scatter.2.cloned.1.call-start = ((), (), s32[]{:S(2)}) async-start(), calls=%async_computation.2 | async-start | bytes 10485760 | tf_op jit(solution)/shard_map/reduce_scatter | solution.py:30
  179.3 115.8 %copy-start = (f32[2048]{0:T(1024)S(1)}, f32[2048]{0:T(1024)}, u32[]{:S(2)}) copy-start(f32[2048]{0:T(1024)} %param.11) | copy-start | bytes 24580
  179.3 115.8 %copy-start.1 = (f32[256]{0:T(256)S(1)}, f32[256]{0:T(256)}, u32[]{:S(2)}) copy-start(f32[256]{0:T(256)} %param.10) | copy-start | bytes 3076
Sparse Core Ops, SparseCore 0:
  12.3 129.2 all-gather.1
  225.2 69.8 reduce-scatter.1
where the time goes:
time: 305 us
  waiting for transfers between devices  123 us (40%)
  local copies, waits for them, and re-layouts  73.6 us (24%)
  matrix products  56.4 us (18%)
  blocking collectives  33.3 us (11%)
  between operations  13.4 us (4%)
  other arithmetic  5.18 us (2%)
    reduce_scatter x1, waiting for transfers between devices, whole_sum(): lax.psum_scatter(partial_value, 'col', scatter_dimension=0, tiled=True)  70 us
    unnamed x9, local copies, waits for them, and re-layouts  62.4 us
    all_gather x1, waiting for transfers between devices, body(): lax.all_gather(packed, 'row', axis=0, tiled=True)  52.8 us
    dot_general x1, matrix products, contract(): lax.dot_general(left, right, (((1,), (1,)), ((), ())), preferred_element_...  45.7 us
    all_gather x1, blocking collectives, body(): lax.all_gather(chosen, 'row', axis=0, tiled=True)  33.3 us
    mul x1, local copies, waits for them, and re-layouts, expand_tiles(): shaped * keep.astype(values.dtype)[:, None, :, None]  11.2 us
    dot_general x1, matrix products, body(): jnp.einsum('bikx,bkt->bitx', got_rows.reshape(nall, IJ_BLK, slots, TILE),...  10.3 us
  transfers between devices with their start and end apart: 2, of which 2 were waited for; matrix products, arithmetic and copies ran while one was open for 14% of the time, Pallas kernels for 0%

commit v1 on v0

v1 whole, which is shorter than its diff:
```python
import functools

import jax
import jax.numpy as jnp
from jax import lax
from jax.experimental import pallas as pl
from jax.experimental.pallas import tpu as pltpu
from jax.sharding import PartitionSpec as P

TILE = 256
IJ_BLK = 32
GRP = 8
KEPT = GRP // 2
LANES = 128
META = 16
PIECE = 2 * IJ_BLK
FLOWS = 4
NBUF = 12
TOP = 32000.0
OCTAVE = 64.0
LN2 = 0.6931471805599453
FLOOR = 1e-30
VMEM = pltpu.VMEM
SMEM = pltpu.SMEM


def vmem():
    return pl.BlockSpec(memory_space=VMEM)


def smem():
    return pl.BlockSpec(memory_space=SMEM)


def pack_kernel(mask_ref, amp_ref, *outs):
    nblock, ntile = mask_ref.shape
    per = nblock // FLOWS
    groups = ntile // GRP
    slots = groups * KEPT
    lane = lax.broadcasted_iota(jnp.int32, (META, LANES), 1)
    for flow in range(FLOWS):
        out = outs[flow]
        meta = jnp.zeros((META, LANES), jnp.int32)
        for q in range(per):
            block = flow * per + q
            rows = slice(block * IJ_BLK, (block + 1) * IJ_BLK)
            for g in range(groups):
                count, bits = jnp.int32(0), jnp.int32(0)
                for j in range(GRP):
                    t = g * GRP + j
                    here = mask_ref[block, t]
                    base = (q * slots + g * KEPT + count) * PIECE

                    @pl.when(here == 1)
                    def _():
                        for half in range(2):
                            at = pl.multiple_of(base + half * IJ_BLK, IJ_BLK)
                            out[pl.ds(at, IJ_BLK), :] = amp_ref[
                                rows,
                                t * TILE + half * LANES : t * TILE + (half + 1) * LANES,
                            ]

                    count += here
                    bits += here << j
                meta = jnp.where(lane == q * groups + g, bits, meta)
        out[per * slots * PIECE :, :] = meta.astype(jnp.float32).astype(jnp.bfloat16)


def pack(amplitudes, amp_mask):
    nblock, ntile = amp_mask.shape
    rows = nblock // FLOWS * (ntile // 2) * PIECE + META
    return pl.pallas_call(
        pack_kernel,
        out_shape=[jax.ShapeDtypeStruct((rows, LANES), jnp.bfloat16)] * FLOWS,
        in_specs=[smem(), vmem()],
        out_specs=[vmem()] * FLOWS,
        compiler_params=pltpu.CompilerParams(vmem_limit_bytes=16 * 2**20),
        name="pack",
    )(amp_mask, amplitudes)


def list_kernel(half_ref, mask_ref, list_ref, off_ref):
    nab, ntile = mask_ref.shape
    first = (1 - half_ref[0]) * (nab // 2)

    def row(ii, count):
        i = lax.rem(ii + first, nab)
        off_ref[ii] = count

        def col(t, count):
            list_ref[count] = i * ntile + t
            return count + mask_ref[i, t]

        return lax.fori_loop(0, ntile, col, count)

    off_ref[nab] = lax.fori_loop(0, nab, row, jnp.int32(0))


def make_list(half, int_mask):
    nab, ntile = int_mask.shape
    return pl.pallas_call(
        list_kernel,
        out_shape=[
            jax.ShapeDtypeStruct((nab * ntile + 1,), jnp.int32),
            jax.ShapeDtypeStruct((nab + 1,), jnp.int32),
        ],
        in_specs=[smem(), smem()],
        out_specs=[smem(), smem()],
        name="tile_list",
    )(half, int_mask)


def ladder_kernel(
    nchunk, per, ntile, list_ref, off_ref, int_ref, *rest
):
    chunks, (other_ref, mine_ref), scratch = (
        rest[:nchunk],
        rest[nchunk : nchunk + 2],
        rest[nchunk + 2 :],
    )
    dense, bufs, meta_v, meta_s, sems, meta_sem = scratch
    nab = off_ref.shape[0] - 1
    groups = ntile // GRP
    slots = groups * KEPT
    total = off_ref[nab]

    def fetch(n):
        at = list_ref[n]
        i, t = at // ntile, lax.rem(at, ntile)
        slot = lax.rem(n, NBUF)
        return pltpu.make_async_copy(
            int_ref.at[
                pl.ds(pl.multiple_of(i * TILE, TILE), TILE),
                pl.ds(pl.multiple_of(t * TILE, TILE), TILE),
            ],
            bufs.at[slot],
            sems.at[slot],
        )

    for n in range(NBUF):

        @pl.when(n < total)
        def _():
            fetch(n).start()

    for c in range(nchunk):
        head = chunks[c][per * slots * PIECE :, :].astype(jnp.float32)
        meta_v[c * 8 : (c + 1) * 8, :] = head[:8].astype(jnp.int32)
    copy = pltpu.make_async_copy(meta_v, meta_s, meta_sem)
    copy.start()
    copy.wait()
    zero = jnp.zeros((IJ_BLK, LANES), jnp.bfloat16)
    for c in range(nchunk):
        for q in range(per):
            row = (c * per + q) * IJ_BLK
            for g in range(groups):
                bits = meta_s[c * 8, q * groups + g]
                count = jnp.int32(0)
                for j in range(GRP):
                    here = (bits >> j) & 1
                    base = (
                        q * slots + g * KEPT + jnp.minimum(count, KEPT - 1)
                    ) * PIECE
                    for half in range(2):
                        at = pl.multiple_of(base + half * IJ_BLK, IJ_BLK)
                        tile = chunks[c][pl.ds(at, IJ_BLK), :]
                        dense[
                            g * GRP + j,
                            row : row + IJ_BLK,
                            half * LANES : (half + 1) * LANES,
                        ] = jnp.where(here == 1, tile, zero)
                    count += here

    for ii in range(nab):
        out = other_ref if ii < nab // 2 else mine_ref
        cols = slice((ii % (nab // 2)) * TILE, (ii % (nab // 2) + 1) * TILE)
        out[:, cols] = jnp.zeros((out.shape[0], TILE), jnp.float32)

        def step(n, carry):
            slot = lax.rem(n, NBUF)
            t = lax.rem(list_ref[n], ntile)
            fetch(n).wait()
            out[:, cols] += lax.dot_general(
                dense[t],
                bufs[slot],
                (((1,), (1,)), ((), ())),
                preferred_element_type=jnp.float32,
            )

            @pl.when(n + NBUF < total)
            def _():
                fetch(n + NBUF).start()

            return carry

        lax.fori_loop(off_ref[ii], off_ref[ii + 1], step, 0)


def ladder(chunks, tile_list, offsets, integrals):
    nchunk = len(chunks)
    rows_ab, rows_cd = integrals.shape
    ntile = rows_cd // TILE
    per = (chunks[0].shape[0] - META) // (ntile // 2 * PIECE)
    m = nchunk * per * IJ_BLK
    out = jax.ShapeDtypeStruct((m, rows_ab // 2), jnp.float32)
    return pl.pallas_call(
        functools.partial(ladder_kernel, nchunk, per, ntile),
        out_shape=[out, out],
        in_specs=[smem(), smem(), pl.BlockSpec(memory_space=pl.ANY)]
        + [vmem()] * nchunk,
        out_specs=[vmem(), vmem()],
        scratch_shapes=[
            VMEM((ntile, m, TILE), jnp.bfloat16),
            VMEM((NBUF, TILE, TILE), jnp.bfloat16),
            VMEM((nchunk * 8, LANES), jnp.int32),
            SMEM((nchunk * 8, LANES), jnp.int32),
            pltpu.SemaphoreType.DMA((NBUF,)),
            pltpu.SemaphoreType.DMA,
        ],
        compiler_params=pltpu.CompilerParams(vmem_limit_bytes=24 * 2**20),
        cost_estimate=pl.CostEstimate(
            flops=m * rows_ab * rows_cd,
            bytes_accessed=rows_ab * rows_cd,
            transcendentals=0,
        ),
        name="ladder",
    )(tile_list, offsets, integrals, *chunks)


def code_kernel(mine_ref, got_ref, sum_ref, code_ref):
    rows, width = mine_ref.shape

    def step(b, carry):
        at = pl.ds(pl.multiple_of(b * IJ_BLK, IJ_BLK), IJ_BLK)
        total = mine_ref[at, :] + got_ref[at, :]
        sum_ref[at, :] = total
        peak = jnp.max(jnp.abs(total), axis=1, keepdims=True)
        level = jnp.ceil(jnp.log(jnp.maximum(peak, FLOOR)) * (OCTAVE / LN2))
        up = jnp.exp(level * (-LN2 / OCTAVE)) * TOP
        code_ref[at, :width] = (
            jnp.round(total * up).astype(jnp.int32).astype(jnp.int16)
        )
        code_ref[at, width:] = jnp.broadcast_to(
            level.astype(jnp.int32), (IJ_BLK, LANES)
        ).astype(jnp.int16)
        return carry

    lax.fori_loop(0, rows // IJ_BLK, step, 0)


def code(mine, got):
    rows, width = mine.shape
    return pl.pallas_call(
        code_kernel,
        out_shape=[
            jax.ShapeDtypeStruct((rows, width), jnp.float32),
            jax.ShapeDtypeStruct((rows, width + LANES), jnp.int16),
        ],
        in_specs=[vmem()] * 2,
        out_specs=[vmem()] * 2,
        compiler_params=pltpu.CompilerParams(vmem_limit_bytes=16 * 2**20),
        name="code",
    )(mine, got)


def final_kernel(
    nsum, npeer, blocks, n, ncol, src_ref, place_ref, occ_ref, vir_ref, *rest
):
    sums, codes, out = (
        rest[:nsum],
        [
            rest[nsum + j * npeer : nsum + (j + 1) * npeer]
            for j in range(nsum)
        ],
        rest[nsum * (1 + npeer)],
    )
    width = vir_ref.shape[1]
    chip, half = place_ref[0], place_ref[1]
    rows_out = out.shape[1]
    vir = vir_ref[...]
    for j, batch in enumerate(blocks):
        for b, (which, block) in enumerate(batch):
            src = src_ref[which]
            owner = src * ncol // n
            row = lax.rem(src, n // ncol) * (rows_out * ncol // n) + block * IJ_BLK
            at = slice(b * IJ_BLK, (b + 1) * IJ_BLK)

            @pl.when(owner // 2 == chip)
            def _():
                side = lax.rem(owner + half, 2)
                to = pl.multiple_of(row, IJ_BLK)
                total = sums[j][at, :]
                for got in codes[j]:
                    level = got[at, width:].astype(jnp.int32).astype(jnp.float32)
                    down = jnp.exp(level[:, :1] * (LN2 / OCTAVE)) * (1.0 / TOP)
                    coded = got[at, :width].astype(jnp.int32).astype(jnp.float32)
                    total = total + coded * down
                denom = vir - occ_ref[side, pl.ds(to, IJ_BLK), :]
                out[side, pl.ds(to, IJ_BLK), :] = (total / denom).astype(out.dtype)


def final(sums, codes, blocks, n, ncol, src, place, occ, vir):
    npeer = len(codes[0])
    flat = [c for batch in codes for c in batch]
    width = vir.shape[1]
    return pl.pallas_call(
        functools.partial(final_kernel, len(sums), npeer, blocks, n, ncol),
        out_shape=jax.ShapeDtypeStruct((2, occ.shape[1], width), jnp.bfloat16),
        in_specs=[smem(), smem()] + [vmem()] * (2 + len(sums) + len(flat)),
        out_specs=vmem(),
        compiler_params=pltpu.CompilerParams(vmem_limit_bytes=32 * 2**20),
        name="final",
    )(src, place, occ, vir, *sums, *flat)


def body(n, ncol, amplitudes, amp_mask, integrals, int_mask, occ_energy, vir_energy):
    cycle = list(range(0, n, 2)) + list(range(n - 1, 0, -2))
    ahead = [(cycle[p], cycle[(p + 1) % n]) for p in range(n)]
    behind = [(b, a) for a, b in ahead]
    row, col = lax.axis_index("row"), lax.axis_index("col")
    half = lax.rem(col, 2)
    core = [(c, c ^ 1) for c in range(ncol)]
    nblock = amp_mask.shape[0]
    per = nblock // FLOWS
    table = [None] * n
    for p in range(n):
        table[cycle[p]] = [cycle[p]] + [
            cycle[(p + sign * s) % n] for s in range(1, n) for sign in (-1, 1)
        ]
    src = jnp.array(table, jnp.int32)[row]
    place = jnp.stack([col // 2, half]).astype(jnp.int32)
    width = integrals.shape[0] // 2

    flows = pack(amplitudes, amp_mask)
    tile_list, offsets = make_list(half.reshape(1).astype(jnp.int32), int_mask)
    occ_other = lax.ppermute(occ_energy, "col", core)
    occ = jnp.stack([occ_energy, occ_other])[:, :, None]
    vir = lax.dynamic_slice_in_dim(vir_energy, half * width, width)[None, :]

    parts = [[(flows[f], 0, f * per) for f in range(FLOWS)]]
    held = list(flows)
    for s in range(1, n):
        held = [
            lax.ppermute(h, "row", ahead if f < FLOWS // 2 else behind)
            for f, h in enumerate(held)
        ]
        parts.append(
            [
                (h, 2 * s - 1 + (f >= FLOWS // 2), f * per)
                for f, h in enumerate(held)
            ]
        )
    batches, now = [], []
    for s in range(n):
        now += parts[s]
        if s % 2 == 1 and s < n - 2 or s >= n - 2:
            batches.append(now)
            now = []
    sums, codes, blocks = [], [], []
    for batch in batches:
        other, mine = ladder([c for c, _, _ in batch], tile_list, offsets, integrals)
        got = lax.ppermute(other, "col", core)
        total, coded = code(mine, got)
        sums.append(total)
        codes.append(
            [
                lax.ppermute(coded, "col", [(c, c ^ (2 * d)) for c in range(ncol)])
                for d in range(1, ncol // 2)
            ]
        )
        blocks.append(
            [(which, b + q) for _, which, b in batch for q in range(per)]
        )
    done = final(sums, codes, blocks, n, ncol, src, place, occ, vir)
    mine, theirs = done[0], done[1]
    got = lax.ppermute(theirs, "col", core)
    return jnp.where(
        half == 0,
        jnp.concatenate([mine, got], axis=1),
        jnp.concatenate([got, mine], axis=1),
    )


def solution(mesh):
    return jax.shard_map(
        functools.partial(body, mesh.shape["row"], mesh.shape["col"]),
        mesh=mesh,
        in_specs=(
            P("row", "col"),
            P("row", "col"),
            P("row", "col"),
            P("row", "col"),
            P("col"),
            P("row"),
        ),
        out_specs=P("col", "row"),
        check_vma=False,
    )
```

time: 305 us -> 309 us (1.013)
  the two profiles are of different devices: /device:TPU:0 before, /device:TPU:17 now
where the time goes in v1:
time: 309 us; the launch traced here: 310 us
  Pallas kernels  178 us (58%)
  waiting for transfers between devices  77.5 us (25%)
  starting transfers between devices  39.1 us (13%)
  local copies, waits for them, and re-layouts  12.8 us (4%)
    pallas_call x5, Pallas kernels, ladder(): pl.pallas_call(functools.partial(ladder_kernel, nchunk, per, ntile), out_...  160 us
    ppermute x28, waiting for transfers between devices, body(): lax.ppermute(h, 'row', ahead if f < FLOWS // 2 else behind)  39.2 us
    ppermute x5, waiting for transfers between devices, body(): lax.ppermute(coded, 'col', [(c, c ^ 2 * d) for c in range(ncol)])  36.7 us
    ppermute x28, starting transfers between devices, body(): lax.ppermute(h, 'row', ahead if f < FLOWS // 2 else behind)  17.7 us
    ppermute x5, starting transfers between devices, body(): got = lax.ppermute(other, 'col', core)  16.8 us
    unnamed x32, local copies, waits for them, and re-layouts  11.8 us
    pallas_call x5, Pallas kernels, code(): pl.pallas_call(code_kernel, out_shape=[jax.ShapeDtypeStruct((rows, width)...  9.71 us
  transfers between devices with their start and end apart: 40, of which 13 were waited for; matrix products, arithmetic and copies ran while one was open for 0% of the time, Pallas kernels for 56%

profile of v1, /device:TPU:17, one launch (start us, length us, event | category | flops | bytes accessed | tf_op | source)
XLA Modules:
  0.0 309.6 jit_solution(16962458077674957548)
XLA Ops:
  0.0 1.6 copy-done
  2.3 1.7 pack.1
  4.0 1.3 collective-permute-start.1
  5.3 1.2 collective-permute-start.2
  7.0 4.3 %collective-permute-done.1.rest_4_ = bf16[1040,128]{1,0:T(8,128)(2,1)S(1)} collective-permute-done((bf16[1040,128]{1,0:T(8,128)(2,1)S(1)}, bf16[1040,128]{1,0:T(8,128)(2,1)S(1)}, u32[]{:S(2)}, u32[]{:S(2)}) %collective-permute-start.1) | collective-permute-done | bytes 266272 | tf_op jit(solution)/shard_map/ppermute | solution.py:344
  11.3 1.3 collective-permute-start.6
  12.6 4.4 %collective-permute-done.2.rest_5_ = bf16[1040,128]{1,0:T(8,128)(2,1)S(1)} collective-permute-done((bf16[1040,128]{1,0:T(8,128)(2,1)S(1)}, bf16[1040,128]{1,0:T(8,128)(2,1)S(1)}, u32[]{:S(2)}, u32[]{:S(2)}) %collective-permute-start.2) | collective-permute-done | bytes 266272 | tf_op jit(solution)/shard_map/ppermute | solution.py:344
  17.0 1.3 collective-permute-start.7
  19.8 2.9 collective-permute-done.6.rest_0_
  22.7 1.3 collective-permute-start.10
  24.0 4.4 %collective-permute-done.7.rest_1_ = bf16[1040,128]{1,0:T(8,128)(2,1)S(1)} collective-permute-done((bf16[1040,128]{1,0:T(8,128)(2,1)S(1)}, bf16[1040,128]{1,0:T(8,128)(2,1)S(1)}, u32[]{:S(2)}, u32[]{:S(2)}) %collective-permute-start.7) | collective-permute-done | bytes 266272 | tf_op jit(solution)/shard_map/ppermute | solution.py:344
  28.4 1.3 collective-permute-start.11
  30.0 4.1 %collective-permute-done.10.rest_4_ = bf16[1040,128]{1,0:T(8,128)(2,1)S(1)} collective-permute-done((bf16[1040,128]{1,0:T(8,128)(2,1)S(1)}, bf16[1040,128]{1,0:T(8,128)(2,1)S(1)}, u32[]{:S(2)}, u32[]{:S(2)}) %collective-permute-start.10) | collective-permute-done | bytes 266272 | tf_op jit(solution)/shard_map/ppermute | solution.py:344
  34.1 1.3 collective-permute-start.15
  35.4 3.4 %tile_list.1 = (s32[257]{0:T(512)}, s32[9]{0:T(128)}) custom-call(s32[1]{0:T(128)} %bitcast.2.half_ref, s32[8,32]{1,0:T(8,128)} %mask_ref.2), custom_call_target="tpu_custom_call" | custom-call | tf_op jit(solution)/shard_map/tile_list/pallas_call | solution.py:101
  38.8 1.1 collective-permute-done.11.rest_5_
  39.9 1.3 collective-permute-start.16
  41.6 4.0 %collective-permute-done.15.rest_0_ = bf16[1040,128]{1,0:T(8,128)(2,1)S(1)} collective-permute-done((bf16[1040,128]{1,0:T(8,128)(2,1)S(1)}, bf16[1040,128]{1,0:T(8,128)(2,1)S(1)}, u32[]{:S(2)}, u32[]{:S(2)}) %collective-permute-start.15) | collective-permute-done | bytes 266272 | tf_op jit(solution)/shard_map/ppermute | solution.py:344
  45.5 1.3 collective-permute-start.19
  49.1 33.3 %ladder.5 = (f32[256,1024]{1,0:T(8,128)S(1)}, f32[256,1024]{1,0:T(8,128)S(1)}) custom-call(s32[257]{0:T(512)S(1)} %copy-done.11, s32[9]{0:T(128)S(1)} %copy-done.12, bf16[2048,8192]{1,0:T(8,128)(2,1)} %int_ref.9, bf16[1040,128]{1,0:T(8,128)(2,1)S(1)} %get-tuple-element.33.rest_0_, bf16[1040,128]{1,0:T(8,128)(2,1)S(1)} %get-tuple-element.34.rest_1_, ...), custom_call_target="tpu_custom_call" | custom-call | flops 4294967296 | bytes 16777216 | tf_op jit(solution)/shard_map/ladder/pallas_call | solution.py:206
  82.4 5.3 %collective-permute-start.5 = (f32[256,1024]{1,0:T(8,128)S(1)}, f32[256,1024]{1,0:T(8,128)S(1)}, u32[]{:S(2)}, u32[]{:S(2)}) collective-permute-start(f32[256,1024]{1,0:T(8,128)S(1)} %get-tuple-element.38), channel_id=1, source_target_pairs={{0,1},{1,0},{2,3},{3,2},{4,5},{5,4},{6,7},{7,6},{8,9},{9,8},{10,11... | collective-permute-start | bytes 3145736 | tf_op jit(solution)/shard_map/ppermute | solution.py:362
  87.7 1.5 collective-permute-start.21
  89.2 1.4 collective-permute-start.24
  90.7 33.9 %ladder.6 = (f32[256,1024]{1,0:T(8,128)S(1)}, f32[256,1024]{1,0:T(8,128)S(1)}) custom-call(s32[257]{0:T(512)S(1)} %copy-done.11, s32[9]{0:T(128)S(1)} %copy-done.12, bf16[2048,8192]{1,0:T(8,128)(2,1)} %int_ref.9, bf16[1040,128]{1,0:T(8,128)(2,1)S(1)} %collective-permute-done.6.rest_0_, bf16[1040,128]{1,0:T(8,128)(2,1)S(1)} %collective-permute-done.7.rest_1_, ...), custom_call_target="tpu_custom_call" | custom-call | flops 4294967296 | bytes 16777216 | tf_op jit(solution)/shard_map/ladder/pallas_call | solution.py:206
  124.5 3.5 %collective-permute-start.14 = (f32[256,1024]{1,0:T(8,128)S(1)}, f32[256,1024]{1,0:T(8,128)S(1)}, u32[]{:S(2)}, u32[]{:S(2)}) collective-permute-start(f32[256,1024]{1,0:T(8,128)S(1)} %get-tuple-element.41), channel_id=1, source_target_pairs={{0,1},{1,0},{2,3},{3,2},{4,5},{5,4},{6,7},{7,6},{8,9},{9,8},{10,11... | collective-permute-start | bytes 3145736 | tf_op jit(solution)/shard_map/ppermute | solution.py:362
  128.1 1.5 collective-permute-start.26
  129.6 33.3 %ladder.7 = (f32[256,1024]{1,0:T(8,128)S(1)}, f32[256,1024]{1,0:T(8,128)S(1)}) custom-call(s32[257]{0:T(512)S(1)} %copy-done.11, s32[9]{0:T(128)S(1)} %copy-done.12, bf16[2048,8192]{1,0:T(8,128)(2,1)} %int_ref.9, bf16[1040,128]{1,0:T(8,128)(2,1)S(1)} %collective-permute-done.15.rest_0_, bf16[1040,128]{1,0:T(8,128)(2,1)S(1)} %collective-permute-done.16.rest_1_, ...), custom_call_target="tpu_custom_call" | custom-call | flops 4294967296 | bytes 16777216 | tf_op jit(solution)/shard_map/ladder/pallas_call | solution.py:206
  162.9 3.0 collective-permute-start.23
  165.9 7.9 %collective-permute-done.29.rest_0_ = bf16[1040,128]{1,0:T(8,128)(2,1)S(1)} collective-permute-done((bf16[1040,128]{1,0:T(8,128)(2,1)S(1)}, bf16[1040,128]{1,0:T(8,128)(2,1)S(1)}, u32[]{:S(2)}, u32[]{:S(2)}) %collective-permute-start.29) | collective-permute-done | bytes 266272 | tf_op jit(solution)/shard_map/ppermute | solution.py:344
  173.8 5.7 %collective-permute-done.30.rest_1_ = bf16[1040,128]{1,0:T(8,128)(2,1)S(1)} collective-permute-done((bf16[1040,128]{1,0:T(8,128)(2,1)S(1)}, bf16[1040,128]{1,0:T(8,128)(2,1)S(1)}, u32[]{:S(2)}, u32[]{:S(2)}) %collective-permute-start.30) | collective-permute-done | bytes 266272 | tf_op jit(solution)/shard_map/ppermute | solution.py:344
  179.5 29.8 %ladder.8 = (f32[128,1024]{1,0:T(8,128)}, f32[128,1024]{1,0:T(8,128)S(1)}) custom-call(s32[257]{0:T(512)S(1)} %copy-done.11, s32[9]{0:T(128)S(1)} %copy-done.12, bf16[2048,8192]{1,0:T(8,128)(2,1)} %int_ref.9, bf16[1040,128]{1,0:T(8,128)(2,1)S(1)} %collective-permute-done.24.rest_0_, bf16[1040,128]{1,0:T(8,128)(2,1)S(1)} %collective-permute-done.25.rest_1_, ...), custom_call_target="tpu_custom_call" | custom-call | flops 2147483648 | bytes 16777216 | tf_op jit(solution)/shard_map/ladder/pallas_call | solution.py:206
  210.1 2.9 collective-permute-start.28
  213.0 29.8 %ladder.9 = (f32[128,1024]{1,0:T(8,128)}, f32[128,1024]{1,0:T(8,128)S(1)}) custom-call(s32[257]{0:T(512)S(1)} %copy-done.11, s32[9]{0:T(128)S(1)} %copy-done.12, bf16[2048,8192]{1,0:T(8,128)(2,1)} %int_ref.9, bf16[1040,128]{1,0:T(8,128)(2,1)S(1)} %collective-permute-done.29.rest_0_, bf16[1040,128]{1,0:T(8,128)(2,1)S(1)} %collective-permute-done.30.rest_1_, ...), custom_call_target="tpu_custom_call" | custom-call | flops 2147483648 | bytes 16777216 | tf_op jit(solution)/shard_map/ladder/pallas_call | solution.py:206
  242.8 2.1 collective-permute-start.33
  244.9 1.8 code.5
  246.7 1.8 code.6
  248.5 1.4 collective-permute-start.35
  249.9 1.8 code.7
  252.3 1.0 copy-done.2
  253.4 2.2 code.8
  256.4 1.7 collective-permute-start.37
  259.1 2.2 code.9
  263.1 30.4 %collective-permute-done.37.rest_8_ = s16[128,1152]{1,0:T(8,128)(2,1)} collective-permute-done((s16[128,1152]{1,0:T(8,128)(2,1)}, s16[128,1152]{1,0:T(8,128)(2,1)}, u32[]{:S(2)}, u32[]{:S(2)}) %collective-permute-start.37) | collective-permute-done | bytes 294944 | tf_op jit(solution)/shard_map/ppermute | solution.py:367
  293.5 6.3 %collective-permute-done.38.rest_9_ = s16[128,1152]{1,0:T(8,128)(2,1)} collective-permute-done((s16[128,1152]{1,0:T(8,128)(2,1)}, s16[128,1152]{1,0:T(8,128)(2,1)}, u32[]{:S(2)}, u32[]{:S(2)}) %collective-permute-start.38) | collective-permute-done | bytes 294944 | tf_op jit(solution)/shard_map/ppermute | solution.py:367
  299.9 1.0 copy-done.6
  301.9 3.8 %final.1 = bf16[2,256,1024]{2,1,0:T(8,128)(2,1)S(1)} custom-call(s32[15]{0:T(128)S(1)} %dynamic-slice_bitcast_fusion.src_ref, s32[2]{0:T(128)S(1)} %pad_add_fusion.place_ref, f32[2,256,1]{2,1,0:T(8,128)S(1)} %copy.8.occ_ref, f32[1,1024]{1,0:T(1,128)S(1)} %bitcast.13, f32[256,1024]{1,0:T(8,128)S(1)} %get-tuple-element.39.rest_0_, ...), custom_call_target="tpu_custom_call" | custom-call | tf_op jit(solution)/shard_map/final/pallas_call | solution.py:306
  306.7 1.5 collective-permute-done.39
  308.2 1.4 maximum_select_fusion
  (84 shorter events, 12.9 us)
Async XLA Ops:
  0.0 1.6 copy-start
  4.0 7.3 %collective-permute-start.1 = (bf16[1040,128]{1,0:T(8,128)(2,1)S(1)}, bf16[1040,128]{1,0:T(8,128)(2,1)S(1)}, u32[]{:S(2)}, u32[]{:S(2)}) collective-permute-start(bf16[1040,128]{1,0:T(8,128)(2,1)S(1)} %get-tuple-element.33.rest_0_), channel_id=1, source_target_pairs={{0,8},{8,16},{16,24},{24,28},{28,20},{20,12},{12,4},{4,0},{1,9},{9... | collective-permute-start | bytes 798728 | tf_op jit(solution)/shard_map/ppermute | solution.py:344
  5.3 11.7 %collective-permute-start.2 = (bf16[1040,128]{1,0:T(8,128)(2,1)S(1)}, bf16[1040,128]{1,0:T(8,128)(2,1)S(1)}, u32[]{:S(2)}, u32[]{:S(2)}) collective-permute-start(bf16[1040,128]{1,0:T(8,128)(2,1)S(1)} %get-tuple-element.34.rest_1_), channel_id=1, source_target_pairs={{0,8},{8,16},{16,24},{24,28},{28,20},{20,12},{12,4},{4,0},{1,9},{9... | collective-permute-start | bytes 798728 | tf_op jit(solution)/shard_map/ppermute | solution.py:344
  6.6 11.7 %collective-permute-start.3 = (bf16[1040,128]{1,0:T(8,128)(2,1)S(1)}, bf16[1040,128]{1,0:T(8,128)(2,1)S(1)}, u32[]{:S(2)}, u32[]{:S(2)}) collective-permute-start(bf16[1040,128]{1,0:T(8,128)(2,1)S(1)} %get-tuple-element.35.rest_2_), channel_id=1, source_target_pairs={{8,0},{16,8},{24,16},{28,24},{20,28},{12,20},{4,12},{0,4},{9,1},{1... | collective-permute-start | bytes 798728 | tf_op jit(solution)/shard_map/ppermute | solution.py:344
  6.8 12.1 %collective-permute-start.4 = (bf16[1040,128]{1,0:T(8,128)(2,1)S(1)}, bf16[1040,128]{1,0:T(8,128)(2,1)S(1)}, u32[]{:S(2)}, u32[]{:S(2)}) collective-permute-start(bf16[1040,128]{1,0:T(8,128)(2,1)S(1)} %get-tuple-element.36.rest_3_), channel_id=1, source_target_pairs={{8,0},{16,8},{24,16},{28,24},{20,28},{12,20},{4,12},{0,4},{9,1},{1... | collective-permute-start | bytes 798728 | tf_op jit(solution)/shard_map/ppermute | solution.py:344
  11.3 11.4 %collective-permute-start.6 = (bf16[1040,128]{1,0:T(8,128)(2,1)S(1)}, bf16[1040,128]{1,0:T(8,128)(2,1)S(1)}, u32[]{:S(2)}, u32[]{:S(2)}) collective-permute-start(bf16[1040,128]{1,0:T(8,128)(2,1)S(1)} %collective-permute-done.1.rest_4_), channel_id=1, source_target_pairs={{0,8},{8,16},{16,24},{24,28},{28,20},{20,12},{12,4},{4,0},{1,9},{9... | collective-permute-start | bytes 798728 | tf_op jit(solution)/shard_map/ppermute | solution.py:344
  17.0 11.4 %collective-permute-start.7 = (bf16[1040,128]{1,0:T(8,128)(2,1)S(1)}, bf16[1040,128]{1,0:T(8,128)(2,1)S(1)}, u32[]{:S(2)}, u32[]{:S(2)}) collective-permute-start(bf16[1040,128]{1,0:T(8,128)(2,1)S(1)} %collective-permute-done.2.rest_5_), channel_id=1, source_target_pairs={{0,8},{8,16},{16,24},{24,28},{28,20},{20,12},{12,4},{4,0},{1,9},{9... | collective-permute-start | bytes 798728 | tf_op jit(solution)/shard_map/ppermute | solution.py:344
  18.3 11.4 %collective-permute-start.8 = (bf16[1040,128]{1,0:T(8,128)(2,1)S(1)}, bf16[1040,128]{1,0:T(8,128)(2,1)S(1)}, u32[]{:S(2)}, u32[]{:S(2)}) collective-permute-start(bf16[1040,128]{1,0:T(8,128)(2,1)S(1)} %collective-permute-done.3.rest_6_), channel_id=1, source_target_pairs={{8,0},{16,8},{24,16},{28,24},{20,28},{12,20},{4,12},{0,4},{9,1},{1... | collective-permute-start | bytes 798728 | tf_op jit(solution)/shard_map/ppermute | solution.py:344
  18.9 11.0 %collective-permute-start.9 = (bf16[1040,128]{1,0:T(8,128)(2,1)S(1)}, bf16[1040,128]{1,0:T(8,128)(2,1)S(1)}, u32[]{:S(2)}, u32[]{:S(2)}) collective-permute-start(bf16[1040,128]{1,0:T(8,128)(2,1)S(1)} %collective-permute-done.4.rest_7_), channel_id=1, source_target_pairs={{8,0},{16,8},{24,16},{28,24},{20,28},{12,20},{4,12},{0,4},{9,1},{1... | collective-permute-start | bytes 798728 | tf_op jit(solution)/shard_map/ppermute | solution.py:344
  22.7 11.4 %collective-permute-start.10 = (bf16[1040,128]{1,0:T(8,128)(2,1)S(1)}, bf16[1040,128]{1,0:T(8,128)(2,1)S(1)}, u32[]{:S(2)}, u32[]{:S(2)}) collective-permute-start(bf16[1040,128]{1,0:T(8,128)(2,1)S(1)} %collective-permute-done.6.rest_0_), channel_id=1, source_target_pairs={{0,8},{8,16},{16,24},{24,28},{28,20},{20,12},{12,4},{4,0},{1,9},{9... | collective-permute-start | bytes 798728 | tf_op jit(solution)/shard_map/ppermute | solution.py:344
  28.4 11.5 %collective-permute-start.11 = (bf16[1040,128]{1,0:T(8,128)(2,1)S(1)}, bf16[1040,128]{1,0:T(8,128)(2,1)}, u32[]{:S(2)}, u32[]{:S(2)}) collective-permute-start(bf16[1040,128]{1,0:T(8,128)(2,1)S(1)} %collective-permute-done.7.rest_1_), channel_id=1, source_target_pairs={{0,8},{8,16},{16,24},{24,28},{28,20},{20,12},{12,4},{4,0},{1,9},{9... | collective-permute-start | bytes 798728 | tf_op jit(solution)/shard_map/ppermute | solution.py:344
  29.7 11.5 %collective-permute-start.12 = (bf16[1040,128]{1,0:T(8,128)(2,1)S(1)}, bf16[1040,128]{1,0:T(8,128)(2,1)}, u32[]{:S(2)}, u32[]{:S(2)}) collective-permute-start(bf16[1040,128]{1,0:T(8,128)(2,1)S(1)} %collective-permute-done.8.rest_2_), channel_id=1, source_target_pairs={{8,0},{16,8},{24,16},{28,24},{20,28},{12,20},{4,12},{0,4},{9,1},{1... | collective-permute-start | bytes 798728 | tf_op jit(solution)/shard_map/ppermute | solution.py:344
  29.9 11.5 %collective-permute-start.13 = (bf16[1040,128]{1,0:T(8,128)(2,1)S(1)}, bf16[1040,128]{1,0:T(8,128)(2,1)}, u32[]{:S(2)}, u32[]{:S(2)}) collective-permute-start(bf16[1040,128]{1,0:T(8,128)(2,1)S(1)} %collective-permute-done.9.rest_3_), channel_id=1, source_target_pairs={{8,0},{16,8},{24,16},{28,24},{20,28},{12,20},{4,12},{0,4},{9,1},{1... | collective-permute-start | bytes 798728 | tf_op jit(solution)/shard_map/ppermute | solution.py:344
  34.1 11.4 %collective-permute-start.15 = (bf16[1040,128]{1,0:T(8,128)(2,1)S(1)}, bf16[1040,128]{1,0:T(8,128)(2,1)S(1)}, u32[]{:S(2)}, u32[]{:S(2)}) collective-permute-start(bf16[1040,128]{1,0:T(8,128)(2,1)S(1)} %collective-permute-done.10.rest_4_), channel_id=1, source_target_pairs={{0,8},{8,16},{16,24},{24,28},{28,20},{20,12},{12,4},{4,0},{1,9},{9... | collective-permute-start | bytes 798728 | tf_op jit(solution)/shard_map/ppermute | solution.py:344
  39.9 47.8 %collective-permute-start.16 = (bf16[1040,128]{1,0:T(8,128)(2,1)}, bf16[1040,128]{1,0:T(8,128)(2,1)S(1)}, u32[]{:S(2)}, u32[]{:S(2)}) collective-permute-start(bf16[1040,128]{1,0:T(8,128)(2,1)} %collective-permute-done.11.rest_5_), channel_id=1, source_target_pairs={{0,8},{8,16},{16,24},{24,28},{28,20},{20,12},{12,4},{4,0},{1,9},{9... | collective-permute-start | bytes 798728 | tf_op jit(solution)/shard_map/ppermute | solution.py:344
  41.2 46.5 %collective-permute-start.17 = (bf16[1040,128]{1,0:T(8,128)(2,1)}, bf16[1040,128]{1,0:T(8,128)(2,1)S(1)}, u32[]{:S(2)}, u32[]{:S(2)}) collective-permute-start(bf16[1040,128]{1,0:T(8,128)(2,1)} %collective-permute-done.12.rest_6_), channel_id=1, source_target_pairs={{8,0},{16,8},{24,16},{28,24},{20,28},{12,20},{4,12},{0,4},{9,1},{1... | collective-permute-start | bytes 798728 | tf_op jit(solution)/shard_map/ppermute | solution.py:344
  41.4 47.8 %collective-permute-start.18 = (bf16[1040,128]{1,0:T(8,128)(2,1)}, bf16[1040,128]{1,0:T(8,128)(2,1)S(1)}, u32[]{:S(2)}, u32[]{:S(2)}) collective-permute-start(bf16[1040,128]{1,0:T(8,128)(2,1)} %collective-permute-done.13.rest_7_), channel_id=1, source_target_pairs={{8,0},{16,8},{24,16},{28,24},{20,28},{12,20},{4,12},{0,4},{9,1},{1... | collective-permute-start | bytes 798728 | tf_op jit(solution)/shard_map/ppermute | solution.py:344
  45.5 43.7 %collective-permute-start.19 = (bf16[1040,128]{1,0:T(8,128)(2,1)S(1)}, bf16[1040,128]{1,0:T(8,128)(2,1)S(1)}, u32[]{:S(2)}, u32[]{:S(2)}) collective-permute-start(bf16[1040,128]{1,0:T(8,128)(2,1)S(1)} %collective-permute-done.15.rest_0_), channel_id=1, source_target_pairs={{0,8},{8,16},{16,24},{24,28},{28,20},{20,12},{12,4},{4,0},{1,9},{9... | collective-permute-start | bytes 798728 | tf_op jit(solution)/shard_map/ppermute | solution.py:344
  82.4 162.5 %collective-permute-start.5 = (f32[256,1024]{1,0:T(8,128)S(1)}, f32[256,1024]{1,0:T(8,128)S(1)}, u32[]{:S(2)}, u32[]{:S(2)}) collective-permute-start(f32[256,1024]{1,0:T(8,128)S(1)} %get-tuple-element.38), channel_id=1, source_target_pairs={{0,1},{1,0},{2,3},{3,2},{4,5},{5,4},{6,7},{7,6},{8,9},{9,8},{10,11... | collective-permute-start | bytes 3145736 | tf_op jit(solution)/shard_map/ppermute | solution.py:362
  87.7 36.8 %collective-permute-start.20 = (bf16[1040,128]{1,0:T(8,128)(2,1)S(1)}, bf16[1040,128]{1,0:T(8,128)(2,1)S(1)}, u32[]{:S(2)}, u32[]{:S(2)}) collective-permute-start(bf16[1040,128]{1,0:T(8,128)(2,1)S(1)} %collective-permute-done.16.rest_1_), channel_id=1, source_target_pairs={{0,8},{8,16},{16,24},{24,28},{28,20},{20,12},{12,4},{4,0},{1,9},{9... | collective-permute-start | bytes 798728 | tf_op jit(solution)/shard_map/ppermute | solution.py:344
  87.7 40.3 %collective-permute-start.21 = (bf16[1040,128]{1,0:T(8,128)(2,1)S(1)}, bf16[1040,128]{1,0:T(8,128)(2,1)S(1)}, u32[]{:S(2)}, u32[]{:S(2)}) collective-permute-start(bf16[1040,128]{1,0:T(8,128)(2,1)S(1)} %collective-permute-done.17.rest_2_), channel_id=1, source_target_pairs={{8,0},{16,8},{24,16},{28,24},{20,28},{12,20},{4,12},{0,4},{9,1},{1... | collective-permute-start | bytes 798728 | tf_op jit(solution)/shard_map/ppermute | solution.py:344
  89.2 38.9 %collective-permute-start.22 = (bf16[1040,128]{1,0:T(8,128)(2,1)S(1)}, bf16[1040,128]{1,0:T(8,128)(2,1)S(1)}, u32[]{:S(2)}, u32[]{:S(2)}) collective-permute-start(bf16[1040,128]{1,0:T(8,128)(2,1)S(1)} %collective-permute-done.18.rest_3_), channel_id=1, source_target_pairs={{8,0},{16,8},{24,16},{28,24},{20,28},{12,20},{4,12},{0,4},{9,1},{1... | collective-permute-start | bytes 798728 | tf_op jit(solution)/shard_map/ppermute | solution.py:344
  89.2 40.3 %collective-permute-start.24 = (bf16[1040,128]{1,0:T(8,128)(2,1)S(1)}, bf16[1040,128]{1,0:T(8,128)(2,1)S(1)}, u32[]{:S(2)}, u32[]{:S(2)}) collective-permute-start(bf16[1040,128]{1,0:T(8,128)(2,1)S(1)} %collective-permute-done.19.rest_4_), channel_id=1, source_target_pairs={{0,8},{8,16},{16,24},{24,28},{28,20},{20,12},{12,4},{4,0},{1,9},{9... | collective-permute-start | bytes 798728 | tf_op jit(solution)/shard_map/ppermute | solution.py:344
  124.5 122.2 %collective-permute-start.14 = (f32[256,1024]{1,0:T(8,128)S(1)}, f32[256,1024]{1,0:T(8,128)S(1)}, u32[]{:S(2)}, u32[]{:S(2)}) collective-permute-start(f32[256,1024]{1,0:T(8,128)S(1)} %get-tuple-element.41), channel_id=1, source_target_pairs={{0,1},{1,0},{2,3},{3,2},{4,5},{5,4},{6,7},{7,6},{8,9},{9,8},{10,11... | collective-permute-start | bytes 3145736 | tf_op jit(solution)/shard_map/ppermute | solution.py:362
  128.1 34.8 %collective-permute-start.25 = (bf16[1040,128]{1,0:T(8,128)(2,1)S(1)}, bf16[1040,128]{1,0:T(8,128)(2,1)S(1)}, u32[]{:S(2)}, u32[]{:S(2)}) collective-permute-start(bf16[1040,128]{1,0:T(8,128)(2,1)S(1)} %collective-permute-done.20.rest_5_), channel_id=1, source_target_pairs={{0,8},{8,16},{16,24},{24,28},{28,20},{20,12},{12,4},{4,0},{1,9},{9... | collective-permute-start | bytes 798728 | tf_op jit(solution)/shard_map/ppermute | solution.py:344
  128.1 37.8 %collective-permute-start.26 = (bf16[1040,128]{1,0:T(8,128)(2,1)S(1)}, bf16[1040,128]{1,0:T(8,128)(2,1)S(1)}, u32[]{:S(2)}, u32[]{:S(2)}) collective-permute-start(bf16[1040,128]{1,0:T(8,128)(2,1)S(1)} %collective-permute-done.21.rest_6_), channel_id=1, source_target_pairs={{8,0},{16,8},{24,16},{28,24},{20,28},{12,20},{4,12},{0,4},{9,1},{1... | collective-permute-start | bytes 798728 | tf_op jit(solution)/shard_map/ppermute | solution.py:344
  129.5 36.3 %collective-permute-start.27 = (bf16[1040,128]{1,0:T(8,128)(2,1)S(1)}, bf16[1040,128]{1,0:T(8,128)(2,1)S(1)}, u32[]{:S(2)}, u32[]{:S(2)}) collective-permute-start(bf16[1040,128]{1,0:T(8,128)(2,1)S(1)} %collective-permute-done.22.rest_7_), channel_id=1, source_target_pairs={{8,0},{16,8},{24,16},{28,24},{20,28},{12,20},{4,12},{0,4},{9,1},{1... | collective-permute-start | bytes 798728 | tf_op jit(solution)/shard_map/ppermute | solution.py:344
  162.9 87.0 %collective-permute-start.23 = (f32[256,1024]{1,0:T(8,128)S(1)}, f32[256,1024]{1,0:T(8,128)S(1)}, u32[]{:S(2)}, u32[]{:S(2)}) collective-permute-start(f32[256,1024]{1,0:T(8,128)S(1)} %get-tuple-element.44), channel_id=1, source_target_pairs={{0,1},{1,0},{2,3},{3,2},{4,5},{5,4},{6,7},{7,6},{8,9},{9,8},{10,11... | collective-permute-start | bytes 3145736 | tf_op jit(solution)/shard_map/ppermute | solution.py:362
  165.9 7.9 %collective-permute-start.29 = (bf16[1040,128]{1,0:T(8,128)(2,1)S(1)}, bf16[1040,128]{1,0:T(8,128)(2,1)S(1)}, u32[]{:S(2)}, u32[]{:S(2)}) collective-permute-start(bf16[1040,128]{1,0:T(8,128)(2,1)S(1)} %collective-permute-done.24.rest_0_), channel_id=1, source_target_pairs={{0,8},{8,16},{16,24},{24,28},{28,20},{20,12},{12,4},{4,0},{1,9},{9... | collective-permute-start | bytes 798728 | tf_op jit(solution)/shard_map/ppermute | solution.py:344
  165.9 13.6 %collective-permute-start.30 = (bf16[1040,128]{1,0:T(8,128)(2,1)S(1)}, bf16[1040,128]{1,0:T(8,128)(2,1)S(1)}, u32[]{:S(2)}, u32[]{:S(2)}) collective-permute-start(bf16[1040,128]{1,0:T(8,128)(2,1)S(1)} %collective-permute-done.25.rest_1_), channel_id=1, source_target_pairs={{0,8},{8,16},{16,24},{24,28},{28,20},{20,12},{12,4},{4,0},{1,9},{9... | collective-permute-start | bytes 798728 | tf_op jit(solution)/shard_map/ppermute | solution.py:344
  173.8 36.3 %collective-permute-start.31 = (bf16[1040,128]{1,0:T(8,128)(2,1)S(1)}, bf16[1040,128]{1,0:T(8,128)(2,1)S(1)}, u32[]{:S(2)}, u32[]{:S(2)}) collective-permute-start(bf16[1040,128]{1,0:T(8,128)(2,1)S(1)} %collective-permute-done.26.rest_2_), channel_id=1, source_target_pairs={{8,0},{16,8},{24,16},{28,24},{20,28},{12,20},{4,12},{0,4},{9,1},{1... | collective-permute-start | bytes 798728 | tf_op jit(solution)/shard_map/ppermute | solution.py:344
  179.5 33.5 %collective-permute-start.32 = (bf16[1040,128]{1,0:T(8,128)(2,1)S(1)}, bf16[1040,128]{1,0:T(8,128)(2,1)S(1)}, u32[]{:S(2)}, u32[]{:S(2)}) collective-permute-start(bf16[1040,128]{1,0:T(8,128)(2,1)S(1)} %collective-permute-done.27.rest_3_), channel_id=1, source_target_pairs={{8,0},{16,8},{24,16},{28,24},{20,28},{12,20},{4,12},{0,4},{9,1},{1... | collective-permute-start | bytes 798728 | tf_op jit(solution)/shard_map/ppermute | solution.py:344
  210.1 41.6 %collective-permute-start.28 = (f32[128,1024]{1,0:T(8,128)}, f32[128,1024]{1,0:T(8,128)}, u32[]{:S(2)}, u32[]{:S(2)}) collective-permute-start(f32[128,1024]{1,0:T(8,128)} %get-tuple-element.47), channel_id=1, source_target_pairs={{0,1},{1,0},{2,3},{3,2},{4,5},{5,4},{6,7},{7,6},{8,9},{9,8},{10,11... | collective-permute-start | bytes 1572872 | tf_op jit(solution)/shard_map/ppermute | solution.py:362
  242.8 5.6 %copy-start.3 = (f32[128,1024]{1,0:T(8,128)}, f32[128,1024]{1,0:T(8,128)S(1)}, u32[]{:S(2)}) copy-start(f32[128,1024]{1,0:T(8,128)S(1)} %get-tuple-element.49.mine_ref) | copy-start | bytes 1572868
  242.8 13.6 %collective-permute-start.33 = (f32[128,1024]{1,0:T(8,128)}, f32[128,1024]{1,0:T(8,128)}, u32[]{:S(2)}, u32[]{:S(2)}) collective-permute-start(f32[128,1024]{1,0:T(8,128)} %get-tuple-element.50), channel_id=1, source_target_pairs={{0,1},{1,0},{2,3},{3,2},{4,5},{5,4},{6,7},{7,6},{8,9},{9,8},{10,11... | collective-permute-start | bytes 1572872 | tf_op jit(solution)/shard_map/ppermute | solution.py:362
  246.7 16.4 %collective-permute-start.34 = (s16[256,1152]{1,0:T(8,128)(2,1)}, s16[256,1152]{1,0:T(8,128)(2,1)}, u32[]{:S(2)}, u32[]{:S(2)}) collective-permute-start(s16[256,1152]{1,0:T(8,128)(2,1)} %get-tuple-element.52), channel_id=1, source_target_pairs={{0,2},{1,3},{2,0},{3,1},{4,6},{5,7},{6,4},{7,5},{8,10},{9,11},{10,... | collective-permute-start | bytes 1769480 | tf_op jit(solution)/shard_map/ppermute | solution.py:367
  246.7 5.0 %copy-start.15 = (f32[256]{0:T(256)S(1)}, f32[256]{0:T(256)}, u32[]{:S(2)}) copy-start(f32[256]{0:T(256)} %param.11) | copy-start | bytes 3076
  246.7 5.7 %copy-start.14 = (f32[2048]{0:T(1024)S(1)}, f32[2048]{0:T(1024)}, u32[]{:S(2)}) copy-start(f32[2048]{0:T(1024)} %param.12) | copy-start | bytes 24580
  248.5 45.1 %collective-permute-start.35 = (s16[256,1152]{1,0:T(8,128)(2,1)}, s16[256,1152]{1,0:T(8,128)(2,1)}, u32[]{:S(2)}, u32[]{:S(2)}) collective-permute-start(s16[256,1152]{1,0:T(8,128)(2,1)} %get-tuple-element.53), channel_id=1, source_target_pairs={{0,2},{1,3},{2,0},{3,1},{4,6},{5,7},{6,4},{7,5},{8,10},{9,11},{10,... | collective-permute-start | bytes 1769480 | tf_op jit(solution)/shard_map/ppermute | solution.py:367
  251.7 48.2 %collective-permute-start.36 = (s16[256,1152]{1,0:T(8,128)(2,1)}, s16[256,1152]{1,0:T(8,128)(2,1)}, u32[]{:S(2)}, u32[]{:S(2)}) collective-permute-start(s16[256,1152]{1,0:T(8,128)(2,1)} %get-tuple-element.54), channel_id=1, source_target_pairs={{0,2},{1,3},{2,0},{3,1},{4,6},{5,7},{6,4},{7,5},{8,10},{9,11},{10,... | collective-permute-start | bytes 1769480 | tf_op jit(solution)/shard_map/ppermute | solution.py:367
  251.7 10.4 %collective-permute-start = (f32[256]{0:T(256)S(1)}, f32[256]{0:T(256)S(1)}, u32[]{:S(2)}, u32[]{:S(2)}) collective-permute-start(f32[256]{0:T(256)S(1)} %copy-done.15), channel_id=1, source_target_pairs={{0,1},{1,0},{2,3},{3,2},{4,5},{5,4},{6,7},{7,6},{8,9},{9,8},{10,11... | collective-permute-start | bytes 3080 | tf_op jit(solution)/shard_map/ppermute | solution.py:336
  252.3 1.0 copy-start.2
  256.4 37.1 %collective-permute-start.37 = (s16[128,1152]{1,0:T(8,128)(2,1)}, s16[128,1152]{1,0:T(8,128)(2,1)}, u32[]{:S(2)}, u32[]{:S(2)}) collective-permute-start(s16[128,1152]{1,0:T(8,128)(2,1)} %get-tuple-element.55), channel_id=1, source_target_pairs={{0,2},{1,3},{2,0},{3,1},{4,6},{5,7},{6,4},{7,5},{8,10},{9,11},{10,... | collective-permute-start | bytes 884744 | tf_op jit(solution)/shard_map/ppermute | solution.py:367
  258.1 1.0 copy-start.4
  262.1 37.7 %collective-permute-start.38 = (s16[128,1152]{1,0:T(8,128)(2,1)}, s16[128,1152]{1,0:T(8,128)(2,1)}, u32[]{:S(2)}, u32[]{:S(2)}) collective-permute-start(s16[128,1152]{1,0:T(8,128)(2,1)} %get-tuple-element.56), channel_id=1, source_target_pairs={{0,2},{1,3},{2,0},{3,1},{4,6},{5,7},{6,4},{7,5},{8,10},{9,11},{10,... | collective-permute-start | bytes 884744 | tf_op jit(solution)/shard_map/ppermute | solution.py:367
  299.9 1.0 copy-start.6
  300.9 1.0 copy-start.8
  305.8 2.4 collective-permute-start.39
  (8 other events, 6.1 us)

commit v2 on v1

v2 whole, which is shorter than its diff:
```python
import functools

import jax
import jax.numpy as jnp
from jax import lax
from jax.experimental import pallas as pl
from jax.experimental.pallas import tpu as pltpu
from jax.sharding import PartitionSpec as P

TILE = 256
IJ_BLK = 32
GRP = 8
KEPT = GRP // 2
LANES = 128
META = 16
PIECE = 2 * IJ_BLK
FLOWS = 2
RUN = 4
PAR = 4
SLOTS = 4
TOP = 32000.0
OCTAVE = 64.0
LN2 = 0.6931471805599453
FLOOR = 1e-30
VMEM = pltpu.VMEM
SMEM = pltpu.SMEM


def vmem():
    return pl.BlockSpec(memory_space=VMEM)


def smem():
    return pl.BlockSpec(memory_space=SMEM)


def pack_kernel(mask_ref, amp_ref, *rest):
    outs, (held, sems) = rest[:FLOWS], rest[FLOWS:]
    nblock, ntile = mask_ref.shape
    per = nblock // FLOWS
    groups = ntile // GRP
    slots = groups * KEPT
    lane = lax.broadcasted_iota(jnp.int32, (META, LANES), 1)

    def fetch(block):
        rows = pl.ds(block * IJ_BLK, IJ_BLK)
        return pltpu.make_async_copy(amp_ref.at[rows], held.at[rows], sems.at[block])

    order = [flow * per + q for q in range(per) for flow in range(FLOWS)]
    metas = [jnp.zeros((META, LANES), jnp.int32)] * FLOWS
    for block in order:
        fetch(block).start()
    for block in order:
        flow, q = block // per, block % per
        out = outs[flow]
        rows = slice(block * IJ_BLK, (block + 1) * IJ_BLK)
        fetch(block).wait()
        for g in range(groups):
            count, bits = jnp.int32(0), jnp.int32(0)
            for j in range(GRP):
                t = g * GRP + j
                here = mask_ref[block, t]
                base = (q * slots + g * KEPT + count) * PIECE

                @pl.when(here == 1)
                def _():
                    for half in range(2):
                        at = pl.multiple_of(base + half * IJ_BLK, IJ_BLK)
                        out[pl.ds(at, IJ_BLK), :] = held[
                            rows,
                            t * TILE + half * LANES : t * TILE + (half + 1) * LANES,
                        ]

                count += here
                bits += here << j
            metas[flow] = jnp.where(lane == q * groups + g, bits, metas[flow])
    for flow in range(FLOWS):
        meta = metas[flow].astype(jnp.float32).astype(jnp.bfloat16)
        outs[flow][per * slots * PIECE :, :] = meta


def pack(amplitudes, amp_mask):
    nblock, ntile = amp_mask.shape
    rows = nblock // FLOWS * (ntile // 2) * PIECE + META
    return pl.pallas_call(
        pack_kernel,
        out_shape=[jax.ShapeDtypeStruct((rows, LANES), jnp.bfloat16)] * FLOWS,
        in_specs=[smem(), pl.BlockSpec(memory_space=pl.ANY)],
        out_specs=[vmem()] * FLOWS,
        scratch_shapes=[
            VMEM(amplitudes.shape, jnp.bfloat16),
            pltpu.SemaphoreType.DMA((nblock,)),
        ],
        compiler_params=pltpu.CompilerParams(vmem_limit_bytes=60 * 2**20),
        name="pack",
    )(amp_mask, amplitudes)


def list_kernel(half_ref, mask_ref, list_ref):
    nab, ntile = mask_ref.shape
    steps, size, rows_at, steps_at = list_sizes(nab, ntile)
    first = (1 - half_ref[0]) * (nab // 2)
    none = jnp.int32(ntile)

    def clear(k, carry):
        for u in range(GRP):
            list_ref[k * GRP + u] = none
        return carry

    lax.fori_loop(0, rows_at // GRP, clear, 0)
    for k in range(rows_at, steps_at):
        list_ref[k] = jnp.int32(0)

    def row(ii, base):
        i = lax.rem(ii + first, nab)
        at = base * RUN
        for t in range(ntile):
            here = mask_ref[i, t]
            list_ref[at] = jnp.where(here == 1, i * (ntile + 1) + t, none)
            at += here
        runs = (at - base * RUN + RUN - 1) // RUN

        def note(k, carry):
            list_ref[rows_at + base + k] = lax.rem(ii, nab // 2)
            return carry

        lax.fori_loop(0, runs, note, 0)
        return base + runs

    list_ref[steps_at] = jnp.int32(0)
    middle = lax.fori_loop(0, nab // 2, row, jnp.int32(0))
    middle = (middle + PAR - 1) // PAR
    list_ref[steps_at + 1] = middle
    end = lax.fori_loop(nab // 2, nab, row, middle * PAR)
    list_ref[steps_at + 2] = (end + PAR - 1) // PAR


def list_sizes(nab, ntile):
    runs = nab * ((ntile + RUN - 1) // RUN) + 2 * PAR
    rows_at = -(-(runs * RUN + 1) // GRP) * GRP
    return runs // PAR, rows_at + runs + 3, rows_at, rows_at + runs


def make_list(half, int_mask):
    nab, ntile = int_mask.shape
    return pl.pallas_call(
        list_kernel,
        out_shape=jax.ShapeDtypeStruct((list_sizes(nab, ntile)[1],), jnp.int32),
        in_specs=[smem(), smem()],
        out_specs=smem(),
        name="tile_list",
    )(half, int_mask)


def ladder_kernel(nchunk, per, nab, ntile, list_ref, int_ref, *rest):
    chunks, (other_ref, mine_ref), scratch = (
        rest[:nchunk],
        rest[nchunk : nchunk + 2],
        rest[nchunk + 2 :],
    )
    dense, bufs, meta_v, meta_s, sems, meta_sem = scratch
    group = RUN * PAR
    _, _, rows_at, steps_at = list_sizes(nab, ntile)
    groups = ntile // GRP
    slots = groups * KEPT
    total = list_ref[steps_at + 2]

    def start(n):
        slot = lax.rem(n, SLOTS)
        for u in range(group):
            at = list_ref[n * group + u]
            i, t = at // (ntile + 1), lax.rem(at, ntile + 1)
            t = jnp.minimum(t, ntile - 1)
            pltpu.make_async_copy(
                int_ref.at[
                    pl.ds(pl.multiple_of(i * TILE, TILE), TILE),
                    pl.ds(pl.multiple_of(t * TILE, TILE), TILE),
                ],
                bufs.at[slot, u],
                sems.at[slot],
            ).start()

    for n in range(SLOTS):

        @pl.when(n < total)
        def _():
            start(n)

    for c in range(nchunk):
        head = chunks[c][per * slots * PIECE :, :].astype(jnp.float32)
        meta_v[c * 8 : (c + 1) * 8, :] = head[:8].astype(jnp.int32)
    copy = pltpu.make_async_copy(meta_v, meta_s, meta_sem)
    copy.start()
    other_ref[...] = jnp.zeros_like(other_ref)
    mine_ref[...] = jnp.zeros_like(mine_ref)
    dense[ntile] = jnp.zeros(dense.shape[1:], jnp.bfloat16)
    copy.wait()
    zero = jnp.zeros((IJ_BLK, LANES), jnp.bfloat16)
    for c in range(nchunk):
        for q in range(per):
            row = (c * per + q) * IJ_BLK
            for g in range(groups):
                bits = meta_s[c * 8, q * groups + g]
                count = jnp.int32(0)
                for j in range(GRP):
                    here = (bits >> j) & 1
                    base = (
                        q * slots + g * KEPT + jnp.minimum(count, KEPT - 1)
                    ) * PIECE
                    for half in range(2):
                        at = pl.multiple_of(base + half * IJ_BLK, IJ_BLK)
                        tile = chunks[c][pl.ds(at, IJ_BLK), :]
                        dense[
                            g * GRP + j,
                            row : row + IJ_BLK,
                            half * LANES : (half + 1) * LANES,
                        ] = jnp.where(here == 1, tile, zero)
                    count += here

    for side, out in enumerate((other_ref, mine_ref)):

        def step(n, carry):
            slot = lax.rem(n, SLOTS)
            pltpu.make_async_copy(bufs.at[slot], bufs.at[slot], sems.at[slot]).wait()
            parts = []
            for r in range(PAR):
                acc = None
                for u in range(r * RUN, (r + 1) * RUN):
                    t = lax.rem(list_ref[n * group + u], ntile + 1)
                    part = lax.dot_general(
                        dense[t],
                        bufs[slot, u],
                        (((1,), (1,)), ((), ())),
                        preferred_element_type=jnp.float32,
                    )
                    acc = part if acc is None else acc + part
                parts.append(acc)
            for r in range(PAR):
                left = pl.multiple_of(list_ref[rows_at + n * PAR + r] * TILE, TILE)
                out[:, pl.ds(left, TILE)] += parts[r]

            @pl.when(n + SLOTS < total)
            def _():
                start(n + SLOTS)

            return carry

        lax.fori_loop(list_ref[steps_at + side], list_ref[steps_at + side + 1], step, 0)


def ladder(chunks, tile_list, integrals):
    nchunk = len(chunks)
    rows_ab, rows_cd = integrals.shape
    ntile = rows_cd // TILE
    per = (chunks[0].shape[0] - META) // (ntile // 2 * PIECE)
    m = nchunk * per * IJ_BLK
    out = jax.ShapeDtypeStruct((m, rows_ab // 2), jnp.float32)
    return pl.pallas_call(
        functools.partial(ladder_kernel, nchunk, per, rows_ab // TILE, ntile),
        out_shape=[out, out],
        in_specs=[smem(), pl.BlockSpec(memory_space=pl.ANY)]
        + [vmem()] * nchunk,
        out_specs=[vmem(), vmem()],
        scratch_shapes=[
            VMEM((ntile + 1, m, TILE), jnp.bfloat16),
            VMEM((SLOTS, RUN * PAR, TILE, TILE), jnp.bfloat16),
            VMEM((nchunk * 8, LANES), jnp.int32),
            SMEM((nchunk * 8, LANES), jnp.int32),
            pltpu.SemaphoreType.DMA((SLOTS,)),
            pltpu.SemaphoreType.DMA,
        ],
        compiler_params=pltpu.CompilerParams(vmem_limit_bytes=24 * 2**20),
        cost_estimate=pl.CostEstimate(
            flops=2 * m * rows_ab * rows_cd,
            bytes_accessed=rows_ab * rows_cd,
            transcendentals=0,
        ),
        name="ladder",
    )(tile_list, integrals, *chunks)


def code_kernel(mine_ref, got_ref, sum_ref, code_ref):
    rows, width = mine_ref.shape

    def step(b, carry):
        at = pl.ds(pl.multiple_of(b * IJ_BLK, IJ_BLK), IJ_BLK)
        total = mine_ref[at, :] + got_ref[at, :]
        sum_ref[at, :] = total
        peak = jnp.max(jnp.abs(total), axis=1, keepdims=True)
        level = jnp.ceil(jnp.log(jnp.maximum(peak, FLOOR)) * (OCTAVE / LN2))
        up = jnp.exp(level * (-LN2 / OCTAVE)) * TOP
        code_ref[at, :width] = (
            jnp.round(total * up).astype(jnp.int32).astype(jnp.int16)
        )
        code_ref[at, width:] = jnp.broadcast_to(
            level.astype(jnp.int32), (IJ_BLK, LANES)
        ).astype(jnp.int16)
        return carry

    lax.fori_loop(0, rows // IJ_BLK, step, 0)


def code(mine, got):
    rows, width = mine.shape
    return pl.pallas_call(
        code_kernel,
        out_shape=[
            jax.ShapeDtypeStruct((rows, width), jnp.float32),
            jax.ShapeDtypeStruct((rows, width + LANES), jnp.int16),
        ],
        in_specs=[vmem()] * 2,
        out_specs=[vmem()] * 2,
        compiler_params=pltpu.CompilerParams(vmem_limit_bytes=16 * 2**20),
        name="code",
    )(mine, got)


def final_kernel(
    nsum, npeer, blocks, n, ncol, src_ref, place_ref, occ_ref, vir_ref, *rest
):
    sums, codes, out = (
        rest[:nsum],
        [
            rest[nsum + j * npeer : nsum + (j + 1) * npeer]
            for j in range(nsum)
        ],
        rest[-1],
    )
    width = vir_ref.shape[1]
    chip, half = place_ref[0], place_ref[1]
    rows_out = out.shape[1]
    vir = vir_ref[...]
    for j, batch in enumerate(blocks):
        for b, (which, block) in enumerate(batch):
            src = src_ref[which]
            owner = src * ncol // n
            row = lax.rem(src, n // ncol) * (rows_out * ncol // n) + block * IJ_BLK
            at = slice(b * IJ_BLK, (b + 1) * IJ_BLK)

            @pl.when(owner // 2 == chip)
            def _():
                side = lax.rem(owner + half, 2)
                to = pl.multiple_of(row, IJ_BLK)
                total = sums[j][at, :]
                for got in codes[j]:
                    level = got[at, width:].astype(jnp.int32).astype(jnp.float32)
                    down = jnp.exp(level[:, :1] * (LN2 / OCTAVE)) * (1.0 / TOP)
                    coded = got[at, :width].astype(jnp.int32).astype(jnp.float32)
                    total = total + coded * down
                denom = vir - occ_ref[side, pl.ds(to, IJ_BLK), :]
                out[side, pl.ds(to, IJ_BLK), :] = (total / denom).astype(out.dtype)


def final(sums, codes, blocks, n, ncol, src, place, occ, vir, so_far):
    npeer = len(codes[0])
    flat = [c for batch in codes for c in batch]
    width = vir.shape[1]
    more = [] if so_far is None else [so_far]
    return pl.pallas_call(
        functools.partial(final_kernel, len(sums), npeer, blocks, n, ncol),
        out_shape=jax.ShapeDtypeStruct((2, occ.shape[1], width), jnp.bfloat16),
        in_specs=[smem(), smem()] + [vmem()] * (2 + len(sums) + len(flat) + len(more)),
        out_specs=vmem(),
        input_output_aliases={4 + len(sums) + len(flat): 0} if more else {},
        compiler_params=pltpu.CompilerParams(vmem_limit_bytes=32 * 2**20),
        name="final",
    )(src, place, occ, vir, *sums, *flat, *more)


def body(n, ncol, amplitudes, amp_mask, integrals, int_mask, occ_energy, vir_energy):
    cycle = list(range(0, n, 2)) + list(range(n - 1, 0, -2))
    ahead = [(cycle[p], cycle[(p + 1) % n]) for p in range(n)]
    behind = [(b, a) for a, b in ahead]
    row, col = lax.axis_index("row"), lax.axis_index("col")
    half = lax.rem(col, 2)
    core = [(c, c ^ 1) for c in range(ncol)]
    nblock = amp_mask.shape[0]
    per = nblock // FLOWS
    table = [None] * n
    for p in range(n):
        table[cycle[p]] = [cycle[p]] + [
            cycle[(p + sign * s) % n] for s in range(1, n) for sign in (-1, 1)
        ]
    src = jnp.array(table, jnp.int32)[row]
    place = jnp.stack([col // 2, half]).astype(jnp.int32)
    width = integrals.shape[0] // 2

    flows = pack(amplitudes, amp_mask)
    tile_list = make_list(half.reshape(1).astype(jnp.int32), int_mask)
    occ_other = lax.ppermute(occ_energy, "col", core)
    occ = jnp.stack([occ_energy, occ_other])[:, :, None]
    vir = lax.dynamic_slice_in_dim(vir_energy, half * width, width)[None, :]

    def tie(arrays, others):
        return lax.optimization_barrier((arrays, others))

    def ladder_of(steps, coded):
        batch = [part for s in steps for part in parts[s]]
        other, mine = ladder([c for c, _, _ in batch], tile_list, integrals)
        if coded:
            total, peers, blocks = coded.pop()
            other, peers = tie(other, peers)
            coded.append((total, peers, blocks))
        blocks = [(which, b + q) for _, which, b in batch for q in range(per)]
        return lax.ppermute(other, "col", core), mine, blocks

    def code_of(got, mine, blocks):
        total, coded = code(mine, got)
        peers = [
            lax.ppermute(coded, "col", [(c, c ^ (2 * d)) for c in range(ncol)])
            for d in range(1, ncol // 2)
        ]
        return total, peers, blocks

    def final_of(coded, so_far):
        sums, codes, blocks = zip(*coded, strict=True)
        return final(sums, codes, blocks, n, ncol, src, place, occ, vir, so_far)

    parts = [[(flows[f], 0, f * per) for f in range(FLOWS)]]
    held = list(flows)
    waiting, coded = None, []
    for s in range(1, n):
        sent = [
            lax.ppermute(h, "row", ahead if f < FLOWS // 2 else behind)
            for f, h in enumerate(held)
        ]
        if s == 1:
            fixed = [tile_list, occ, vir, src, place]
            held, (tile_list, occ, vir, src, place) = tie(sent, fixed)
        elif s % 2 == 0:
            waiting = ladder_of([s - 2, s - 1], coded)
            held, mine = tie(sent, waiting[1])
            waiting = (waiting[0], mine, waiting[2])
        else:
            total, peers, blocks = code_of(*waiting)
            held, total = tie(sent, total)
            coded.append((total, peers, blocks))
        parts.append(
            [
                (h, 2 * s - 1 + (f >= FLOWS // 2), f * per)
                for f, h in enumerate(held)
            ]
        )
    last = code_of(*ladder_of([n - 2, n - 1], coded))
    done = final_of([last], final_of(coded, None))
    mine, theirs = done[0], done[1]
    got = lax.ppermute(theirs, "col", core)
    return jnp.where(
        half == 0,
        jnp.concatenate([mine, got], axis=1),
        jnp.concatenate([got, mine], axis=1),
    )


def solution(mesh):
    return jax.shard_map(
        functools.partial(body, mesh.shape["row"], mesh.shape["col"]),
        mesh=mesh,
        in_specs=(
            P("row", "col"),
            P("row", "col"),
            P("row", "col"),
            P("row", "col"),
            P("col"),
            P("row"),
        ),
        out_specs=P("col", "row"),
        check_vma=False,
    )
```

time: 309 us -> 158 us (0.51)
  the two profiles are of different devices: /device:TPU:17 before, /device:TPU:0 now
where the time goes in v2:
time: 158 us; the launch traced here: 157 us
  Pallas kernels  65.5 us (41%)
  waiting for transfers between devices  65 us (41%)
  starting transfers between devices  17.3 us (11%)
  local copies, waits for them, and re-layouts  7.85 us (5%)
    pallas_call x4, Pallas kernels, ladder(): pl.pallas_call(functools.partial(ladder_kernel, nchunk, per, rows_ab // T...  50.5 us
    ppermute x14, waiting for transfers between devices, body(): lax.ppermute(h, 'row', ahead if f < FLOWS // 2 else behind)  46.5 us
    ppermute x14, starting transfers between devices, body(): lax.ppermute(h, 'row', ahead if f < FLOWS // 2 else behind)  15.8 us
    ppermute x4, waiting for transfers between devices, code_of(): lax.ppermute(coded, 'col', [(c, c ^ 2 * d) for c in range(ncol)])  12.3 us
    unnamed x26, local copies, waits for them, and re-layouts  6.93 us
    pallas_call x4, Pallas kernels, code(): pl.pallas_call(code_kernel, out_shape=[jax.ShapeDtypeStruct((rows, width)...  4.6 us
    ppermute x4, waiting for transfers between devices, ladder_of(): return (lax.ppermute(other, 'col', core), mine, blocks)  4.3 us
    pallas_call x1, Pallas kernels, pack(): pl.pallas_call(pack_kernel, out_shape=[jax.ShapeDtypeStruct((rows, LANES)...  3.97 us
  transfers between devices with their start and end apart: 24, of which 15 were waited for; matrix products, arithmetic and copies ran while one was open for 1% of the time, Pallas kernels for 37%

profile of v2, /device:TPU:0, one launch (start us, length us, event | category | flops | bytes accessed | tf_op | source)
XLA Modules:
  0.0 157.3 jit_solution(16271736540686306011)
XLA Ops:
  0.0 4.0 %pack.1 = (bf16[2064,128]{1,0:T(8,128)(2,1)}, bf16[2064,128]{1,0:T(8,128)(2,1)}) custom-call(s32[4,32]{1,0:T(4,128)} %mask_ref.2, bf16[128,8192]{1,0:T(8,128)(2,1)} %amp_ref.1), custom_call_target="tpu_custom_call" | custom-call | tf_op jit(solution)/shard_map/pack/pallas_call | solution.py:85
  4.0 3.1 %collective-permute-start = (bf16[2064,128]{1,0:T(8,128)(2,1)}, bf16[2064,128]{1,0:T(8,128)(2,1)S(1)}, u32[]{:S(2)}, u32[]{:S(2)}) collective-permute-start(bf16[2064,128]{1,0:T(8,128)(2,1)} %get-tuple-element.54.rest_0_), channel_id=1, source_target_pairs={{0,8},{8,16},{16,24},{24,28},{28,20},{20,12},{12,4},{4,0},{1,9},{9... | collective-permute-start | bytes 1585160 | tf_op jit(solution)/shard_map/ppermute | solution.py:424
  7.2 0.7 dynamic-slice_bitcast_fusion.src_ref
  7.9 2.6 %tile_list.1.list_ref = s32[371]{0:T(512)} custom-call(s32[1]{0:T(128)} %bitcast.half_ref, s32[8,32]{1,0:T(8,128)} %mask_ref.3), custom_call_target="tpu_custom_call" | custom-call | tf_op jit(solution)/shard_map/tile_list/pallas_call | solution.py:146
  10.5 8.7 %collective-permute-done.rest_2_ = bf16[2064,128]{1,0:T(8,128)(2,1)S(1)} collective-permute-done((bf16[2064,128]{1,0:T(8,128)(2,1)}, bf16[2064,128]{1,0:T(8,128)(2,1)S(1)}, u32[]{:S(2)}, u32[]{:S(2)}) %collective-permute-start) | collective-permute-done | bytes 528416 | tf_op jit(solution)/shard_map/ppermute | solution.py:424
  19.2 1.5 collective-permute-done.1.rest_3_
  20.7 1.6 collective-permute-start.3
  22.3 0.5 collective-permute-start.4
  22.8 1.0 copy-done.8
  23.8 1.0 copy-done.9
  24.9 0.7 copy-done.10
  25.5 12.6 %ladder.4 = (f32[256,1024]{1,0:T(8,128)S(1)}, f32[256,1024]{1,0:T(8,128)S(1)}) custom-call(s32[371]{0:T(512)S(1)} %copy-done.10, bf16[2048,8192]{1,0:T(8,128)(2,1)} %int_ref.7, bf16[2064,128]{1,0:T(8,128)(2,1)S(1)} %copy-done.8, bf16[2064,128]{1,0:T(8,128)(2,1)S(1)} %copy-done.9, bf16[2064,128]{1,0:T(8,128)(2,1)S(1)} %collective-permute-done.rest_2_, ...), custom_call_target="tpu_custom_call" | custom-call | flops 8589934592 | bytes 16777216 | tf_op jit(solution)/shard_map/ladder/pallas_call | solution.py:258
  38.2 0.6 collective-permute-start.5
  38.9 1.4 collective-permute-start.6
  40.3 0.5 collective-permute-done.7.got_ref
  40.8 0.9 code.4
  41.8 0.6 collective-permute-start.12
  42.4 10.3 %collective-permute-done.5.rest_2_ = bf16[2064,128]{1,0:T(8,128)(2,1)S(1)} collective-permute-done((bf16[2064,128]{1,0:T(8,128)(2,1)S(1)}, bf16[2064,128]{1,0:T(8,128)(2,1)S(1)}, u32[]{:S(2)}, u32[]{:S(2)}) %collective-permute-start.5) | collective-permute-done | bytes 528416 | tf_op jit(solution)/shard_map/ppermute | solution.py:424
  52.6 1.1 collective-permute-done.6.rest_3_
  53.7 1.7 %collective-permute-start.8 = (bf16[2064,128]{1,0:T(8,128)(2,1)S(1)}, bf16[2064,128]{1,0:T(8,128)(2,1)S(1)}, u32[]{:S(2)}, u32[]{:S(2)}) collective-permute-start(bf16[2064,128]{1,0:T(8,128)(2,1)S(1)} %collective-permute-done.5.rest_2_), channel_id=1, source_target_pairs={{0,8},{8,16},{16,24},{24,28},{28,20},{20,12},{12,4},{4,0},{1,9},{9... | collective-permute-start | bytes 1585160 | tf_op jit(solution)/shard_map/ppermute | solution.py:424
  55.8 12.6 %ladder.5 = (f32[256,1024]{1,0:T(8,128)S(1)}, f32[256,1024]{1,0:T(8,128)S(1)}) custom-call(s32[371]{0:T(512)S(1)} %copy-done.10, bf16[2048,8192]{1,0:T(8,128)(2,1)} %int_ref.7, bf16[2064,128]{1,0:T(8,128)(2,1)S(1)} %collective-permute-done.3.rest_0_, bf16[2064,128]{1,0:T(8,128)(2,1)S(1)} %collective-permute-done.4.rest_1_, ...), custom_call_target="tpu_custom_call" | custom-call | flops 8589934592 | bytes 16777216 | tf_op jit(solution)/shard_map/ladder/pallas_call | solution.py:258
  68.5 1.7 %collective-permute-start.10 = (bf16[2064,128]{1,0:T(8,128)(2,1)S(1)}, bf16[2064,128]{1,0:T(8,128)(2,1)S(1)}, u32[]{:S(2)}, u32[]{:S(2)}) collective-permute-start(bf16[2064,128]{1,0:T(8,128)(2,1)S(1)} %collective-permute-done.8.rest_0_), channel_id=1, source_target_pairs={{0,8},{8,16},{16,24},{24,28},{28,20},{20,12},{12,4},{4,0},{1,9},{9... | collective-permute-start | bytes 1585160 | tf_op jit(solution)/shard_map/ppermute | solution.py:424
  70.1 0.4 collective-permute-start.11
  70.5 0.5 collective-permute-done.13.got_ref
  71.1 0.9 code.5
  72.0 10.8 %collective-permute-done.10.rest_2_ = bf16[2064,128]{1,0:T(8,128)(2,1)S(1)} collective-permute-done((bf16[2064,128]{1,0:T(8,128)(2,1)S(1)}, bf16[2064,128]{1,0:T(8,128)(2,1)S(1)}, u32[]{:S(2)}, u32[]{:S(2)}) %collective-permute-start.10) | collective-permute-done | bytes 528416 | tf_op jit(solution)/shard_map/ppermute | solution.py:424
  82.9 1.4 collective-permute-done.11.rest_3_
  84.6 2.4 %collective-permute-start.14 = (bf16[2064,128]{1,0:T(8,128)(2,1)S(1)}, bf16[2064,128]{1,0:T(8,128)(2,1)S(1)}, u32[]{:S(2)}, u32[]{:S(2)}) collective-permute-start(bf16[2064,128]{1,0:T(8,128)(2,1)S(1)} %collective-permute-done.10.rest_2_), channel_id=1, source_target_pairs={{0,8},{8,16},{16,24},{24,28},{28,20},{20,12},{12,4},{4,0},{1,9},{9... | collective-permute-start | bytes 1585160 | tf_op jit(solution)/shard_map/ppermute | solution.py:424
  87.0 12.7 %ladder.6 = (f32[256,1024]{1,0:T(8,128)S(1)}, f32[256,1024]{1,0:T(8,128)S(1)}) custom-call(s32[371]{0:T(512)S(1)} %copy-done.10, bf16[2048,8192]{1,0:T(8,128)(2,1)} %int_ref.7, bf16[2064,128]{1,0:T(8,128)(2,1)S(1)} %collective-permute-done.8.rest_0_, bf16[2064,128]{1,0:T(8,128)(2,1)S(1)} %collective-permute-done.9.rest_1_, ...), custom_call_target="tpu_custom_call" | custom-call | flops 8589934592 | bytes 16777216 | tf_op jit(solution)/shard_map/ladder/pallas_call | solution.py:258
  99.9 1.5 collective-permute-start.16
  101.5 0.5 collective-permute-start.17
  102.0 0.5 collective-permute-done.19.got_ref
  102.6 0.9 code.6
  103.5 10.8 %collective-permute-done.16.rest_2_ = bf16[2064,128]{1,0:T(8,128)(2,1)S(1)} collective-permute-done((bf16[2064,128]{1,0:T(8,128)(2,1)S(1)}, bf16[2064,128]{1,0:T(8,128)(2,1)S(1)}, u32[]{:S(2)}, u32[]{:S(2)}) %collective-permute-start.16) | collective-permute-done | bytes 528416 | tf_op jit(solution)/shard_map/ppermute | solution.py:424
  114.3 1.8 %collective-permute-done.17.rest_3_ = bf16[2064,128]{1,0:T(8,128)(2,1)S(1)} collective-permute-done((bf16[2064,128]{1,0:T(8,128)(2,1)S(1)}, bf16[2064,128]{1,0:T(8,128)(2,1)S(1)}, u32[]{:S(2)}, u32[]{:S(2)}) %collective-permute-start.17) | collective-permute-done | bytes 528416 | tf_op jit(solution)/shard_map/ppermute | solution.py:424
  116.2 12.6 %ladder.7 = (f32[256,1024]{1,0:T(8,128)S(1)}, f32[256,1024]{1,0:T(8,128)S(1)}) custom-call(s32[371]{0:T(512)S(1)} %copy-done.10, bf16[2048,8192]{1,0:T(8,128)(2,1)} %int_ref.7, bf16[2064,128]{1,0:T(8,128)(2,1)S(1)} %collective-permute-done.14.rest_0_, bf16[2064,128]{1,0:T(8,128)(2,1)S(1)} %collective-permute-done.15.rest_1_, ...), custom_call_target="tpu_custom_call" | custom-call | flops 8589934592 | bytes 16777216 | tf_op jit(solution)/shard_map/ladder/pallas_call | solution.py:258
  128.8 2.3 %collective-permute-done.20.rest_5_ = s16[256,1152]{1,0:T(8,128)(2,1)S(1)} collective-permute-done((s16[256,1152]{1,0:T(8,128)(2,1)S(1)}, s16[256,1152]{1,0:T(8,128)(2,1)S(1)}, u32[]{:S(2)}, u32[]{:S(2)}) %collective-permute-start.20) | collective-permute-done | bytes 589856 | tf_op jit(solution)/shard_map/ppermute | solution.py:410
  131.0 2.7 %collective-permute-done.21.got_ref = f32[256,1024]{1,0:T(8,128)S(1)} collective-permute-done((f32[256,1024]{1,0:T(8,128)S(1)}, f32[256,1024]{1,0:T(8,128)S(1)}, u32[]{:S(2)}, u32[]{:S(2)}) %collective-permute-start.21) | collective-permute-done | bytes 1048608 | tf_op jit(solution)/shard_map/ppermute | solution.py:405
  133.7 1.8 %code.7 = (f32[256,1024]{1,0:T(8,128)S(1)}, s16[256,1152]{1,0:T(8,128)(2,1)}) custom-call(f32[256,1024]{1,0:T(8,128)S(1)} %get-tuple-element.91.mine_ref, f32[256,1024]{1,0:T(8,128)S(1)} %collective-permute-done.21.got_ref), custom_call_target="tpu_custom_call" | custom-call | tf_op jit(solution)/shard_map/code/pallas_call | solution.py:305
  135.4 1.0 copy-done
  136.9 1.1 copy-done.3
  137.9 1.1 copy-done.5
  139.0 1.1 copy-done.7
  140.1 2.0 %final.2.rest_2_ = bf16[2,256,1024]{2,1,0:T(8,128)(2,1)S(1)} custom-call(s32[15]{0:T(128)S(1)} %dynamic-slice_bitcast_fusion.src_ref, s32[2]{0:T(128)S(1)} %pad_add_fusion.place_ref, f32[2,256,1]{2,1,0:T(8,128)S(1)} %copy.10.occ_ref, f32[1,1024]{1,0:T(1,128)S(1)} %bitcast.13, f32[256,1024]{1,0:T(8,128)S(1)} %get-tuple-element.97.rest_0_, ...), custom_call_target="tpu_custom_call" | custom-call | tf_op jit(solution)/shard_map/final/pallas_call | solution.py:359
  142.0 10.1 %collective-permute-done.22.rest_1_ = s16[256,1152]{1,0:T(8,128)(2,1)} collective-permute-done((s16[256,1152]{1,0:T(8,128)(2,1)}, s16[256,1152]{1,0:T(8,128)(2,1)}, u32[]{:S(2)}, u32[]{:S(2)}) %collective-permute-start.22) | collective-permute-done | bytes 589856 | tf_op jit(solution)/shard_map/ppermute | solution.py:410
  152.1 1.8 %final.3 = bf16[2,256,1024]{2,1,0:T(8,128)(2,1)S(1)} custom-call(s32[15]{0:T(128)S(1)} %dynamic-slice_bitcast_fusion.src_ref, s32[2]{0:T(128)S(1)} %pad_add_fusion.place_ref, f32[2,256,1]{2,1,0:T(8,128)S(1)} %copy.10.occ_ref, f32[1,1024]{1,0:T(1,128)S(1)} %bitcast.14, f32[256,1024]{1,0:T(8,128)S(1)} %copy-done.1, ...), custom_call_target="tpu_custom_call", output_to_operand_aliasing={{}: (6, {})} | custom-call | tf_op jit(solution)/shard_map/final/pallas_call | solution.py:359
  154.1 1.9 %collective-permute-done.23 = bf16[256,1024]{1,0:T(8,128)(2,1)S(1)} collective-permute-done((bf16[256,1024]{1,0:T(8,128)(2,1)S(1)}, bf16[256,1024]{1,0:T(8,128)(2,1)S(1)}, u32[]{:S(2)}, u32[]{:S(2)}) %collective-permute-start.23) | collective-permute-done | bytes 524320 | tf_op jit(solution)/shard_map/ppermute | solution.py:447
  156.0 1.4 maximum_select_fusion
  (45 shorter events, 1.6 us)
Async XLA Ops:
  0.0 7.1 %copy-start.12 = (f32[256]{0:T(256)S(1)}, f32[256]{0:T(256)}, u32[]{:S(2)}) copy-start(f32[256]{0:T(256)} %param.11) | copy-start | bytes 3076
  0.0 10.5 %copy-start.11 = (f32[2048]{0:T(1024)S(1)}, f32[2048]{0:T(1024)}, u32[]{:S(2)}) copy-start(f32[2048]{0:T(1024)} %param.12) | copy-start | bytes 24580
  4.0 15.2 %collective-permute-start = (bf16[2064,128]{1,0:T(8,128)(2,1)}, bf16[2064,128]{1,0:T(8,128)(2,1)S(1)}, u32[]{:S(2)}, u32[]{:S(2)}) collective-permute-start(bf16[2064,128]{1,0:T(8,128)(2,1)} %get-tuple-element.54.rest_0_), channel_id=1, source_target_pairs={{0,8},{8,16},{16,24},{24,28},{28,20},{20,12},{12,4},{4,0},{1,9},{9... | collective-permute-start | bytes 1585160 | tf_op jit(solution)/shard_map/ppermute | solution.py:424
  7.1 13.7 %collective-permute-start.1 = (bf16[2064,128]{1,0:T(8,128)(2,1)}, bf16[2064,128]{1,0:T(8,128)(2,1)S(1)}, u32[]{:S(2)}, u32[]{:S(2)}) collective-permute-start(bf16[2064,128]{1,0:T(8,128)(2,1)} %get-tuple-element.55.rest_1_), channel_id=1, source_target_pairs={{8,0},{16,8},{24,16},{28,24},{20,28},{12,20},{4,12},{0,4},{9,1},{1... | collective-permute-start | bytes 1585160 | tf_op jit(solution)/shard_map/ppermute | solution.py:424
  7.1 3.5 %collective-permute-start.2 = (f32[256]{0:T(256)S(1)}, f32[256]{0:T(256)S(1)}, u32[]{:S(2)}, u32[]{:S(2)}) collective-permute-start(f32[256]{0:T(256)S(1)} %copy-done.12), channel_id=1, source_target_pairs={{0,1},{1,0},{2,3},{3,2},{4,5},{5,4},{6,7},{7,6},{8,9},{9,8},{10,11... | collective-permute-start | bytes 3080 | tf_op jit(solution)/shard_map/ppermute | solution.py:390
  20.7 17.4 %collective-permute-start.3 = (bf16[2064,128]{1,0:T(8,128)(2,1)S(1)}, bf16[2064,128]{1,0:T(8,128)(2,1)S(1)}, u32[]{:S(2)}, u32[]{:S(2)}) collective-permute-start(bf16[2064,128]{1,0:T(8,128)(2,1)S(1)} %collective-permute-done.rest_2_), channel_id=1, source_target_pairs={{0,8},{8,16},{16,24},{24,28},{28,20},{20,12},{12,4},{4,0},{1,9},{9... | collective-permute-start | bytes 1585160 | tf_op jit(solution)/shard_map/ppermute | solution.py:424
  22.3 15.9 %collective-permute-start.4 = (bf16[2064,128]{1,0:T(8,128)(2,1)S(1)}, bf16[2064,128]{1,0:T(8,128)(2,1)S(1)}, u32[]{:S(2)}, u32[]{:S(2)}) collective-permute-start(bf16[2064,128]{1,0:T(8,128)(2,1)S(1)} %collective-permute-done.1.rest_3_), channel_id=1, source_target_pairs={{8,0},{16,8},{24,16},{28,24},{20,28},{12,20},{4,12},{0,4},{9,1},{1... | collective-permute-start | bytes 1585160 | tf_op jit(solution)/shard_map/ppermute | solution.py:424
  22.8 1.0 copy-start.8
  23.8 1.0 copy-start.9
  24.9 0.7 copy-start.10
  38.1 2.7 %collective-permute-start.7 = (f32[256,1024]{1,0:T(8,128)S(1)}, f32[256,1024]{1,0:T(8,128)S(1)}, u32[]{:S(2)}, u32[]{:S(2)}) collective-permute-start(f32[256,1024]{1,0:T(8,128)S(1)} %get-tuple-element.67), channel_id=1, source_target_pairs={{0,1},{1,0},{2,3},{3,2},{4,5},{5,4},{6,7},{7,6},{8,9},{9,8},{10,11... | collective-permute-start | bytes 3145736 | tf_op jit(solution)/shard_map/ppermute | solution.py:405
  38.2 14.4 %collective-permute-start.5 = (bf16[2064,128]{1,0:T(8,128)(2,1)S(1)}, bf16[2064,128]{1,0:T(8,128)(2,1)S(1)}, u32[]{:S(2)}, u32[]{:S(2)}) collective-permute-start(bf16[2064,128]{1,0:T(8,128)(2,1)S(1)} %collective-permute-done.3.rest_0_), channel_id=1, source_target_pairs={{0,8},{8,16},{16,24},{24,28},{28,20},{20,12},{12,4},{4,0},{1,9},{9... | collective-permute-start | bytes 1585160 | tf_op jit(solution)/shard_map/ppermute | solution.py:424
  38.9 14.9 %collective-permute-start.6 = (bf16[2064,128]{1,0:T(8,128)(2,1)S(1)}, bf16[2064,128]{1,0:T(8,128)(2,1)S(1)}, u32[]{:S(2)}, u32[]{:S(2)}) collective-permute-start(bf16[2064,128]{1,0:T(8,128)(2,1)S(1)} %collective-permute-done.4.rest_1_), channel_id=1, source_target_pairs={{8,0},{16,8},{24,16},{28,24},{20,28},{12,20},{4,12},{0,4},{9,1},{1... | collective-permute-start | bytes 1585160 | tf_op jit(solution)/shard_map/ppermute | solution.py:424
  41.8 26.5 %collective-permute-start.12 = (s16[256,1152]{1,0:T(8,128)(2,1)S(1)}, s16[256,1152]{1,0:T(8,128)(2,1)S(1)}, u32[]{:S(2)}, u32[]{:S(2)}) collective-permute-start(s16[256,1152]{1,0:T(8,128)(2,1)S(1)} %get-tuple-element.76), channel_id=1, source_target_pairs={{0,2},{1,3},{2,0},{3,1},{4,6},{5,7},{6,4},{7,5},{8,10},{9,11},{10,... | collective-permute-start | bytes 1769480 | tf_op jit(solution)/shard_map/ppermute | solution.py:410
  53.7 14.7 %collective-permute-start.8 = (bf16[2064,128]{1,0:T(8,128)(2,1)S(1)}, bf16[2064,128]{1,0:T(8,128)(2,1)S(1)}, u32[]{:S(2)}, u32[]{:S(2)}) collective-permute-start(bf16[2064,128]{1,0:T(8,128)(2,1)S(1)} %collective-permute-done.5.rest_2_), channel_id=1, source_target_pairs={{0,8},{8,16},{16,24},{24,28},{28,20},{20,12},{12,4},{4,0},{1,9},{9... | collective-permute-start | bytes 1585160 | tf_op jit(solution)/shard_map/ppermute | solution.py:424
  55.5 13.0 %collective-permute-start.9 = (bf16[2064,128]{1,0:T(8,128)(2,1)S(1)}, bf16[2064,128]{1,0:T(8,128)(2,1)S(1)}, u32[]{:S(2)}, u32[]{:S(2)}) collective-permute-start(bf16[2064,128]{1,0:T(8,128)(2,1)S(1)} %collective-permute-done.6.rest_3_), channel_id=1, source_target_pairs={{8,0},{16,8},{24,16},{28,24},{20,28},{12,20},{4,12},{0,4},{9,1},{1... | collective-permute-start | bytes 1585160 | tf_op jit(solution)/shard_map/ppermute | solution.py:424
  68.3 31.5 %copy-start.2 = (s16[256,1152]{1,0:T(8,128)(2,1)}, s16[256,1152]{1,0:T(8,128)(2,1)S(1)}, u32[]{:S(2)}) copy-start(s16[256,1152]{1,0:T(8,128)(2,1)S(1)} %collective-permute-done.12.rest_3_) | copy-start | bytes 1769476
  68.4 2.7 %collective-permute-start.13 = (f32[256,1024]{1,0:T(8,128)S(1)}, f32[256,1024]{1,0:T(8,128)S(1)}, u32[]{:S(2)}, u32[]{:S(2)}) collective-permute-start(f32[256,1024]{1,0:T(8,128)S(1)} %get-tuple-element.77), channel_id=1, source_target_pairs={{0,1},{1,0},{2,3},{3,2},{4,5},{5,4},{6,7},{7,6},{8,9},{9,8},{10,11... | collective-permute-start | bytes 3145736 | tf_op jit(solution)/shard_map/ppermute | solution.py:405
  68.5 14.4 %collective-permute-start.10 = (bf16[2064,128]{1,0:T(8,128)(2,1)S(1)}, bf16[2064,128]{1,0:T(8,128)(2,1)S(1)}, u32[]{:S(2)}, u32[]{:S(2)}) collective-permute-start(bf16[2064,128]{1,0:T(8,128)(2,1)S(1)} %collective-permute-done.8.rest_0_), channel_id=1, source_target_pairs={{0,8},{8,16},{16,24},{24,28},{28,20},{20,12},{12,4},{4,0},{1,9},{9... | collective-permute-start | bytes 1585160 | tf_op jit(solution)/shard_map/ppermute | solution.py:424
  70.1 14.2 %collective-permute-start.11 = (bf16[2064,128]{1,0:T(8,128)(2,1)S(1)}, bf16[2064,128]{1,0:T(8,128)(2,1)S(1)}, u32[]{:S(2)}, u32[]{:S(2)}) collective-permute-start(bf16[2064,128]{1,0:T(8,128)(2,1)S(1)} %collective-permute-done.9.rest_1_), channel_id=1, source_target_pairs={{8,0},{16,8},{24,16},{28,24},{20,28},{12,20},{4,12},{0,4},{9,1},{1... | collective-permute-start | bytes 1585160 | tf_op jit(solution)/shard_map/ppermute | solution.py:424
  84.3 15.5 %collective-permute-start.18 = (s16[256,1152]{1,0:T(8,128)(2,1)S(1)}, s16[256,1152]{1,0:T(8,128)(2,1)S(1)}, u32[]{:S(2)}, u32[]{:S(2)}) collective-permute-start(s16[256,1152]{1,0:T(8,128)(2,1)S(1)} %get-tuple-element.86), channel_id=1, source_target_pairs={{0,2},{1,3},{2,0},{3,1},{4,6},{5,7},{6,4},{7,5},{8,10},{9,11},{10,... | collective-permute-start | bytes 1769480 | tf_op jit(solution)/shard_map/ppermute | solution.py:410
  84.6 15.3 %collective-permute-start.14 = (bf16[2064,128]{1,0:T(8,128)(2,1)S(1)}, bf16[2064,128]{1,0:T(8,128)(2,1)S(1)}, u32[]{:S(2)}, u32[]{:S(2)}) collective-permute-start(bf16[2064,128]{1,0:T(8,128)(2,1)S(1)} %collective-permute-done.10.rest_2_), channel_id=1, source_target_pairs={{0,8},{8,16},{16,24},{24,28},{28,20},{20,12},{12,4},{4,0},{1,9},{9... | collective-permute-start | bytes 1585160 | tf_op jit(solution)/shard_map/ppermute | solution.py:424
  87.0 12.9 %collective-permute-start.15 = (bf16[2064,128]{1,0:T(8,128)(2,1)S(1)}, bf16[2064,128]{1,0:T(8,128)(2,1)S(1)}, u32[]{:S(2)}, u32[]{:S(2)}) collective-permute-start(bf16[2064,128]{1,0:T(8,128)(2,1)S(1)} %collective-permute-done.11.rest_3_), channel_id=1, source_target_pairs={{8,0},{16,8},{24,16},{28,24},{20,28},{12,20},{4,12},{0,4},{9,1},{1... | collective-permute-start | bytes 1585160 | tf_op jit(solution)/shard_map/ppermute | solution.py:424
  99.8 28.9 %copy-start.4 = (s16[256,1152]{1,0:T(8,128)(2,1)}, s16[256,1152]{1,0:T(8,128)(2,1)S(1)}, u32[]{:S(2)}) copy-start(s16[256,1152]{1,0:T(8,128)(2,1)S(1)} %collective-permute-done.18.rest_4_) | copy-start | bytes 1769476
  99.8 2.7 %collective-permute-start.19 = (f32[256,1024]{1,0:T(8,128)S(1)}, f32[256,1024]{1,0:T(8,128)S(1)}, u32[]{:S(2)}, u32[]{:S(2)}) collective-permute-start(f32[256,1024]{1,0:T(8,128)S(1)} %get-tuple-element.87), channel_id=1, source_target_pairs={{0,1},{1,0},{2,3},{3,2},{4,5},{5,4},{6,7},{7,6},{8,9},{9,8},{10,11... | collective-permute-start | bytes 3145736 | tf_op jit(solution)/shard_map/ppermute | solution.py:405
  99.9 14.4 %collective-permute-start.16 = (bf16[2064,128]{1,0:T(8,128)(2,1)S(1)}, bf16[2064,128]{1,0:T(8,128)(2,1)S(1)}, u32[]{:S(2)}, u32[]{:S(2)}) collective-permute-start(bf16[2064,128]{1,0:T(8,128)(2,1)S(1)} %collective-permute-done.14.rest_0_), channel_id=1, source_target_pairs={{0,8},{8,16},{16,24},{24,28},{28,20},{20,12},{12,4},{4,0},{1,9},{9... | collective-permute-start | bytes 1585160 | tf_op jit(solution)/shard_map/ppermute | solution.py:424
  101.5 14.6 %collective-permute-start.17 = (bf16[2064,128]{1,0:T(8,128)(2,1)S(1)}, bf16[2064,128]{1,0:T(8,128)(2,1)S(1)}, u32[]{:S(2)}, u32[]{:S(2)}) collective-permute-start(bf16[2064,128]{1,0:T(8,128)(2,1)S(1)} %collective-permute-done.15.rest_1_), channel_id=1, source_target_pairs={{8,0},{16,8},{24,16},{28,24},{20,28},{12,20},{4,12},{0,4},{9,1},{1... | collective-permute-start | bytes 1585160 | tf_op jit(solution)/shard_map/ppermute | solution.py:424
  116.1 14.9 %collective-permute-start.20 = (s16[256,1152]{1,0:T(8,128)(2,1)S(1)}, s16[256,1152]{1,0:T(8,128)(2,1)S(1)}, u32[]{:S(2)}, u32[]{:S(2)}) collective-permute-start(s16[256,1152]{1,0:T(8,128)(2,1)S(1)} %get-tuple-element.93), channel_id=1, source_target_pairs={{0,2},{1,3},{2,0},{3,1},{4,6},{5,7},{6,4},{7,5},{8,10},{9,11},{10,... | collective-permute-start | bytes 1769480 | tf_op jit(solution)/shard_map/ppermute | solution.py:410
  131.0 5.4 %copy-start.6 = (s16[256,1152]{1,0:T(8,128)(2,1)}, s16[256,1152]{1,0:T(8,128)(2,1)S(1)}, u32[]{:S(2)}) copy-start(s16[256,1152]{1,0:T(8,128)(2,1)S(1)} %collective-permute-done.20.rest_5_) | copy-start | bytes 1769476
  131.0 2.7 %collective-permute-start.21 = (f32[256,1024]{1,0:T(8,128)S(1)}, f32[256,1024]{1,0:T(8,128)S(1)}, u32[]{:S(2)}, u32[]{:S(2)}) collective-permute-start(f32[256,1024]{1,0:T(8,128)S(1)} %get-tuple-element.94), channel_id=1, source_target_pairs={{0,1},{1,0},{2,3},{3,2},{4,5},{5,4},{6,7},{7,6},{8,9},{9,8},{10,11... | collective-permute-start | bytes 3145736 | tf_op jit(solution)/shard_map/ppermute | solution.py:405
  135.4 1.0 copy-start
  136.4 15.7 %collective-permute-start.22 = (s16[256,1152]{1,0:T(8,128)(2,1)}, s16[256,1152]{1,0:T(8,128)(2,1)}, u32[]{:S(2)}, u32[]{:S(2)}) collective-permute-start(s16[256,1152]{1,0:T(8,128)(2,1)} %get-tuple-element.96), channel_id=1, source_target_pairs={{0,2},{1,3},{2,0},{3,1},{4,6},{5,7},{6,4},{7,5},{8,10},{9,11},{10,... | collective-permute-start | bytes 1769480 | tf_op jit(solution)/shard_map/ppermute | solution.py:410
  136.9 1.1 copy-start.3
  137.9 1.1 copy-start.5
  139.0 1.1 copy-start.7
  140.1 12.1 %copy-start.1 = (f32[256,1024]{1,0:T(8,128)S(1)}, f32[256,1024]{1,0:T(8,128)}, u32[]{:S(2)}) copy-start(f32[256,1024]{1,0:T(8,128)} %copy-done) | copy-start | bytes 3145732
  154.0 2.0 %collective-permute-start.23 = (bf16[256,1024]{1,0:T(8,128)(2,1)S(1)}, bf16[256,1024]{1,0:T(8,128)(2,1)S(1)}, u32[]{:S(2)}, u32[]{:S(2)}) collective-permute-start(bf16[256,1024]{1,0:T(8,128)(2,1)S(1)} %get-tuple-element.104), channel_id=1, source_target_pairs={{0,1},{1,0},{2,3},{3,2},{4,5},{5,4},{6,7},{7,6},{8,9},{9,8},{10,11... | collective-permute-start | bytes 1572872 | tf_op jit(solution)/shard_map/ppermute | solution.py:447

commit v3 on v2

--- a/solution.py
+++ b/solution.py
@@ -91,7 +91,7 @@
             VMEM(amplitudes.shape, jnp.bfloat16),
             pltpu.SemaphoreType.DMA((nblock,)),
         ],
-        compiler_params=pltpu.CompilerParams(vmem_limit_bytes=60 * 2**20),
+        compiler_params=pltpu.CompilerParams(vmem_limit_bytes=16 * 2**20),
         name="pack",
     )(amp_mask, amplitudes)
 
@@ -152,18 +152,19 @@
     )(half, int_mask)
 
 
-def ladder_kernel(nchunk, per, nab, ntile, list_ref, int_ref, *rest):
-    chunks, (other_ref, mine_ref), scratch = (
+def ladder_kernel(nchunk, per, nab, ntile, sides, list_ref, int_ref, *rest):
+    chunks, outs, scratch = (
         rest[:nchunk],
-        rest[nchunk : nchunk + 2],
-        rest[nchunk + 2 :],
+        rest[nchunk : nchunk + len(sides)],
+        rest[nchunk + len(sides) :],
     )
     dense, bufs, meta_v, meta_s, sems, meta_sem = scratch
     group = RUN * PAR
     _, _, rows_at, steps_at = list_sizes(nab, ntile)
     groups = ntile // GRP
     slots = groups * KEPT
-    total = list_ref[steps_at + 2]
+    begin = list_ref[steps_at + sides[0]]
+    total = list_ref[steps_at + sides[-1] + 1]
 
     def start(n):
         slot = lax.rem(n, SLOTS)
@@ -182,17 +183,17 @@
 
     for n in range(SLOTS):
 
-        @pl.when(n < total)
+        @pl.when(begin + n < total)
         def _():
-            start(n)
+            start(begin + n)
 
     for c in range(nchunk):
         head = chunks[c][per * slots * PIECE :, :].astype(jnp.float32)
         meta_v[c * 8 : (c + 1) * 8, :] = head[:8].astype(jnp.int32)
     copy = pltpu.make_async_copy(meta_v, meta_s, meta_sem)
     copy.start()
-    other_ref[...] = jnp.zeros_like(other_ref)
-    mine_ref[...] = jnp.zeros_like(mine_ref)
+    for out in outs:
+        out[...] = jnp.zeros_like(out)
     dense[ntile] = jnp.zeros(dense.shape[1:], jnp.bfloat16)
     copy.wait()
     zero = jnp.zeros((IJ_BLK, LANES), jnp.bfloat16)
@@ -217,7 +218,7 @@
                         ] = jnp.where(here == 1, tile, zero)
                     count += here
 
-    for side, out in enumerate((other_ref, mine_ref)):
+    for side, out in zip(sides, outs, strict=True):
 
         def step(n, carry):
             slot = lax.rem(n, SLOTS)
@@ -248,7 +249,7 @@
         lax.fori_loop(list_ref[steps_at + side], list_ref[steps_at + side + 1], step, 0)
 
 
-def ladder(chunks, tile_list, integrals):
+def ladder(chunks, tile_list, integrals, sides):
     nchunk = len(chunks)
     rows_ab, rows_cd = integrals.shape
     ntile = rows_cd // TILE
@@ -256,11 +257,11 @@
     m = nchunk * per * IJ_BLK
     out = jax.ShapeDtypeStruct((m, rows_ab // 2), jnp.float32)
     return pl.pallas_call(
-        functools.partial(ladder_kernel, nchunk, per, rows_ab // TILE, ntile),
-        out_shape=[out, out],
+        functools.partial(ladder_kernel, nchunk, per, rows_ab // TILE, ntile, sides),
+        out_shape=[out] * len(sides),
         in_specs=[smem(), pl.BlockSpec(memory_space=pl.ANY)]
         + [vmem()] * nchunk,
-        out_specs=[vmem(), vmem()],
+        out_specs=[vmem()] * len(sides),
         scratch_shapes=[
             VMEM((ntile + 1, m, TILE), jnp.bfloat16),
             VMEM((SLOTS, RUN * PAR, TILE, TILE), jnp.bfloat16),
@@ -269,63 +270,58 @@
             pltpu.SemaphoreType.DMA((SLOTS,)),
             pltpu.SemaphoreType.DMA,
         ],
-        compiler_params=pltpu.CompilerParams(vmem_limit_bytes=24 * 2**20),
+        compiler_params=pltpu.CompilerParams(vmem_limit_bytes=30 * 2**20),
         cost_estimate=pl.CostEstimate(
-            flops=2 * m * rows_ab * rows_cd,
-            bytes_accessed=rows_ab * rows_cd,
+            flops=len(sides) * m * rows_ab * rows_cd,
+            bytes_accessed=len(sides) * rows_ab * rows_cd // 2,
             transcendentals=0,
         ),
         name="ladder",
     )(tile_list, integrals, *chunks)
 
 
-def code_kernel(mine_ref, got_ref, sum_ref, code_ref):
-    rows, width = mine_ref.shape
-
-    def step(b, carry):
-        at = pl.ds(pl.multiple_of(b * IJ_BLK, IJ_BLK), IJ_BLK)
-        total = mine_ref[at, :] + got_ref[at, :]
-        sum_ref[at, :] = total
-        peak = jnp.max(jnp.abs(total), axis=1, keepdims=True)
-        level = jnp.ceil(jnp.log(jnp.maximum(peak, FLOOR)) * (OCTAVE / LN2))
-        up = jnp.exp(level * (-LN2 / OCTAVE)) * TOP
-        code_ref[at, :width] = (
-            jnp.round(total * up).astype(jnp.int32).astype(jnp.int16)
-        )
-        code_ref[at, width:] = jnp.broadcast_to(
-            level.astype(jnp.int32), (IJ_BLK, LANES)
-        ).astype(jnp.int16)
-        return carry
-
-    lax.fori_loop(0, rows // IJ_BLK, step, 0)
-
-
-def code(mine, got):
+def code_kernel(pieces, mine_ref, got_ref, sum_ref, *code_refs):
+    width = mine_ref.shape[1]
+    above = 0
+    for rows, code_ref in zip(pieces, code_refs, strict=True):
+
+        def step(b, carry, above=above, code_ref=code_ref):
+            row = pl.multiple_of(b * IJ_BLK, IJ_BLK)
+            at, to = pl.ds(above + row, IJ_BLK), pl.ds(row, IJ_BLK)
+            total = mine_ref[at, :] + got_ref[at, :]
+            sum_ref[at, :] = total
+            peak = jnp.max(jnp.abs(total), axis=1, keepdims=True)
+            level = jnp.ceil(jnp.log(jnp.maximum(peak, FLOOR)) * (OCTAVE / LN2))
+            up = jnp.exp(level * (-LN2 / OCTAVE)) * TOP
+            code_ref[to, :width] = (
+                jnp.round(total * up).astype(jnp.int32).astype(jnp.int16)
+            )
+            code_ref[to, width:] = jnp.broadcast_to(
+                level.astype(jnp.int32), (IJ_BLK, LANES)
+            ).astype(jnp.int16)
+            return carry
+
+        lax.fori_loop(0, rows // IJ_BLK, step, 0)
+        above += rows
+
+
+def code(mine, got, pieces):
     rows, width = mine.shape
     return pl.pallas_call(
-        code_kernel,
-        out_shape=[
-            jax.ShapeDtypeStruct((rows, width), jnp.float32),
-            jax.ShapeDtypeStruct((rows, width + LANES), jnp.int16),
-        ],
+        functools.partial(code_kernel, pieces),
+        out_shape=[jax.ShapeDtypeStruct((rows, width), jnp.float32)]
+        + [jax.ShapeDtypeStruct((p, width + LANES), jnp.int16) for p in pieces],
         in_specs=[vmem()] * 2,
-        out_specs=[vmem()] * 2,
-        compiler_params=pltpu.CompilerParams(vmem_limit_bytes=16 * 2**20),
+        out_specs=[vmem()] * (1 + len(pieces)),
+        compiler_params=pltpu.CompilerParams(vmem_limit_bytes=8 * 2**20),
         name="code",
     )(mine, got)
 
 
-def final_kernel(
-    nsum, npeer, blocks, n, ncol, src_ref, place_ref, occ_ref, vir_ref, *rest
-):
-    sums, codes, out = (
-        rest[:nsum],
-        [
-            rest[nsum + j * npeer : nsum + (j + 1) * npeer]
-            for j in range(nsum)
-        ],
-        rest[-1],
-    )
+def final_kernel(pieces, npeer, blocks, n, ncol, src_ref, place_ref, occ_ref, vir_ref, *rest):
+    out, rest = rest[-1], list(rest)
+    sums = [rest.pop(0) for _ in pieces]
+    codes = [[[rest.pop(0) for _ in range(npeer)] for _ in cut] for cut in pieces]
     width = vir_ref.shape[1]
     chip, half = place_ref[0], place_ref[1]
     rows_out = out.shape[1]
@@ -336,33 +332,39 @@
             owner = src * ncol // n
             row = lax.rem(src, n // ncol) * (rows_out * ncol // n) + block * IJ_BLK
             at = slice(b * IJ_BLK, (b + 1) * IJ_BLK)
+            piece, above = 0, 0
+            while b * IJ_BLK >= above + pieces[j][piece]:
+                above += pieces[j][piece]
+                piece += 1
+            sent = slice(b * IJ_BLK - above, (b + 1) * IJ_BLK - above)
 
             @pl.when(owner // 2 == chip)
             def _():
                 side = lax.rem(owner + half, 2)
                 to = pl.multiple_of(row, IJ_BLK)
                 total = sums[j][at, :]
-                for got in codes[j]:
-                    level = got[at, width:].astype(jnp.int32).astype(jnp.float32)
+                for got in codes[j][piece]:
+                    level = got[sent, width:].astype(jnp.int32).astype(jnp.float32)
                     down = jnp.exp(level[:, :1] * (LN2 / OCTAVE)) * (1.0 / TOP)
-                    coded = got[at, :width].astype(jnp.int32).astype(jnp.float32)
+                    coded = got[sent, :width].astype(jnp.int32).astype(jnp.float32)
                     total = total + coded * down
                 denom = vir - occ_ref[side, pl.ds(to, IJ_BLK), :]
                 out[side, pl.ds(to, IJ_BLK), :] = (total / denom).astype(out.dtype)
 
 
 def final(sums, codes, blocks, n, ncol, src, place, occ, vir, so_far):
-    npeer = len(codes[0])
-    flat = [c for batch in codes for c in batch]
+    npeer = len(codes[0][0])
+    pieces = [[part[0].shape[0] for part in batch] for batch in codes]
+    flat = [c for batch in codes for part in batch for c in part]
     width = vir.shape[1]
     more = [] if so_far is None else [so_far]
     return pl.pallas_call(
-        functools.partial(final_kernel, len(sums), npeer, blocks, n, ncol),
+        functools.partial(final_kernel, pieces, npeer, blocks, n, ncol),
         out_shape=jax.ShapeDtypeStruct((2, occ.shape[1], width), jnp.bfloat16),
         in_specs=[smem(), smem()] + [vmem()] * (2 + len(sums) + len(flat) + len(more)),
         out_specs=vmem(),
         input_output_aliases={4 + len(sums) + len(flat): 0} if more else {},
-        compiler_params=pltpu.CompilerParams(vmem_limit_bytes=32 * 2**20),
+        compiler_params=pltpu.CompilerParams(vmem_limit_bytes=8 * 2**20),
         name="final",
     )(src, place, occ, vir, *sums, *flat, *more)
 
@@ -394,23 +396,28 @@
     def tie(arrays, others):
         return lax.optimization_barrier((arrays, others))
 
-    def ladder_of(steps, coded):
+    def ladder_of(steps, sides):
         batch = [part for s in steps for part in parts[s]]
-        other, mine = ladder([c for c, _, _ in batch], tile_list, integrals)
+        outs = ladder([c for c, _, _ in batch], tile_list, integrals, sides)
+        return *outs, [(which, b + q) for _, which, b in batch for q in range(per)]
+
+    def code_of(got, mine, blocks):
+        total, *coded = code(mine, got, [mine.shape[0]])
+        sent = [
+            [
+                lax.ppermute(piece, "col", [(c, c ^ (2 * d)) for c in range(ncol)])
+                for d in range(1, ncol // 2)
+            ]
+            for piece in coded
+        ]
+        return total, sent, blocks
+
+    def after_codes(array, coded):
         if coded:
             total, peers, blocks = coded.pop()
-            other, peers = tie(other, peers)
+            array, peers = tie(array, peers)
             coded.append((total, peers, blocks))
-        blocks = [(which, b + q) for _, which, b in batch for q in range(per)]
-        return lax.ppermute(other, "col", core), mine, blocks
-
-    def code_of(got, mine, blocks):
-        total, coded = code(mine, got)
-        peers = [
-            lax.ppermute(coded, "col", [(c, c ^ (2 * d)) for c in range(ncol)])
-            for d in range(1, ncol // 2)
-        ]
-        return total, peers, blocks
+        return array
 
     def final_of(coded, so_far):
         sums, codes, blocks = zip(*coded, strict=True)
@@ -418,7 +425,7 @@
 
     parts = [[(flows[f], 0, f * per) for f in range(FLOWS)]]
     held = list(flows)
-    waiting, coded = None, []
+    coded = []
     for s in range(1, n):
         sent = [
             lax.ppermute(h, "row", ahead if f < FLOWS // 2 else behind)
@@ -427,12 +434,25 @@
         if s == 1:
             fixed = [tile_list, occ, vir, src, place]
             held, (tile_list, occ, vir, src, place) = tie(sent, fixed)
+        elif s == n - 2:
+            other, mine, blocks = ladder_of([s - 2, s - 1], (0, 1))
+            other = after_codes(other, coded)
+            held, (mine, other) = tie(sent, (mine, other))
+            got = lax.ppermute(other, "col", core)
+        elif s == n - 1:
+            coded.append(code_of(got, mine, blocks))
+            other, mine, blocks = ladder_of([s - 1], (0, 1))
+            other = after_codes(other, coded)
+            held, (mine, other) = tie(sent, (mine, other))
+            got = lax.ppermute(other, "col", core)
         elif s % 2 == 0:
-            waiting = ladder_of([s - 2, s - 1], coded)
-            held, mine = tie(sent, waiting[1])
-            waiting = (waiting[0], mine, waiting[2])
+            other, _ = ladder_of([s - 2, s - 1], (0,))
+            other = after_codes(other, coded)
+            held, other = tie(sent, other)
+            got = lax.ppermute(other, "col", core)
         else:
-            total, peers, blocks = code_of(*waiting)
+            mine, blocks = ladder_of([s - 3, s - 2], (1,))
+            total, peers, blocks = code_of(got, mine, blocks)
             held, total = tie(sent, total)
             coded.append((total, peers, blocks))
         parts.append(
@@ -441,7 +461,10 @@
                 for f, h in enumerate(held)
             ]
         )
-    last = code_of(*ladder_of([n - 2, n - 1], coded))
+    coded.append(code_of(got, mine, blocks))
+    other, mine, blocks = ladder_of([n - 1], (0, 1))
+    other = after_codes(other, coded)
+    last = code_of(lax.ppermute(other, "col", core), mine, blocks)
     done = final_of([last], final_of(coded, None))
     mine, theirs = done[0], done[1]
     got = lax.ppermute(theirs, "col", core)

time: 158 us -> 150 us (0.949)
  waiting for transfers between devices: 65 us -> 35.6 us
  Pallas kernels: 65.5 us -> 75.1 us
  starting transfers between devices: 17.3 us -> 24.1 us
  local copies, waits for them, and re-layouts: 7.85 us -> 11.5 us
    ppermute x14, waiting for transfers between devices: 46.5 us -> 26.1 us  [body(): lax.ppermute(h, 'row', ahead if f < FLOWS // 2 else behind)]
    pallas_call x4 -> x7, Pallas kernels: 50.5 us -> 62.4 us  [ladder(): pl.pallas_call(functools.partial(ladder_kernel, nchunk, per, rows_ab // T...]
    ppermute x8 -> x10, waiting for transfers between devices: 16.6 us -> 7.67 us  [the longest x4 4.56 us: body(): got = lax.ppermute(other, 'col', core)]
    ppermute x8 -> x10, starting transfers between devices: 1.42 us -> 8.8 us  [the longest x5 8.65 us: code_of(): lax.ppermute(piece, 'col', [(c, c ^ 2 * d) for c in range(ncol)])]
    unnamed x26 -> x34, local copies, waits for them, and re-layouts: 6.93 us -> 10.6 us
    pallas_call x1, Pallas kernels: 3.97 us -> 1.88 us  [pack(): pl.pallas_call(pack_kernel, out_shape=[jax.ShapeDtypeStruct((rows, LANES)...]
    pallas_call x6 -> x7, Pallas kernels: 8.4 us -> 8.29 us  [the longest x5 4.6 us: code(): pl.pallas_call(functools.partial(code_kernel, pieces), out_shape=[jax.Sha...]
  transfers between devices with their start and end apart: 24 -> 26, of which waited for: 15 -> 17; matrix products, arithmetic and copies ran while one was open for 1% -> 1% of each run, Pallas kernels for 37% -> 47%
where the time goes in v3:
time: 150 us; the launch traced here: 148 us
  Pallas kernels  75.1 us (50%)
  waiting for transfers between devices  35.6 us (24%)
  starting transfers between devices  24.1 us (16%)
  local copies, waits for them, and re-layouts  11.5 us (8%)
    pallas_call x7, Pallas kernels, ladder(): pl.pallas_call(functools.partial(ladder_kernel, nchunk, per, rows_ab // T...  62.4 us
    ppermute x14, waiting for transfers between devices, body(): lax.ppermute(h, 'row', ahead if f < FLOWS // 2 else behind)  26.1 us
    ppermute x14, starting transfers between devices, body(): lax.ppermute(h, 'row', ahead if f < FLOWS // 2 else behind)  15.2 us
    unnamed x34, local copies, waits for them, and re-layouts  10.6 us
    ppermute x5, starting transfers between devices, code_of(): lax.ppermute(piece, 'col', [(c, c ^ 2 * d) for c in range(ncol)])  8.65 us
    pallas_call x5, Pallas kernels, code(): pl.pallas_call(functools.partial(code_kernel, pieces), out_shape=[jax.Sha...  4.6 us
    ppermute x4, waiting for transfers between devices, body(): got = lax.ppermute(other, 'col', core)  4.56 us
    pallas_call x2, Pallas kernels, final(): pl.pallas_call(functools.partial(final_kernel, pieces, npeer, blocks, n,...  3.7 us
  transfers between devices with their start and end apart: 26, of which 17 were waited for; matrix products, arithmetic and copies ran while one was open for 1% of the time, Pallas kernels for 47%

profile of v3, /device:TPU:0, one launch (start us, length us, event | category | flops | bytes accessed | tf_op | source)
XLA Modules:
  0.0 148.2 jit_solution(6598760214079172223)
XLA Ops:
  0.0 1.6 %copy-done = bf16[128,8192]{1,0:T(8,128)(2,1)S(1)} copy-done((bf16[128,8192]{1,0:T(8,128)(2,1)S(1)}, bf16[128,8192]{1,0:T(8,128)(2,1)}, u32[]{:S(2)}) %copy-start) | copy-done | bytes 2097176
  2.3 1.9 %pack.1 = (bf16[2064,128]{1,0:T(8,128)(2,1)S(1)}, bf16[2064,128]{1,0:T(8,128)(2,1)S(1)}) custom-call(s32[4,32]{1,0:T(4,128)S(1)} %copy-done.14, bf16[128,8192]{1,0:T(8,128)(2,1)S(1)} %copy-done), custom_call_target="tpu_custom_call" | custom-call | tf_op jit(solution)/shard_map/pack/pallas_call | solution.py:85
  4.2 3.1 %collective-permute-start = (bf16[2064,128]{1,0:T(8,128)(2,1)S(1)}, bf16[2064,128]{1,0:T(8,128)(2,1)S(1)}, u32[]{:S(2)}, u32[]{:S(2)}) collective-permute-start(bf16[2064,128]{1,0:T(8,128)(2,1)S(1)} %get-tuple-element.58.rest_0_), channel_id=1, source_target_pairs={{0,8},{8,16},{16,24},{24,28},{28,20},{20,12},{12,4},{4,0},{1,9},{9... | collective-permute-start | bytes 1585160 | tf_op jit(solution)/shard_map/ppermute | solution.py:431
  8.0 2.6 %tile_list.1.list_ref = s32[371]{0:T(512)} custom-call(s32[1]{0:T(128)} %bitcast.half_ref, s32[8,32]{1,0:T(8,128)} %mask_ref.3), custom_call_target="tpu_custom_call" | custom-call | tf_op jit(solution)/shard_map/tile_list/pallas_call | solution.py:146
  10.7 8.5 %collective-permute-done.rest_2_ = bf16[2064,128]{1,0:T(8,128)(2,1)S(1)} collective-permute-done((bf16[2064,128]{1,0:T(8,128)(2,1)S(1)}, bf16[2064,128]{1,0:T(8,128)(2,1)S(1)}, u32[]{:S(2)}, u32[]{:S(2)}) %collective-permute-start) | collective-permute-done | bytes 528416 | tf_op jit(solution)/shard_map/ppermute | solution.py:431
  19.2 1.5 %collective-permute-done.1.rest_3_ = bf16[2064,128]{1,0:T(8,128)(2,1)S(1)} collective-permute-done((bf16[2064,128]{1,0:T(8,128)(2,1)S(1)}, bf16[2064,128]{1,0:T(8,128)(2,1)S(1)}, u32[]{:S(2)}, u32[]{:S(2)}) %collective-permute-start.1) | collective-permute-done | bytes 528416 | tf_op jit(solution)/shard_map/ppermute | solution.py:431
  20.7 1.6 %collective-permute-start.3 = (bf16[2064,128]{1,0:T(8,128)(2,1)S(1)}, bf16[2064,128]{1,0:T(8,128)(2,1)S(1)}, u32[]{:S(2)}, u32[]{:S(2)}) collective-permute-start(bf16[2064,128]{1,0:T(8,128)(2,1)S(1)} %collective-permute-done.rest_2_), channel_id=1, source_target_pairs={{0,8},{8,16},{16,24},{24,28},{28,20},{20,12},{12,4},{4,0},{1,9},{9... | collective-permute-start | bytes 1585160 | tf_op jit(solution)/shard_map/ppermute | solution.py:431
  23.4 7.7 %ladder.7 = f32[256,1024]{1,0:T(8,128)S(1)} custom-call(s32[371]{0:T(512)S(1)} %copy-done.13, bf16[2048,8192]{1,0:T(8,128)(2,1)} %int_ref.13, bf16[2064,128]{1,0:T(8,128)(2,1)S(1)} %get-tuple-element.58.rest_0_, bf16[2064,128]{1,0:T(8,128)(2,1)S(1)} %get-tuple-element.59.rest_1_, bf16[2064,128]{1,0:T(8,128)(2,1)S(1)} %collective-permute-done.rest_2_, ...), custom_call_target="tpu_custom_call" | custom-call | flops 4294967296 | bytes 8388608 | tf_op jit(solution)/shard_map/ladder/pallas_call | solution.py:259
  31.1 2.2 %collective-permute-done.3.rest_0_ = bf16[2064,128]{1,0:T(8,128)(2,1)S(1)} collective-permute-done((bf16[2064,128]{1,0:T(8,128)(2,1)S(1)}, bf16[2064,128]{1,0:T(8,128)(2,1)S(1)}, u32[]{:S(2)}, u32[]{:S(2)}) %collective-permute-start.3) | collective-permute-done | bytes 528416 | tf_op jit(solution)/shard_map/ppermute | solution.py:431
  33.3 1.3 collective-permute-done.4.rest_1_
  34.6 1.6 %collective-permute-start.5 = (bf16[2064,128]{1,0:T(8,128)(2,1)S(1)}, bf16[2064,128]{1,0:T(8,128)(2,1)S(1)}, u32[]{:S(2)}, u32[]{:S(2)}) collective-permute-start(bf16[2064,128]{1,0:T(8,128)(2,1)S(1)} %collective-permute-done.3.rest_0_), channel_id=1, source_target_pairs={{0,8},{8,16},{16,24},{24,28},{28,20},{20,12},{12,4},{4,0},{1,9},{9... | collective-permute-start | bytes 1585160 | tf_op jit(solution)/shard_map/ppermute | solution.py:431
  36.6 6.7 %ladder.8.mine_ref = f32[256,1024]{1,0:T(8,128)S(1)} custom-call(s32[371]{0:T(512)S(1)} %copy-done.13, bf16[2048,8192]{1,0:T(8,128)(2,1)} %int_ref.13, bf16[2064,128]{1,0:T(8,128)(2,1)S(1)} %get-tuple-element.58.rest_0_, bf16[2064,128]{1,0:T(8,128)(2,1)S(1)} %get-tuple-element.59.rest_1_, bf16[2064,128]{1,0:T(8,128)(2,1)S(1)} %collective-permute-done.rest_2_, ...), custom_call_target="tpu_custom_call" | custom-call | flops 4294967296 | bytes 8388608 | tf_op jit(solution)/shard_map/ladder/pallas_call | solution.py:259
  43.3 1.0 code.5
  44.3 2.5 %collective-permute-start.10 = (s16[256,1152]{1,0:T(8,128)(2,1)S(1)}, s16[256,1152]{1,0:T(8,128)(2,1)S(1)}, u32[]{:S(2)}, u32[]{:S(2)}) collective-permute-start(s16[256,1152]{1,0:T(8,128)(2,1)S(1)} %get-tuple-element.73), channel_id=1, source_target_pairs={{0,2},{1,3},{2,0},{3,1},{4,6},{5,7},{6,4},{7,5},{8,10},{9,11},{10,... | collective-permute-start | bytes 1769480 | tf_op jit(solution)/shard_map/ppermute | solution.py:408
  46.8 2.2 %collective-permute-done.5.rest_2_ = bf16[2064,128]{1,0:T(8,128)(2,1)S(1)} collective-permute-done((bf16[2064,128]{1,0:T(8,128)(2,1)S(1)}, bf16[2064,128]{1,0:T(8,128)(2,1)S(1)}, u32[]{:S(2)}, u32[]{:S(2)}) %collective-permute-start.5) | collective-permute-done | bytes 528416 | tf_op jit(solution)/shard_map/ppermute | solution.py:431
  49.0 1.3 collective-permute-done.6.rest_3_
  50.3 1.5 %collective-permute-start.8 = (bf16[2064,128]{1,0:T(8,128)(2,1)S(1)}, bf16[2064,128]{1,0:T(8,128)(2,1)S(1)}, u32[]{:S(2)}, u32[]{:S(2)}) collective-permute-start(bf16[2064,128]{1,0:T(8,128)(2,1)S(1)} %collective-permute-done.5.rest_2_), channel_id=1, source_target_pairs={{0,8},{8,16},{16,24},{24,28},{28,20},{20,12},{12,4},{4,0},{1,9},{9... | collective-permute-start | bytes 1585160 | tf_op jit(solution)/shard_map/ppermute | solution.py:431
  52.3 7.7 %ladder.9 = f32[256,1024]{1,0:T(8,128)S(1)} custom-call(s32[371]{0:T(512)S(1)} %copy-done.13, bf16[2048,8192]{1,0:T(8,128)(2,1)} %int_ref.13, bf16[2064,128]{1,0:T(8,128)(2,1)S(1)} %collective-permute-done.3.rest_0_, bf16[2064,128]{1,0:T(8,128)(2,1)S(1)} %collective-permute-done.4.rest_1_, bf16[2064,128]{1,0:T(8,128)(2,1)S(1)} %collective-permute-done.5.rest_2_, ...), custom_call_target="tpu_custom_call" | custom-call | flops 4294967296 | bytes 8388608 | tf_op jit(solution)/shard_map/ladder/pallas_call | solution.py:259
  60.8 2.8 %collective-permute-done.8.rest_0_ = bf16[2064,128]{1,0:T(8,128)(2,1)S(1)} collective-permute-done((bf16[2064,128]{1,0:T(8,128)(2,1)S(1)}, bf16[2064,128]{1,0:T(8,128)(2,1)S(1)}, u32[]{:S(2)}, u32[]{:S(2)}) %collective-permute-start.8) | collective-permute-done | bytes 528416 | tf_op jit(solution)/shard_map/ppermute | solution.py:431
  63.6 1.2 collective-permute-done.9.rest_1_
  65.5 1.4 collective-permute-start.12
  66.9 6.9 %ladder.10.mine_ref = f32[256,1024]{1,0:T(8,128)S(1)} custom-call(s32[371]{0:T(512)S(1)} %copy-done.13, bf16[2048,8192]{1,0:T(8,128)(2,1)} %int_ref.13, bf16[2064,128]{1,0:T(8,128)(2,1)S(1)} %collective-permute-done.3.rest_0_, bf16[2064,128]{1,0:T(8,128)(2,1)S(1)} %collective-permute-done.4.rest_1_, bf16[2064,128]{1,0:T(8,128)(2,1)S(1)} %collective-permute-done.5.rest_2_, ...), custom_call_target="tpu_custom_call" | custom-call | flops 4294967296 | bytes 8388608 | tf_op jit(solution)/shard_map/ladder/pallas_call | solution.py:259
  73.8 1.0 code.6
  74.8 4.5 %collective-permute-done.11.rest_2_ = bf16[2064,128]{1,0:T(8,128)(2,1)S(1)} collective-permute-done((bf16[2064,128]{1,0:T(8,128)(2,1)S(1)}, bf16[2064,128]{1,0:T(8,128)(2,1)S(1)}, u32[]{:S(2)}, u32[]{:S(2)}) %collective-permute-start.11) | collective-permute-done | bytes 528416 | tf_op jit(solution)/shard_map/ppermute | solution.py:431
  79.6 1.5 %collective-permute-start.16 = (s16[256,1152]{1,0:T(8,128)(2,1)S(1)}, s16[256,1152]{1,0:T(8,128)(2,1)S(1)}, u32[]{:S(2)}, u32[]{:S(2)}) collective-permute-start(s16[256,1152]{1,0:T(8,128)(2,1)S(1)} %get-tuple-element.83), channel_id=1, source_target_pairs={{0,2},{1,3},{2,0},{3,1},{4,6},{5,7},{6,4},{7,5},{8,10},{9,11},{10,... | collective-permute-start | bytes 1769480 | tf_op jit(solution)/shard_map/ppermute | solution.py:408
  81.7 1.4 collective-permute-start.15
  83.1 11.6 %ladder.11 = (f32[256,1024]{1,0:T(8,128)S(1)}, f32[256,1024]{1,0:T(8,128)S(1)}) custom-call(s32[371]{0:T(512)S(1)} %copy-done.13, bf16[2048,8192]{1,0:T(8,128)(2,1)} %int_ref.13, bf16[2064,128]{1,0:T(8,128)(2,1)S(1)} %collective-permute-done.8.rest_0_, bf16[2064,128]{1,0:T(8,128)(2,1)S(1)} %collective-permute-done.9.rest_1_, ...), custom_call_target="tpu_custom_call" | custom-call | flops 8589934592 | bytes 16777216 | tf_op jit(solution)/shard_map/ladder/pallas_call | solution.py:259
  94.9 2.6 %collective-permute-done.19.got_ref = f32[256,1024]{1,0:T(8,128)S(1)} collective-permute-done((f32[256,1024]{1,0:T(8,128)S(1)}, f32[256,1024]{1,0:T(8,128)S(1)}, u32[]{:S(2)}, u32[]{:S(2)}) %collective-permute-start.19) | collective-permute-done | bytes 1048608 | tf_op jit(solution)/shard_map/ppermute | solution.py:441
  97.5 0.9 code.7
  98.5 1.6 %collective-permute-start.20 = (s16[256,1152]{1,0:T(8,128)(2,1)S(1)}, s16[256,1152]{1,0:T(8,128)(2,1)S(1)}, u32[]{:S(2)}, u32[]{:S(2)}) collective-permute-start(s16[256,1152]{1,0:T(8,128)(2,1)S(1)} %get-tuple-element.91), channel_id=1, source_target_pairs={{0,2},{1,3},{2,0},{3,1},{4,6},{5,7},{6,4},{7,5},{8,10},{9,11},{10,... | collective-permute-start | bytes 1769480 | tf_op jit(solution)/shard_map/ppermute | solution.py:408
  100.7 1.4 collective-permute-start.18
  102.1 10.8 %ladder.12 = (f32[128,1024]{1,0:T(8,128)S(1)}, f32[128,1024]{1,0:T(8,128)S(1)}) custom-call(s32[371]{0:T(512)S(1)} %copy-done.13, bf16[2048,8192]{1,0:T(8,128)(2,1)} %int_ref.13, bf16[2064,128]{1,0:T(8,128)(2,1)S(1)} %collective-permute-done.14.rest_0_, bf16[2064,128]{1,0:T(8,128)(2,1)S(1)} %collective-permute-done.15.rest_1_), custom_call_target="tpu_custom_call" | custom-call | flops 4294967296 | bytes 16777216 | tf_op jit(solution)/shard_map/ladder/pallas_call | solution.py:259
  112.9 1.0 collective-permute-done.20.rest_6_
  114.2 1.9 %collective-permute-done.21.got_ref = f32[128,1024]{1,0:T(8,128)S(1)} collective-permute-done((f32[128,1024]{1,0:T(8,128)S(1)}, f32[128,1024]{1,0:T(8,128)S(1)}, u32[]{:S(2)}, u32[]{:S(2)}) %collective-permute-start.21) | collective-permute-done | bytes 524320 | tf_op jit(solution)/shard_map/ppermute | solution.py:447
  117.4 1.5 %collective-permute-start.22 = (s16[128,1152]{1,0:T(8,128)(2,1)S(1)}, s16[128,1152]{1,0:T(8,128)(2,1)S(1)}, u32[]{:S(2)}, u32[]{:S(2)}) collective-permute-start(s16[128,1152]{1,0:T(8,128)(2,1)S(1)} %get-tuple-element.99), channel_id=1, source_target_pairs={{0,2},{1,3},{2,0},{3,1},{4,6},{5,7},{6,4},{7,5},{8,10},{9,11},{10,... | collective-permute-start | bytes 884744 | tf_op jit(solution)/shard_map/ppermute | solution.py:408
  118.9 11.0 %ladder.13 = (f32[128,1024]{1,0:T(8,128)S(1)}, f32[128,1024]{1,0:T(8,128)S(1)}) custom-call(s32[371]{0:T(512)S(1)} %copy-done.13, bf16[2048,8192]{1,0:T(8,128)(2,1)} %int_ref.13, bf16[2064,128]{1,0:T(8,128)(2,1)S(1)} %collective-permute-done.17.rest_0_, bf16[2064,128]{1,0:T(8,128)(2,1)S(1)} %collective-permute-done.18.rest_1_), custom_call_target="tpu_custom_call" | custom-call | flops 4294967296 | bytes 16777216 | tf_op jit(solution)/shard_map/ladder/pallas_call | solution.py:259
  130.0 1.9 %collective-permute-done.23.got_ref = f32[128,1024]{1,0:T(8,128)S(1)} collective-permute-done((f32[128,1024]{1,0:T(8,128)S(1)}, f32[128,1024]{1,0:T(8,128)S(1)}, u32[]{:S(2)}, u32[]{:S(2)}) %collective-permute-start.23) | collective-permute-done | bytes 524320 | tf_op jit(solution)/shard_map/ppermute | solution.py:467
  131.9 1.2 code.9
  134.0 1.5 %collective-permute-start.24 = (s16[128,1152]{1,0:T(8,128)(2,1)}, s16[128,1152]{1,0:T(8,128)(2,1)}, u32[]{:S(2)}, u32[]{:S(2)}) collective-permute-start(s16[128,1152]{1,0:T(8,128)(2,1)} %get-tuple-element.102), channel_id=1, source_target_pairs={{0,2},{1,3},{2,0},{3,1},{4,6},{5,7},{6,4},{7,5},{8,10},{9,11},{10,... | collective-permute-start | bytes 884744 | tf_op jit(solution)/shard_map/ppermute | solution.py:408
  135.6 1.1 copy-done.2
  136.7 1.1 copy-done.4
  137.7 1.1 copy-done.6
  138.8 1.0 copy-done.8
  139.8 1.0 copy-done.12
  140.8 2.3 %final.2.rest_2_ = bf16[2,256,1024]{2,1,0:T(8,128)(2,1)S(1)} custom-call(s32[15]{0:T(128)S(1)} %dynamic-slice_bitcast_fusion.src_ref, s32[2]{0:T(128)S(1)} %pad_add_fusion.place_ref, f32[2,256,1]{2,1,0:T(8,128)S(1)} %copy.10.occ_ref, f32[1,1024]{1,0:T(1,128)S(1)} %bitcast.13, f32[256,1024]{1,0:T(8,128)S(1)} %get-tuple-element.103.rest_0_, ...), custom_call_target="tpu_custom_call" | custom-call | tf_op jit(solution)/shard_map/final/pallas_call | solution.py:361
  143.3 1.4 final.3
  144.9 1.9 %collective-permute-done.25 = bf16[256,1024]{1,0:T(8,128)(2,1)S(1)} collective-permute-done((bf16[256,1024]{1,0:T(8,128)(2,1)S(1)}, bf16[256,1024]{1,0:T(8,128)(2,1)S(1)}, u32[]{:S(2)}, u32[]{:S(2)}) %collective-permute-start.25) | collective-permute-done | bytes 524320 | tf_op jit(solution)/shard_map/ppermute | solution.py:470
  146.8 1.4 maximum_select_fusion
  (61 shorter events, 9.5 us)
Async XLA Ops:
  0.0 1.6 %copy-start = (bf16[128,8192]{1,0:T(8,128)(2,1)S(1)}, bf16[128,8192]{1,0:T(8,128)(2,1)}, u32[]{:S(2)}) copy-start(bf16[128,8192]{1,0:T(8,128)(2,1)} %amp_ref.1) | copy-start | bytes 6291460
  1.6 0.7 copy-start.14
  2.3 5.0 %copy-start.16 = (f32[256]{0:T(256)S(1)}, f32[256]{0:T(256)}, u32[]{:S(2)}) copy-start(f32[256]{0:T(256)} %param.11) | copy-start | bytes 3076
  2.3 8.4 %copy-start.15 = (f32[2048]{0:T(1024)S(1)}, f32[2048]{0:T(1024)}, u32[]{:S(2)}) copy-start(f32[2048]{0:T(1024)} %param.12) | copy-start | bytes 24580
  4.2 15.0 %collective-permute-start = (bf16[2064,128]{1,0:T(8,128)(2,1)S(1)}, bf16[2064,128]{1,0:T(8,128)(2,1)S(1)}, u32[]{:S(2)}, u32[]{:S(2)}) collective-permute-start(bf16[2064,128]{1,0:T(8,128)(2,1)S(1)} %get-tuple-element.58.rest_0_), channel_id=1, source_target_pairs={{0,8},{8,16},{16,24},{24,28},{28,20},{20,12},{12,4},{4,0},{1,9},{9... | collective-permute-start | bytes 1585160 | tf_op jit(solution)/shard_map/ppermute | solution.py:431
  7.2 13.5 %collective-permute-start.1 = (bf16[2064,128]{1,0:T(8,128)(2,1)S(1)}, bf16[2064,128]{1,0:T(8,128)(2,1)S(1)}, u32[]{:S(2)}, u32[]{:S(2)}) collective-permute-start(bf16[2064,128]{1,0:T(8,128)(2,1)S(1)} %get-tuple-element.59.rest_1_), channel_id=1, source_target_pairs={{8,0},{16,8},{24,16},{28,24},{20,28},{12,20},{4,12},{0,4},{9,1},{1... | collective-permute-start | bytes 1585160 | tf_op jit(solution)/shard_map/ppermute | solution.py:431
  7.3 3.4 %collective-permute-start.2 = (f32[256]{0:T(256)S(1)}, f32[256]{0:T(256)S(1)}, u32[]{:S(2)}, u32[]{:S(2)}) collective-permute-start(f32[256]{0:T(256)S(1)} %copy-done.16), channel_id=1, source_target_pairs={{0,1},{1,0},{2,3},{3,2},{4,5},{5,4},{6,7},{7,6},{8,9},{9,8},{10,11... | collective-permute-start | bytes 3080 | tf_op jit(solution)/shard_map/ppermute | solution.py:392
  20.7 12.6 %collective-permute-start.3 = (bf16[2064,128]{1,0:T(8,128)(2,1)S(1)}, bf16[2064,128]{1,0:T(8,128)(2,1)S(1)}, u32[]{:S(2)}, u32[]{:S(2)}) collective-permute-start(bf16[2064,128]{1,0:T(8,128)(2,1)S(1)} %collective-permute-done.rest_2_), channel_id=1, source_target_pairs={{0,8},{8,16},{16,24},{24,28},{28,20},{20,12},{12,4},{4,0},{1,9},{9... | collective-permute-start | bytes 1585160 | tf_op jit(solution)/shard_map/ppermute | solution.py:431
  22.3 12.3 %collective-permute-start.4 = (bf16[2064,128]{1,0:T(8,128)(2,1)S(1)}, bf16[2064,128]{1,0:T(8,128)(2,1)S(1)}, u32[]{:S(2)}, u32[]{:S(2)}) collective-permute-start(bf16[2064,128]{1,0:T(8,128)(2,1)S(1)} %collective-permute-done.1.rest_3_), channel_id=1, source_target_pairs={{8,0},{16,8},{24,16},{28,24},{20,28},{12,20},{4,12},{0,4},{9,1},{1... | collective-permute-start | bytes 1585160 | tf_op jit(solution)/shard_map/ppermute | solution.py:431
  22.7 0.7 copy-start.13
  34.6 8.7 %collective-permute-start.7 = (f32[256,1024]{1,0:T(8,128)S(1)}, f32[256,1024]{1,0:T(8,128)S(1)}, u32[]{:S(2)}, u32[]{:S(2)}) collective-permute-start(f32[256,1024]{1,0:T(8,128)S(1)} %ladder.7), channel_id=1, source_target_pairs={{0,1},{1,0},{2,3},{3,2},{4,5},{5,4},{6,7},{7,6},{8,9},{9,8},{10,11... | collective-permute-start | bytes 3145736 | tf_op jit(solution)/shard_map/ppermute | solution.py:452
  34.6 14.4 %collective-permute-start.5 = (bf16[2064,128]{1,0:T(8,128)(2,1)S(1)}, bf16[2064,128]{1,0:T(8,128)(2,1)S(1)}, u32[]{:S(2)}, u32[]{:S(2)}) collective-permute-start(bf16[2064,128]{1,0:T(8,128)(2,1)S(1)} %collective-permute-done.3.rest_0_), channel_id=1, source_target_pairs={{0,8},{8,16},{16,24},{24,28},{28,20},{20,12},{12,4},{4,0},{1,9},{9... | collective-permute-start | bytes 1585160 | tf_op jit(solution)/shard_map/ppermute | solution.py:431
  36.2 14.1 %collective-permute-start.6 = (bf16[2064,128]{1,0:T(8,128)(2,1)S(1)}, bf16[2064,128]{1,0:T(8,128)(2,1)S(1)}, u32[]{:S(2)}, u32[]{:S(2)}) collective-permute-start(bf16[2064,128]{1,0:T(8,128)(2,1)S(1)} %collective-permute-done.4.rest_1_), channel_id=1, source_target_pairs={{8,0},{16,8},{24,16},{28,24},{20,28},{12,20},{4,12},{0,4},{9,1},{1... | collective-permute-start | bytes 1585160 | tf_op jit(solution)/shard_map/ppermute | solution.py:431
  44.3 15.7 %collective-permute-start.10 = (s16[256,1152]{1,0:T(8,128)(2,1)S(1)}, s16[256,1152]{1,0:T(8,128)(2,1)S(1)}, u32[]{:S(2)}, u32[]{:S(2)}) collective-permute-start(s16[256,1152]{1,0:T(8,128)(2,1)S(1)} %get-tuple-element.73), channel_id=1, source_target_pairs={{0,2},{1,3},{2,0},{3,1},{4,6},{5,7},{6,4},{7,5},{8,10},{9,11},{10,... | collective-permute-start | bytes 1769480 | tf_op jit(solution)/shard_map/ppermute | solution.py:408
  50.3 13.3 %collective-permute-start.8 = (bf16[2064,128]{1,0:T(8,128)(2,1)S(1)}, bf16[2064,128]{1,0:T(8,128)(2,1)S(1)}, u32[]{:S(2)}, u32[]{:S(2)}) collective-permute-start(bf16[2064,128]{1,0:T(8,128)(2,1)S(1)} %collective-permute-done.5.rest_2_), channel_id=1, source_target_pairs={{0,8},{8,16},{16,24},{24,28},{28,20},{20,12},{12,4},{4,0},{1,9},{9... | collective-permute-start | bytes 1585160 | tf_op jit(solution)/shard_map/ppermute | solution.py:431
  51.8 13.0 %collective-permute-start.9 = (bf16[2064,128]{1,0:T(8,128)(2,1)S(1)}, bf16[2064,128]{1,0:T(8,128)(2,1)S(1)}, u32[]{:S(2)}, u32[]{:S(2)}) collective-permute-start(bf16[2064,128]{1,0:T(8,128)(2,1)S(1)} %collective-permute-done.6.rest_3_), channel_id=1, source_target_pairs={{8,0},{16,8},{24,16},{28,24},{20,28},{12,20},{4,12},{0,4},{9,1},{1... | collective-permute-start | bytes 1585160 | tf_op jit(solution)/shard_map/ppermute | solution.py:431
  60.0 0.8 copy-start.1
  64.9 8.9 %collective-permute-start.13 = (f32[256,1024]{1,0:T(8,128)S(1)}, f32[256,1024]{1,0:T(8,128)S(1)}, u32[]{:S(2)}, u32[]{:S(2)}) collective-permute-start(f32[256,1024]{1,0:T(8,128)S(1)} %ladder.9), channel_id=1, source_target_pairs={{0,1},{1,0},{2,3},{3,2},{4,5},{5,4},{6,7},{7,6},{8,9},{9,8},{10,11... | collective-permute-start | bytes 3145736 | tf_op jit(solution)/shard_map/ppermute | solution.py:452
  64.9 14.4 %collective-permute-start.11 = (bf16[2064,128]{1,0:T(8,128)(2,1)S(1)}, bf16[2064,128]{1,0:T(8,128)(2,1)S(1)}, u32[]{:S(2)}, u32[]{:S(2)}) collective-permute-start(bf16[2064,128]{1,0:T(8,128)(2,1)S(1)} %collective-permute-done.8.rest_0_), channel_id=1, source_target_pairs={{0,8},{8,16},{16,24},{24,28},{28,20},{20,12},{12,4},{4,0},{1,9},{9... | collective-permute-start | bytes 1585160 | tf_op jit(solution)/shard_map/ppermute | solution.py:431
  65.5 14.1 %collective-permute-start.12 = (bf16[2064,128]{1,0:T(8,128)(2,1)S(1)}, bf16[2064,128]{1,0:T(8,128)(2,1)S(1)}, u32[]{:S(2)}, u32[]{:S(2)}) collective-permute-start(bf16[2064,128]{1,0:T(8,128)(2,1)S(1)} %collective-permute-done.9.rest_1_), channel_id=1, source_target_pairs={{8,0},{16,8},{24,16},{28,24},{20,28},{12,20},{4,12},{0,4},{9,1},{1... | collective-permute-start | bytes 1585160 | tf_op jit(solution)/shard_map/ppermute | solution.py:431
  79.6 15.1 %collective-permute-start.16 = (s16[256,1152]{1,0:T(8,128)(2,1)S(1)}, s16[256,1152]{1,0:T(8,128)(2,1)S(1)}, u32[]{:S(2)}, u32[]{:S(2)}) collective-permute-start(s16[256,1152]{1,0:T(8,128)(2,1)S(1)} %get-tuple-element.83), channel_id=1, source_target_pairs={{0,2},{1,3},{2,0},{3,1},{4,6},{5,7},{6,4},{7,5},{8,10},{9,11},{10,... | collective-permute-start | bytes 1769480 | tf_op jit(solution)/shard_map/ppermute | solution.py:408
  81.1 13.7 %collective-permute-start.14 = (bf16[2064,128]{1,0:T(8,128)(2,1)S(1)}, bf16[2064,128]{1,0:T(8,128)(2,1)S(1)}, u32[]{:S(2)}, u32[]{:S(2)}) collective-permute-start(bf16[2064,128]{1,0:T(8,128)(2,1)S(1)} %collective-permute-done.11.rest_2_), channel_id=1, source_target_pairs={{0,8},{8,16},{16,24},{24,28},{28,20},{20,12},{12,4},{4,0},{1,9},{9... | collective-permute-start | bytes 1585160 | tf_op jit(solution)/shard_map/ppermute | solution.py:431
  81.7 13.1 %collective-permute-start.15 = (bf16[2064,128]{1,0:T(8,128)(2,1)S(1)}, bf16[2064,128]{1,0:T(8,128)(2,1)S(1)}, u32[]{:S(2)}, u32[]{:S(2)}) collective-permute-start(bf16[2064,128]{1,0:T(8,128)(2,1)S(1)} %collective-permute-done.12.rest_3_), channel_id=1, source_target_pairs={{8,0},{16,8},{24,16},{28,24},{20,28},{12,20},{4,12},{0,4},{9,1},{1... | collective-permute-start | bytes 1585160 | tf_op jit(solution)/shard_map/ppermute | solution.py:431
  94.8 18.2 %copy-start.3 = (s16[256,1152]{1,0:T(8,128)(2,1)}, s16[256,1152]{1,0:T(8,128)(2,1)S(1)}, u32[]{:S(2)}) copy-start(s16[256,1152]{1,0:T(8,128)(2,1)S(1)} %collective-permute-done.16.rest_5_) | copy-start | bytes 1769476
  94.8 2.7 %collective-permute-start.19 = (f32[256,1024]{1,0:T(8,128)S(1)}, f32[256,1024]{1,0:T(8,128)S(1)}, u32[]{:S(2)}, u32[]{:S(2)}) collective-permute-start(f32[256,1024]{1,0:T(8,128)S(1)} %get-tuple-element.90), channel_id=1, source_target_pairs={{0,1},{1,0},{2,3},{3,2},{4,5},{5,4},{6,7},{7,6},{8,9},{9,8},{10,11... | collective-permute-start | bytes 3145736 | tf_op jit(solution)/shard_map/ppermute | solution.py:441
  98.5 15.4 %collective-permute-start.20 = (s16[256,1152]{1,0:T(8,128)(2,1)S(1)}, s16[256,1152]{1,0:T(8,128)(2,1)S(1)}, u32[]{:S(2)}, u32[]{:S(2)}) collective-permute-start(s16[256,1152]{1,0:T(8,128)(2,1)S(1)} %get-tuple-element.91), channel_id=1, source_target_pairs={{0,2},{1,3},{2,0},{3,1},{4,6},{5,7},{6,4},{7,5},{8,10},{9,11},{10,... | collective-permute-start | bytes 1769480 | tf_op jit(solution)/shard_map/ppermute | solution.py:408
  100.1 13.8 %collective-permute-start.17 = (bf16[2064,128]{1,0:T(8,128)(2,1)S(1)}, bf16[2064,128]{1,0:T(8,128)(2,1)S(1)}, u32[]{:S(2)}, u32[]{:S(2)}) collective-permute-start(bf16[2064,128]{1,0:T(8,128)(2,1)S(1)} %collective-permute-done.14.rest_0_), channel_id=1, source_target_pairs={{0,8},{8,16},{16,24},{24,28},{28,20},{20,12},{12,4},{4,0},{1,9},{9... | collective-permute-start | bytes 1585160 | tf_op jit(solution)/shard_map/ppermute | solution.py:431
  100.7 13.5 %collective-permute-start.18 = (bf16[2064,128]{1,0:T(8,128)(2,1)S(1)}, bf16[2064,128]{1,0:T(8,128)(2,1)S(1)}, u32[]{:S(2)}, u32[]{:S(2)}) collective-permute-start(bf16[2064,128]{1,0:T(8,128)(2,1)S(1)} %collective-permute-done.15.rest_1_), channel_id=1, source_target_pairs={{8,0},{16,8},{24,16},{28,24},{20,28},{12,20},{4,12},{0,4},{9,1},{1... | collective-permute-start | bytes 1585160 | tf_op jit(solution)/shard_map/ppermute | solution.py:431
  113.9 16.0 %copy-start.5 = (s16[256,1152]{1,0:T(8,128)(2,1)}, s16[256,1152]{1,0:T(8,128)(2,1)S(1)}, u32[]{:S(2)}) copy-start(s16[256,1152]{1,0:T(8,128)(2,1)S(1)} %collective-permute-done.20.rest_6_) | copy-start | bytes 1769476
  114.2 1.9 %collective-permute-start.21 = (f32[128,1024]{1,0:T(8,128)S(1)}, f32[128,1024]{1,0:T(8,128)S(1)}, u32[]{:S(2)}, u32[]{:S(2)}) collective-permute-start(f32[128,1024]{1,0:T(8,128)S(1)} %get-tuple-element.98), channel_id=1, source_target_pairs={{0,1},{1,0},{2,3},{3,2},{4,5},{5,4},{6,7},{7,6},{8,9},{9,8},{10,11... | collective-permute-start | bytes 1572872 | tf_op jit(solution)/shard_map/ppermute | solution.py:447
  116.6 0.8 copy-start.7
  117.4 12.6 %collective-permute-start.22 = (s16[128,1152]{1,0:T(8,128)(2,1)S(1)}, s16[128,1152]{1,0:T(8,128)(2,1)S(1)}, u32[]{:S(2)}, u32[]{:S(2)}) collective-permute-start(s16[128,1152]{1,0:T(8,128)(2,1)S(1)} %get-tuple-element.99), channel_id=1, source_target_pairs={{0,2},{1,3},{2,0},{3,1},{4,6},{5,7},{6,4},{7,5},{8,10},{9,11},{10,... | collective-permute-start | bytes 884744 | tf_op jit(solution)/shard_map/ppermute | solution.py:408
  130.0 4.0 %copy-start.11 = (s16[128,1152]{1,0:T(8,128)(2,1)}, s16[128,1152]{1,0:T(8,128)(2,1)S(1)}, u32[]{:S(2)}) copy-start(s16[128,1152]{1,0:T(8,128)(2,1)S(1)} %collective-permute-done.22.rest_7_) | copy-start | bytes 884740
  130.0 2.0 %collective-permute-start.23 = (f32[128,1024]{1,0:T(8,128)S(1)}, f32[128,1024]{1,0:T(8,128)S(1)}, u32[]{:S(2)}, u32[]{:S(2)}) collective-permute-start(f32[128,1024]{1,0:T(8,128)S(1)} %get-tuple-element.100), channel_id=1, source_target_pairs={{0,1},{1,0},{2,3},{3,2},{4,5},{5,4},{6,7},{7,6},{8,9},{9,8},{10,11... | collective-permute-start | bytes 1572872 | tf_op jit(solution)/shard_map/ppermute | solution.py:467
  133.2 0.8 copy-start.9
  134.0 9.4 %collective-permute-start.24 = (s16[128,1152]{1,0:T(8,128)(2,1)}, s16[128,1152]{1,0:T(8,128)(2,1)}, u32[]{:S(2)}, u32[]{:S(2)}) collective-permute-start(s16[128,1152]{1,0:T(8,128)(2,1)} %get-tuple-element.102), channel_id=1, source_target_pairs={{0,2},{1,3},{2,0},{3,1},{4,6},{5,7},{6,4},{7,5},{8,10},{9,11},{10,... | collective-permute-start | bytes 884744 | tf_op jit(solution)/shard_map/ppermute | solution.py:408
  135.6 1.1 copy-start.2
  136.7 1.1 copy-start.4
  137.7 1.1 copy-start.6
  138.8 1.0 copy-start.8
  139.8 1.0 copy-start.12
  140.8 2.5 %copy-start.10 = (f32[128,1024]{1,0:T(8,128)S(1)}, f32[128,1024]{1,0:T(8,128)}, u32[]{:S(2)}) copy-start(f32[128,1024]{1,0:T(8,128)} %copy-done.9) | copy-start | bytes 1572868
  144.8 2.0 %collective-permute-start.25 = (bf16[256,1024]{1,0:T(8,128)(2,1)S(1)}, bf16[256,1024]{1,0:T(8,128)(2,1)S(1)}, u32[]{:S(2)}, u32[]{:S(2)}) collective-permute-start(bf16[256,1024]{1,0:T(8,128)(2,1)S(1)} %get-tuple-element.112), channel_id=1, source_target_pairs={{0,1},{1,0},{2,3},{3,2},{4,5},{5,4},{6,7},{7,6},{8,9},{9,8},{10,11... | collective-permute-start | bytes 1572872 | tf_op jit(solution)/shard_map/ppermute | solution.py:470

commit v4 on v3

--- a/solution.py
+++ b/solution.py
@@ -15,8 +15,8 @@
 META = 16
 PIECE = 2 * IJ_BLK
 FLOWS = 2
-RUN = 4
-PAR = 4
+RUN = 3
+PAR = 5
 SLOTS = 4
 TOP = 32000.0
 OCTAVE = 64.0

time: 150 us -> 149 us (level)
  no operation moved by 1% of the time
where the time goes in v4:
time: 149 us; the launch traced here: 148 us
  Pallas kernels  76.4 us (51%)
  waiting for transfers between devices  34.9 us (23%)
  starting transfers between devices  23.9 us (16%)
  local copies, waits for them, and re-layouts  11.5 us (8%)
    pallas_call x7, Pallas kernels, ladder(): pl.pallas_call(functools.partial(ladder_kernel, nchunk, per, rows_ab // T...  63.4 us
    ppermute x14, waiting for transfers between devices, body(): lax.ppermute(h, 'row', ahead if f < FLOWS // 2 else behind)  25.3 us
    ppermute x14, starting transfers between devices, body(): lax.ppermute(h, 'row', ahead if f < FLOWS // 2 else behind)  15.2 us
    unnamed x34, local copies, waits for them, and re-layouts  10.6 us
    ppermute x5, starting transfers between devices, code_of(): lax.ppermute(piece, 'col', [(c, c ^ 2 * d) for c in range(ncol)])  8.36 us
    pallas_call x5, Pallas kernels, code(): pl.pallas_call(functools.partial(code_kernel, pieces), out_shape=[jax.Sha...  4.6 us
    ppermute x4, waiting for transfers between devices, body(): got = lax.ppermute(other, 'col', core)  4.55 us
    pallas_call x2, Pallas kernels, final(): pl.pallas_call(functools.partial(final_kernel, pieces, npeer, blocks, n,...  3.7 us
  transfers between devices with their start and end apart: 26, of which 17 were waited for; matrix products, arithmetic and copies ran while one was open for 1% of the time, Pallas kernels for 47%

profile of v4, /device:TPU:0, one launch (start us, length us, event | category | flops | bytes accessed | tf_op | source)
XLA Modules:
  0.0 148.4 jit_solution(3433561205195818162)
XLA Ops:
  0.0 1.6 %copy-done = bf16[128,8192]{1,0:T(8,128)(2,1)S(1)} copy-done((bf16[128,8192]{1,0:T(8,128)(2,1)S(1)}, bf16[128,8192]{1,0:T(8,128)(2,1)}, u32[]{:S(2)}) %copy-start) | copy-done | bytes 2097176
  2.3 1.9 %pack.1 = (bf16[2064,128]{1,0:T(8,128)(2,1)S(1)}, bf16[2064,128]{1,0:T(8,128)(2,1)S(1)}) custom-call(s32[4,32]{1,0:T(4,128)S(1)} %copy-done.14, bf16[128,8192]{1,0:T(8,128)(2,1)S(1)} %copy-done), custom_call_target="tpu_custom_call" | custom-call | tf_op jit(solution)/shard_map/pack/pallas_call | solution.py:85
  4.2 3.1 %collective-permute-start = (bf16[2064,128]{1,0:T(8,128)(2,1)S(1)}, bf16[2064,128]{1,0:T(8,128)(2,1)S(1)}, u32[]{:S(2)}, u32[]{:S(2)}) collective-permute-start(bf16[2064,128]{1,0:T(8,128)(2,1)S(1)} %get-tuple-element.58.rest_0_), channel_id=1, source_target_pairs={{0,8},{8,16},{16,24},{24,28},{28,20},{20,12},{12,4},{4,0},{1,9},{9... | collective-permute-start | bytes 1585160 | tf_op jit(solution)/shard_map/ppermute | solution.py:431
  8.0 2.8 %tile_list.1.list_ref = s32[397]{0:T(512)} custom-call(s32[1]{0:T(128)} %bitcast.half_ref, s32[8,32]{1,0:T(8,128)} %mask_ref.3), custom_call_target="tpu_custom_call" | custom-call | tf_op jit(solution)/shard_map/tile_list/pallas_call | solution.py:146
  10.9 8.3 %collective-permute-done.rest_2_ = bf16[2064,128]{1,0:T(8,128)(2,1)S(1)} collective-permute-done((bf16[2064,128]{1,0:T(8,128)(2,1)S(1)}, bf16[2064,128]{1,0:T(8,128)(2,1)S(1)}, u32[]{:S(2)}, u32[]{:S(2)}) %collective-permute-start) | collective-permute-done | bytes 528416 | tf_op jit(solution)/shard_map/ppermute | solution.py:431
  19.2 1.5 %collective-permute-done.1.rest_3_ = bf16[2064,128]{1,0:T(8,128)(2,1)S(1)} collective-permute-done((bf16[2064,128]{1,0:T(8,128)(2,1)S(1)}, bf16[2064,128]{1,0:T(8,128)(2,1)S(1)}, u32[]{:S(2)}, u32[]{:S(2)}) %collective-permute-start.1) | collective-permute-done | bytes 528416 | tf_op jit(solution)/shard_map/ppermute | solution.py:431
  20.7 1.6 %collective-permute-start.3 = (bf16[2064,128]{1,0:T(8,128)(2,1)S(1)}, bf16[2064,128]{1,0:T(8,128)(2,1)S(1)}, u32[]{:S(2)}, u32[]{:S(2)}) collective-permute-start(bf16[2064,128]{1,0:T(8,128)(2,1)S(1)} %collective-permute-done.rest_2_), channel_id=1, source_target_pairs={{0,8},{8,16},{16,24},{24,28},{28,20},{20,12},{12,4},{4,0},{1,9},{9... | collective-permute-start | bytes 1585160 | tf_op jit(solution)/shard_map/ppermute | solution.py:431
  23.4 7.2 %ladder.7 = f32[256,1024]{1,0:T(8,128)S(1)} custom-call(s32[397]{0:T(512)S(1)} %copy-done.13, bf16[2048,8192]{1,0:T(8,128)(2,1)} %int_ref.13, bf16[2064,128]{1,0:T(8,128)(2,1)S(1)} %get-tuple-element.58.rest_0_, bf16[2064,128]{1,0:T(8,128)(2,1)S(1)} %get-tuple-element.59.rest_1_, bf16[2064,128]{1,0:T(8,128)(2,1)S(1)} %collective-permute-done.rest_2_, ...), custom_call_target="tpu_custom_call" | custom-call | flops 4294967296 | bytes 8388608 | tf_op jit(solution)/shard_map/ladder/pallas_call | solution.py:259
  30.6 2.7 %collective-permute-done.3.rest_0_ = bf16[2064,128]{1,0:T(8,128)(2,1)S(1)} collective-permute-done((bf16[2064,128]{1,0:T(8,128)(2,1)S(1)}, bf16[2064,128]{1,0:T(8,128)(2,1)S(1)}, u32[]{:S(2)}, u32[]{:S(2)}) %collective-permute-start.3) | collective-permute-done | bytes 528416 | tf_op jit(solution)/shard_map/ppermute | solution.py:431
  33.3 1.3 collective-permute-done.4.rest_1_
  34.6 1.6 %collective-permute-start.5 = (bf16[2064,128]{1,0:T(8,128)(2,1)S(1)}, bf16[2064,128]{1,0:T(8,128)(2,1)S(1)}, u32[]{:S(2)}, u32[]{:S(2)}) collective-permute-start(bf16[2064,128]{1,0:T(8,128)(2,1)S(1)} %collective-permute-done.3.rest_0_), channel_id=1, source_target_pairs={{0,8},{8,16},{16,24},{24,28},{28,20},{20,12},{12,4},{4,0},{1,9},{9... | collective-permute-start | bytes 1585160 | tf_op jit(solution)/shard_map/ppermute | solution.py:431
  36.6 7.2 %ladder.8.mine_ref = f32[256,1024]{1,0:T(8,128)S(1)} custom-call(s32[397]{0:T(512)S(1)} %copy-done.13, bf16[2048,8192]{1,0:T(8,128)(2,1)} %int_ref.13, bf16[2064,128]{1,0:T(8,128)(2,1)S(1)} %get-tuple-element.58.rest_0_, bf16[2064,128]{1,0:T(8,128)(2,1)S(1)} %get-tuple-element.59.rest_1_, bf16[2064,128]{1,0:T(8,128)(2,1)S(1)} %collective-permute-done.rest_2_, ...), custom_call_target="tpu_custom_call" | custom-call | flops 4294967296 | bytes 8388608 | tf_op jit(solution)/shard_map/ladder/pallas_call | solution.py:259
  43.8 1.0 code.5
  44.8 2.4 %collective-permute-start.10 = (s16[256,1152]{1,0:T(8,128)(2,1)S(1)}, s16[256,1152]{1,0:T(8,128)(2,1)S(1)}, u32[]{:S(2)}, u32[]{:S(2)}) collective-permute-start(s16[256,1152]{1,0:T(8,128)(2,1)S(1)} %get-tuple-element.73), channel_id=1, source_target_pairs={{0,2},{1,3},{2,0},{3,1},{4,6},{5,7},{6,4},{7,5},{8,10},{9,11},{10,... | collective-permute-start | bytes 1769480 | tf_op jit(solution)/shard_map/ppermute | solution.py:408
  47.2 1.8 %collective-permute-done.5.rest_2_ = bf16[2064,128]{1,0:T(8,128)(2,1)S(1)} collective-permute-done((bf16[2064,128]{1,0:T(8,128)(2,1)S(1)}, bf16[2064,128]{1,0:T(8,128)(2,1)S(1)}, u32[]{:S(2)}, u32[]{:S(2)}) %collective-permute-start.5) | collective-permute-done | bytes 528416 | tf_op jit(solution)/shard_map/ppermute | solution.py:431
  49.0 1.3 collective-permute-done.6.rest_3_
  50.3 1.5 %collective-permute-start.8 = (bf16[2064,128]{1,0:T(8,128)(2,1)S(1)}, bf16[2064,128]{1,0:T(8,128)(2,1)S(1)}, u32[]{:S(2)}, u32[]{:S(2)}) collective-permute-start(bf16[2064,128]{1,0:T(8,128)(2,1)S(1)} %collective-permute-done.5.rest_2_), channel_id=1, source_target_pairs={{0,8},{8,16},{16,24},{24,28},{28,20},{20,12},{12,4},{4,0},{1,9},{9... | collective-permute-start | bytes 1585160 | tf_op jit(solution)/shard_map/ppermute | solution.py:431
  52.3 7.2 %ladder.9 = f32[256,1024]{1,0:T(8,128)S(1)} custom-call(s32[397]{0:T(512)S(1)} %copy-done.13, bf16[2048,8192]{1,0:T(8,128)(2,1)} %int_ref.13, bf16[2064,128]{1,0:T(8,128)(2,1)S(1)} %collective-permute-done.3.rest_0_, bf16[2064,128]{1,0:T(8,128)(2,1)S(1)} %collective-permute-done.4.rest_1_, bf16[2064,128]{1,0:T(8,128)(2,1)S(1)} %collective-permute-done.5.rest_2_, ...), custom_call_target="tpu_custom_call" | custom-call | flops 4294967296 | bytes 8388608 | tf_op jit(solution)/shard_map/ladder/pallas_call | solution.py:259
  60.0 0.8 copy-done.1
  60.8 2.8 %collective-permute-done.8.rest_0_ = bf16[2064,128]{1,0:T(8,128)(2,1)S(1)} collective-permute-done((bf16[2064,128]{1,0:T(8,128)(2,1)S(1)}, bf16[2064,128]{1,0:T(8,128)(2,1)S(1)}, u32[]{:S(2)}, u32[]{:S(2)}) %collective-permute-start.8) | collective-permute-done | bytes 528416 | tf_op jit(solution)/shard_map/ppermute | solution.py:431
  63.6 1.2 collective-permute-done.9.rest_1_
  65.5 1.4 collective-permute-start.12
  66.9 7.3 %ladder.10.mine_ref = f32[256,1024]{1,0:T(8,128)S(1)} custom-call(s32[397]{0:T(512)S(1)} %copy-done.13, bf16[2048,8192]{1,0:T(8,128)(2,1)} %int_ref.13, bf16[2064,128]{1,0:T(8,128)(2,1)S(1)} %collective-permute-done.3.rest_0_, bf16[2064,128]{1,0:T(8,128)(2,1)S(1)} %collective-permute-done.4.rest_1_, bf16[2064,128]{1,0:T(8,128)(2,1)S(1)} %collective-permute-done.5.rest_2_, ...), custom_call_target="tpu_custom_call" | custom-call | flops 4294967296 | bytes 8388608 | tf_op jit(solution)/shard_map/ladder/pallas_call | solution.py:259
  74.3 1.0 code.6
  75.2 4.0 %collective-permute-done.11.rest_2_ = bf16[2064,128]{1,0:T(8,128)(2,1)S(1)} collective-permute-done((bf16[2064,128]{1,0:T(8,128)(2,1)S(1)}, bf16[2064,128]{1,0:T(8,128)(2,1)S(1)}, u32[]{:S(2)}, u32[]{:S(2)}) %collective-permute-start.11) | collective-permute-done | bytes 528416 | tf_op jit(solution)/shard_map/ppermute | solution.py:431
  79.6 1.5 %collective-permute-start.16 = (s16[256,1152]{1,0:T(8,128)(2,1)S(1)}, s16[256,1152]{1,0:T(8,128)(2,1)S(1)}, u32[]{:S(2)}, u32[]{:S(2)}) collective-permute-start(s16[256,1152]{1,0:T(8,128)(2,1)S(1)} %get-tuple-element.83), channel_id=1, source_target_pairs={{0,2},{1,3},{2,0},{3,1},{4,6},{5,7},{6,4},{7,5},{8,10},{9,11},{10,... | collective-permute-start | bytes 1769480 | tf_op jit(solution)/shard_map/ppermute | solution.py:408
  81.7 1.4 collective-permute-start.15
  83.1 11.6 %ladder.11 = (f32[256,1024]{1,0:T(8,128)S(1)}, f32[256,1024]{1,0:T(8,128)S(1)}) custom-call(s32[397]{0:T(512)S(1)} %copy-done.13, bf16[2048,8192]{1,0:T(8,128)(2,1)} %int_ref.13, bf16[2064,128]{1,0:T(8,128)(2,1)S(1)} %collective-permute-done.8.rest_0_, bf16[2064,128]{1,0:T(8,128)(2,1)S(1)} %collective-permute-done.9.rest_1_, ...), custom_call_target="tpu_custom_call" | custom-call | flops 8589934592 | bytes 16777216 | tf_op jit(solution)/shard_map/ladder/pallas_call | solution.py:259
  94.9 2.6 %collective-permute-done.19.got_ref = f32[256,1024]{1,0:T(8,128)S(1)} collective-permute-done((f32[256,1024]{1,0:T(8,128)S(1)}, f32[256,1024]{1,0:T(8,128)S(1)}, u32[]{:S(2)}, u32[]{:S(2)}) %collective-permute-start.19) | collective-permute-done | bytes 1048608 | tf_op jit(solution)/shard_map/ppermute | solution.py:441
  97.5 0.9 code.7
  98.5 1.5 collective-permute-start.20
  100.1 1.9 %collective-permute-start.18 = (bf16[2064,128]{1,0:T(8,128)(2,1)S(1)}, bf16[2064,128]{1,0:T(8,128)(2,1)S(1)}, u32[]{:S(2)}, u32[]{:S(2)}) collective-permute-start(bf16[2064,128]{1,0:T(8,128)(2,1)S(1)} %collective-permute-done.15.rest_1_), channel_id=1, source_target_pairs={{8,0},{16,8},{24,16},{28,24},{20,28},{12,20},{4,12},{0,4},{9,1},{1... | collective-permute-start | bytes 1585160 | tf_op jit(solution)/shard_map/ppermute | solution.py:431
  102.0 11.4 %ladder.12 = (f32[128,1024]{1,0:T(8,128)S(1)}, f32[128,1024]{1,0:T(8,128)S(1)}) custom-call(s32[397]{0:T(512)S(1)} %copy-done.13, bf16[2048,8192]{1,0:T(8,128)(2,1)} %int_ref.13, bf16[2064,128]{1,0:T(8,128)(2,1)S(1)} %collective-permute-done.14.rest_0_, bf16[2064,128]{1,0:T(8,128)(2,1)S(1)} %collective-permute-done.15.rest_1_), custom_call_target="tpu_custom_call" | custom-call | flops 4294967296 | bytes 16777216 | tf_op jit(solution)/shard_map/ladder/pallas_call | solution.py:259
  114.0 1.9 %collective-permute-done.21.got_ref = f32[128,1024]{1,0:T(8,128)S(1)} collective-permute-done((f32[128,1024]{1,0:T(8,128)S(1)}, f32[128,1024]{1,0:T(8,128)S(1)}, u32[]{:S(2)}, u32[]{:S(2)}) %collective-permute-start.21) | collective-permute-done | bytes 524320 | tf_op jit(solution)/shard_map/ppermute | solution.py:447
  117.2 1.4 collective-permute-start.22
  118.6 11.6 %ladder.13 = (f32[128,1024]{1,0:T(8,128)S(1)}, f32[128,1024]{1,0:T(8,128)S(1)}) custom-call(s32[397]{0:T(512)S(1)} %copy-done.13, bf16[2048,8192]{1,0:T(8,128)(2,1)} %int_ref.13, bf16[2064,128]{1,0:T(8,128)(2,1)S(1)} %collective-permute-done.17.rest_0_, bf16[2064,128]{1,0:T(8,128)(2,1)S(1)} %collective-permute-done.18.rest_1_), custom_call_target="tpu_custom_call" | custom-call | flops 4294967296 | bytes 16777216 | tf_op jit(solution)/shard_map/ladder/pallas_call | solution.py:259
  130.3 1.9 %collective-permute-done.23.got_ref = f32[128,1024]{1,0:T(8,128)S(1)} collective-permute-done((f32[128,1024]{1,0:T(8,128)S(1)}, f32[128,1024]{1,0:T(8,128)S(1)}, u32[]{:S(2)}, u32[]{:S(2)}) %collective-permute-start.23) | collective-permute-done | bytes 524320 | tf_op jit(solution)/shard_map/ppermute | solution.py:467
  132.2 1.2 code.9
  134.2 1.6 %collective-permute-start.24 = (s16[128,1152]{1,0:T(8,128)(2,1)}, s16[128,1152]{1,0:T(8,128)(2,1)}, u32[]{:S(2)}, u32[]{:S(2)}) collective-permute-start(s16[128,1152]{1,0:T(8,128)(2,1)} %get-tuple-element.102), channel_id=1, source_target_pairs={{0,2},{1,3},{2,0},{3,1},{4,6},{5,7},{6,4},{7,5},{8,10},{9,11},{10,... | collective-permute-start | bytes 884744 | tf_op jit(solution)/shard_map/ppermute | solution.py:408
  135.9 1.1 copy-done.2
  137.0 1.1 copy-done.4
  138.1 1.1 copy-done.6
  139.1 1.0 copy-done.8
  140.2 1.0 copy-done.12
  141.1 2.3 %final.2.rest_2_ = bf16[2,256,1024]{2,1,0:T(8,128)(2,1)S(1)} custom-call(s32[15]{0:T(128)S(1)} %dynamic-slice_bitcast_fusion.src_ref, s32[2]{0:T(128)S(1)} %pad_add_fusion.place_ref, f32[2,256,1]{2,1,0:T(8,128)S(1)} %copy.10.occ_ref, f32[1,1024]{1,0:T(1,128)S(1)} %bitcast.13, f32[256,1024]{1,0:T(8,128)S(1)} %get-tuple-element.103.rest_0_, ...), custom_call_target="tpu_custom_call" | custom-call | tf_op jit(solution)/shard_map/final/pallas_call | solution.py:361
  143.6 1.4 final.3
  145.2 1.9 %collective-permute-done.25 = bf16[256,1024]{1,0:T(8,128)(2,1)S(1)} collective-permute-done((bf16[256,1024]{1,0:T(8,128)(2,1)S(1)}, bf16[256,1024]{1,0:T(8,128)(2,1)S(1)}, u32[]{:S(2)}, u32[]{:S(2)}) %collective-permute-start.25) | collective-permute-done | bytes 524320 | tf_op jit(solution)/shard_map/ppermute | solution.py:470
  147.1 1.4 maximum_select_fusion
  (61 shorter events, 9.1 us)
Async XLA Ops:
  0.0 1.6 %copy-start = (bf16[128,8192]{1,0:T(8,128)(2,1)S(1)}, bf16[128,8192]{1,0:T(8,128)(2,1)}, u32[]{:S(2)}) copy-start(bf16[128,8192]{1,0:T(8,128)(2,1)} %amp_ref.1) | copy-start | bytes 6291460
  1.6 0.7 copy-start.14
  2.3 5.0 %copy-start.16 = (f32[256]{0:T(256)S(1)}, f32[256]{0:T(256)}, u32[]{:S(2)}) copy-start(f32[256]{0:T(256)} %param.11) | copy-start | bytes 3076
  2.3 8.6 %copy-start.15 = (f32[2048]{0:T(1024)S(1)}, f32[2048]{0:T(1024)}, u32[]{:S(2)}) copy-start(f32[2048]{0:T(1024)} %param.12) | copy-start | bytes 24580
  4.2 15.0 %collective-permute-start = (bf16[2064,128]{1,0:T(8,128)(2,1)S(1)}, bf16[2064,128]{1,0:T(8,128)(2,1)S(1)}, u32[]{:S(2)}, u32[]{:S(2)}) collective-permute-start(bf16[2064,128]{1,0:T(8,128)(2,1)S(1)} %get-tuple-element.58.rest_0_), channel_id=1, source_target_pairs={{0,8},{8,16},{16,24},{24,28},{28,20},{20,12},{12,4},{4,0},{1,9},{9... | collective-permute-start | bytes 1585160 | tf_op jit(solution)/shard_map/ppermute | solution.py:431
  7.2 13.5 %collective-permute-start.1 = (bf16[2064,128]{1,0:T(8,128)(2,1)S(1)}, bf16[2064,128]{1,0:T(8,128)(2,1)S(1)}, u32[]{:S(2)}, u32[]{:S(2)}) collective-permute-start(bf16[2064,128]{1,0:T(8,128)(2,1)S(1)} %get-tuple-element.59.rest_1_), channel_id=1, source_target_pairs={{8,0},{16,8},{24,16},{28,24},{20,28},{12,20},{4,12},{0,4},{9,1},{1... | collective-permute-start | bytes 1585160 | tf_op jit(solution)/shard_map/ppermute | solution.py:431
  7.3 3.6 %collective-permute-start.2 = (f32[256]{0:T(256)S(1)}, f32[256]{0:T(256)S(1)}, u32[]{:S(2)}, u32[]{:S(2)}) collective-permute-start(f32[256]{0:T(256)S(1)} %copy-done.16), channel_id=1, source_target_pairs={{0,1},{1,0},{2,3},{3,2},{4,5},{5,4},{6,7},{7,6},{8,9},{9,8},{10,11... | collective-permute-start | bytes 3080 | tf_op jit(solution)/shard_map/ppermute | solution.py:392
  20.7 12.6 %collective-permute-start.3 = (bf16[2064,128]{1,0:T(8,128)(2,1)S(1)}, bf16[2064,128]{1,0:T(8,128)(2,1)S(1)}, u32[]{:S(2)}, u32[]{:S(2)}) collective-permute-start(bf16[2064,128]{1,0:T(8,128)(2,1)S(1)} %collective-permute-done.rest_2_), channel_id=1, source_target_pairs={{0,8},{8,16},{16,24},{24,28},{28,20},{20,12},{12,4},{4,0},{1,9},{9... | collective-permute-start | bytes 1585160 | tf_op jit(solution)/shard_map/ppermute | solution.py:431
  22.3 12.3 %collective-permute-start.4 = (bf16[2064,128]{1,0:T(8,128)(2,1)S(1)}, bf16[2064,128]{1,0:T(8,128)(2,1)S(1)}, u32[]{:S(2)}, u32[]{:S(2)}) collective-permute-start(bf16[2064,128]{1,0:T(8,128)(2,1)S(1)} %collective-permute-done.1.rest_3_), channel_id=1, source_target_pairs={{8,0},{16,8},{24,16},{28,24},{20,28},{12,20},{4,12},{0,4},{9,1},{1... | collective-permute-start | bytes 1585160 | tf_op jit(solution)/shard_map/ppermute | solution.py:431
  22.7 0.7 copy-start.13
  34.6 9.2 %collective-permute-start.7 = (f32[256,1024]{1,0:T(8,128)S(1)}, f32[256,1024]{1,0:T(8,128)S(1)}, u32[]{:S(2)}, u32[]{:S(2)}) collective-permute-start(f32[256,1024]{1,0:T(8,128)S(1)} %ladder.7), channel_id=1, source_target_pairs={{0,1},{1,0},{2,3},{3,2},{4,5},{5,4},{6,7},{7,6},{8,9},{9,8},{10,11... | collective-permute-start | bytes 3145736 | tf_op jit(solution)/shard_map/ppermute | solution.py:452
  34.6 14.4 %collective-permute-start.5 = (bf16[2064,128]{1,0:T(8,128)(2,1)S(1)}, bf16[2064,128]{1,0:T(8,128)(2,1)S(1)}, u32[]{:S(2)}, u32[]{:S(2)}) collective-permute-start(bf16[2064,128]{1,0:T(8,128)(2,1)S(1)} %collective-permute-done.3.rest_0_), channel_id=1, source_target_pairs={{0,8},{8,16},{16,24},{24,28},{28,20},{20,12},{12,4},{4,0},{1,9},{9... | collective-permute-start | bytes 1585160 | tf_op jit(solution)/shard_map/ppermute | solution.py:431
  36.2 14.1 %collective-permute-start.6 = (bf16[2064,128]{1,0:T(8,128)(2,1)S(1)}, bf16[2064,128]{1,0:T(8,128)(2,1)S(1)}, u32[]{:S(2)}, u32[]{:S(2)}) collective-permute-start(bf16[2064,128]{1,0:T(8,128)(2,1)S(1)} %collective-permute-done.4.rest_1_), channel_id=1, source_target_pairs={{8,0},{16,8},{24,16},{28,24},{20,28},{12,20},{4,12},{0,4},{9,1},{1... | collective-permute-start | bytes 1585160 | tf_op jit(solution)/shard_map/ppermute | solution.py:431
  44.8 15.2 %collective-permute-start.10 = (s16[256,1152]{1,0:T(8,128)(2,1)S(1)}, s16[256,1152]{1,0:T(8,128)(2,1)S(1)}, u32[]{:S(2)}, u32[]{:S(2)}) collective-permute-start(s16[256,1152]{1,0:T(8,128)(2,1)S(1)} %get-tuple-element.73), channel_id=1, source_target_pairs={{0,2},{1,3},{2,0},{3,1},{4,6},{5,7},{6,4},{7,5},{8,10},{9,11},{10,... | collective-permute-start | bytes 1769480 | tf_op jit(solution)/shard_map/ppermute | solution.py:408
  50.3 13.3 %collective-permute-start.8 = (bf16[2064,128]{1,0:T(8,128)(2,1)S(1)}, bf16[2064,128]{1,0:T(8,128)(2,1)S(1)}, u32[]{:S(2)}, u32[]{:S(2)}) collective-permute-start(bf16[2064,128]{1,0:T(8,128)(2,1)S(1)} %collective-permute-done.5.rest_2_), channel_id=1, source_target_pairs={{0,8},{8,16},{16,24},{24,28},{28,20},{20,12},{12,4},{4,0},{1,9},{9... | collective-permute-start | bytes 1585160 | tf_op jit(solution)/shard_map/ppermute | solution.py:431
  51.8 13.0 %collective-permute-start.9 = (bf16[2064,128]{1,0:T(8,128)(2,1)S(1)}, bf16[2064,128]{1,0:T(8,128)(2,1)S(1)}, u32[]{:S(2)}, u32[]{:S(2)}) collective-permute-start(bf16[2064,128]{1,0:T(8,128)(2,1)S(1)} %collective-permute-done.6.rest_3_), channel_id=1, source_target_pairs={{8,0},{16,8},{24,16},{28,24},{20,28},{12,20},{4,12},{0,4},{9,1},{1... | collective-permute-start | bytes 1585160 | tf_op jit(solution)/shard_map/ppermute | solution.py:431
  60.0 0.8 copy-start.1
  64.9 9.4 %collective-permute-start.13 = (f32[256,1024]{1,0:T(8,128)S(1)}, f32[256,1024]{1,0:T(8,128)S(1)}, u32[]{:S(2)}, u32[]{:S(2)}) collective-permute-start(f32[256,1024]{1,0:T(8,128)S(1)} %ladder.9), channel_id=1, source_target_pairs={{0,1},{1,0},{2,3},{3,2},{4,5},{5,4},{6,7},{7,6},{8,9},{9,8},{10,11... | collective-permute-start | bytes 3145736 | tf_op jit(solution)/shard_map/ppermute | solution.py:452
  64.9 14.4 %collective-permute-start.11 = (bf16[2064,128]{1,0:T(8,128)(2,1)S(1)}, bf16[2064,128]{1,0:T(8,128)(2,1)S(1)}, u32[]{:S(2)}, u32[]{:S(2)}) collective-permute-start(bf16[2064,128]{1,0:T(8,128)(2,1)S(1)} %collective-permute-done.8.rest_0_), channel_id=1, source_target_pairs={{0,8},{8,16},{16,24},{24,28},{28,20},{20,12},{12,4},{4,0},{1,9},{9... | collective-permute-start | bytes 1585160 | tf_op jit(solution)/shard_map/ppermute | solution.py:431
  65.5 14.1 %collective-permute-start.12 = (bf16[2064,128]{1,0:T(8,128)(2,1)S(1)}, bf16[2064,128]{1,0:T(8,128)(2,1)S(1)}, u32[]{:S(2)}, u32[]{:S(2)}) collective-permute-start(bf16[2064,128]{1,0:T(8,128)(2,1)S(1)} %collective-permute-done.9.rest_1_), channel_id=1, source_target_pairs={{8,0},{16,8},{24,16},{28,24},{20,28},{12,20},{4,12},{0,4},{9,1},{1... | collective-permute-start | bytes 1585160 | tf_op jit(solution)/shard_map/ppermute | solution.py:431
  79.6 15.1 %collective-permute-start.16 = (s16[256,1152]{1,0:T(8,128)(2,1)S(1)}, s16[256,1152]{1,0:T(8,128)(2,1)S(1)}, u32[]{:S(2)}, u32[]{:S(2)}) collective-permute-start(s16[256,1152]{1,0:T(8,128)(2,1)S(1)} %get-tuple-element.83), channel_id=1, source_target_pairs={{0,2},{1,3},{2,0},{3,1},{4,6},{5,7},{6,4},{7,5},{8,10},{9,11},{10,... | collective-permute-start | bytes 1769480 | tf_op jit(solution)/shard_map/ppermute | solution.py:408
  81.1 13.7 %collective-permute-start.14 = (bf16[2064,128]{1,0:T(8,128)(2,1)S(1)}, bf16[2064,128]{1,0:T(8,128)(2,1)S(1)}, u32[]{:S(2)}, u32[]{:S(2)}) collective-permute-start(bf16[2064,128]{1,0:T(8,128)(2,1)S(1)} %collective-permute-done.11.rest_2_), channel_id=1, source_target_pairs={{0,8},{8,16},{16,24},{24,28},{28,20},{20,12},{12,4},{4,0},{1,9},{9... | collective-permute-start | bytes 1585160 | tf_op jit(solution)/shard_map/ppermute | solution.py:431
  81.7 13.1 %collective-permute-start.15 = (bf16[2064,128]{1,0:T(8,128)(2,1)S(1)}, bf16[2064,128]{1,0:T(8,128)(2,1)S(1)}, u32[]{:S(2)}, u32[]{:S(2)}) collective-permute-start(bf16[2064,128]{1,0:T(8,128)(2,1)S(1)} %collective-permute-done.12.rest_3_), channel_id=1, source_target_pairs={{8,0},{16,8},{24,16},{28,24},{20,28},{12,20},{4,12},{0,4},{9,1},{1... | collective-permute-start | bytes 1585160 | tf_op jit(solution)/shard_map/ppermute | solution.py:431
  94.8 18.6 %copy-start.3 = (s16[256,1152]{1,0:T(8,128)(2,1)}, s16[256,1152]{1,0:T(8,128)(2,1)S(1)}, u32[]{:S(2)}) copy-start(s16[256,1152]{1,0:T(8,128)(2,1)S(1)} %collective-permute-done.16.rest_5_) | copy-start | bytes 1769476
  94.8 2.7 %collective-permute-start.19 = (f32[256,1024]{1,0:T(8,128)S(1)}, f32[256,1024]{1,0:T(8,128)S(1)}, u32[]{:S(2)}, u32[]{:S(2)}) collective-permute-start(f32[256,1024]{1,0:T(8,128)S(1)} %get-tuple-element.90), channel_id=1, source_target_pairs={{0,1},{1,0},{2,3},{3,2},{4,5},{5,4},{6,7},{7,6},{8,9},{9,8},{10,11... | collective-permute-start | bytes 3145736 | tf_op jit(solution)/shard_map/ppermute | solution.py:441
  98.5 15.4 %collective-permute-start.20 = (s16[256,1152]{1,0:T(8,128)(2,1)S(1)}, s16[256,1152]{1,0:T(8,128)(2,1)S(1)}, u32[]{:S(2)}, u32[]{:S(2)}) collective-permute-start(s16[256,1152]{1,0:T(8,128)(2,1)S(1)} %get-tuple-element.91), channel_id=1, source_target_pairs={{0,2},{1,3},{2,0},{3,1},{4,6},{5,7},{6,4},{7,5},{8,10},{9,11},{10,... | collective-permute-start | bytes 1769480 | tf_op jit(solution)/shard_map/ppermute | solution.py:408
  99.9 14.0 %collective-permute-start.17 = (bf16[2064,128]{1,0:T(8,128)(2,1)S(1)}, bf16[2064,128]{1,0:T(8,128)(2,1)S(1)}, u32[]{:S(2)}, u32[]{:S(2)}) collective-permute-start(bf16[2064,128]{1,0:T(8,128)(2,1)S(1)} %collective-permute-done.14.rest_0_), channel_id=1, source_target_pairs={{0,8},{8,16},{16,24},{24,28},{28,20},{20,12},{12,4},{4,0},{1,9},{9... | collective-permute-start | bytes 1585160 | tf_op jit(solution)/shard_map/ppermute | solution.py:431
  100.1 13.8 %collective-permute-start.18 = (bf16[2064,128]{1,0:T(8,128)(2,1)S(1)}, bf16[2064,128]{1,0:T(8,128)(2,1)S(1)}, u32[]{:S(2)}, u32[]{:S(2)}) collective-permute-start(bf16[2064,128]{1,0:T(8,128)(2,1)S(1)} %collective-permute-done.15.rest_1_), channel_id=1, source_target_pairs={{8,0},{16,8},{24,16},{28,24},{20,28},{12,20},{4,12},{0,4},{9,1},{1... | collective-permute-start | bytes 1585160 | tf_op jit(solution)/shard_map/ppermute | solution.py:431
  113.9 16.3 %copy-start.5 = (s16[256,1152]{1,0:T(8,128)(2,1)}, s16[256,1152]{1,0:T(8,128)(2,1)S(1)}, u32[]{:S(2)}) copy-start(s16[256,1152]{1,0:T(8,128)(2,1)S(1)} %collective-permute-done.20.rest_6_) | copy-start | bytes 1769476
  113.9 2.0 %collective-permute-start.21 = (f32[128,1024]{1,0:T(8,128)S(1)}, f32[128,1024]{1,0:T(8,128)S(1)}, u32[]{:S(2)}, u32[]{:S(2)}) collective-permute-start(f32[128,1024]{1,0:T(8,128)S(1)} %get-tuple-element.98), channel_id=1, source_target_pairs={{0,1},{1,0},{2,3},{3,2},{4,5},{5,4},{6,7},{7,6},{8,9},{9,8},{10,11... | collective-permute-start | bytes 1572872 | tf_op jit(solution)/shard_map/ppermute | solution.py:447
  116.4 0.8 copy-start.7
  117.2 13.0 %collective-permute-start.22 = (s16[128,1152]{1,0:T(8,128)(2,1)S(1)}, s16[128,1152]{1,0:T(8,128)(2,1)S(1)}, u32[]{:S(2)}, u32[]{:S(2)}) collective-permute-start(s16[128,1152]{1,0:T(8,128)(2,1)S(1)} %get-tuple-element.99), channel_id=1, source_target_pairs={{0,2},{1,3},{2,0},{3,1},{4,6},{5,7},{6,4},{7,5},{8,10},{9,11},{10,... | collective-permute-start | bytes 884744 | tf_op jit(solution)/shard_map/ppermute | solution.py:408
  130.2 4.0 %copy-start.11 = (s16[128,1152]{1,0:T(8,128)(2,1)}, s16[128,1152]{1,0:T(8,128)(2,1)S(1)}, u32[]{:S(2)}) copy-start(s16[128,1152]{1,0:T(8,128)(2,1)S(1)} %collective-permute-done.22.rest_7_) | copy-start | bytes 884740
  130.2 2.0 %collective-permute-start.23 = (f32[128,1024]{1,0:T(8,128)S(1)}, f32[128,1024]{1,0:T(8,128)S(1)}, u32[]{:S(2)}, u32[]{:S(2)}) collective-permute-start(f32[128,1024]{1,0:T(8,128)S(1)} %get-tuple-element.100), channel_id=1, source_target_pairs={{0,1},{1,0},{2,3},{3,2},{4,5},{5,4},{6,7},{7,6},{8,9},{9,8},{10,11... | collective-permute-start | bytes 1572872 | tf_op jit(solution)/shard_map/ppermute | solution.py:467
  133.4 0.8 copy-start.9
  134.2 9.4 %collective-permute-start.24 = (s16[128,1152]{1,0:T(8,128)(2,1)}, s16[128,1152]{1,0:T(8,128)(2,1)}, u32[]{:S(2)}, u32[]{:S(2)}) collective-permute-start(s16[128,1152]{1,0:T(8,128)(2,1)} %get-tuple-element.102), channel_id=1, source_target_pairs={{0,2},{1,3},{2,0},{3,1},{4,6},{5,7},{6,4},{7,5},{8,10},{9,11},{10,... | collective-permute-start | bytes 884744 | tf_op jit(solution)/shard_map/ppermute | solution.py:408
  135.9 1.1 copy-start.2
  137.0 1.1 copy-start.4
  138.1 1.1 copy-start.6
  139.1 1.0 copy-start.8
  140.2 1.0 copy-start.12
  141.1 2.4 %copy-start.10 = (f32[128,1024]{1,0:T(8,128)S(1)}, f32[128,1024]{1,0:T(8,128)}, u32[]{:S(2)}) copy-start(f32[128,1024]{1,0:T(8,128)} %copy-done.9) | copy-start | bytes 1572868
  145.1 2.0 %collective-permute-start.25 = (bf16[256,1024]{1,0:T(8,128)(2,1)S(1)}, bf16[256,1024]{1,0:T(8,128)(2,1)S(1)}, u32[]{:S(2)}, u32[]{:S(2)}) collective-permute-start(bf16[256,1024]{1,0:T(8,128)(2,1)S(1)} %get-tuple-element.112), channel_id=1, source_target_pairs={{0,1},{1,0},{2,3},{3,2},{4,5},{5,4},{6,7},{7,6},{8,9},{9,8},{10,11... | collective-permute-start | bytes 1572872 | tf_op jit(solution)/shard_map/ppermute | solution.py:470

commit v5 on v4

--- a/solution.py
+++ b/solution.py
@@ -17,7 +17,7 @@
 FLOWS = 2
 RUN = 3
 PAR = 5
-SLOTS = 4
+SLOTS = 5
 TOP = 32000.0
 OCTAVE = 64.0
 LN2 = 0.6931471805599453

time: 149 us -> 149 us (level)
  waiting for transfers between devices: 34.9 us -> 36.9 us
  starting transfers between devices: 23.9 us -> 22 us
    ppermute x5, starting transfers between devices: 8.36 us -> 5.65 us  [code_of(): lax.ppermute(piece, 'col', [(c, c ^ 2 * d) for c in range(ncol)])]
    ppermute x5, waiting for transfers between devices: 1.24 us -> 2.79 us  [code_of(): lax.ppermute(piece, 'col', [(c, c ^ 2 * d) for c in range(ncol)])]
  transfers between devices with their start and end apart: 26 -> 26, of which waited for: 17 -> 17; matrix products, arithmetic and copies ran while one was open for 1% -> 1% of each run, Pallas kernels for 47% -> 48%
where the time goes in v5:
time: 149 us
  Pallas kernels  76.7 us (51%)
  waiting for transfers between devices  36.9 us (25%)
  starting transfers between devices  22 us (15%)
  local copies, waits for them, and re-layouts  11.5 us (8%)
    pallas_call x7, Pallas kernels, ladder(): pl.pallas_call(functools.partial(ladder_kernel, nchunk, per, rows_ab // T...  63.7 us
    ppermute x14, waiting for transfers between devices, body(): lax.ppermute(h, 'row', ahead if f < FLOWS // 2 else behind)  26.1 us
    ppermute x14, starting transfers between devices, body(): lax.ppermute(h, 'row', ahead if f < FLOWS // 2 else behind)  15.2 us
    unnamed x34, local copies, waits for them, and re-layouts  10.6 us
    ppermute x5, starting transfers between devices, code_of(): lax.ppermute(piece, 'col', [(c, c ^ 2 * d) for c in range(ncol)])  5.65 us
    pallas_call x5, Pallas kernels, code(): pl.pallas_call(functools.partial(code_kernel, pieces), out_shape=[jax.Sha...  4.6 us
    ppermute x4, waiting for transfers between devices, body(): got = lax.ppermute(other, 'col', core)  4.55 us
    pallas_call x2, Pallas kernels, final(): pl.pallas_call(functools.partial(final_kernel, pieces, npeer, blocks, n,...  3.7 us
  transfers between devices with their start and end apart: 26, of which 17 were waited for; matrix products, arithmetic and copies ran while one was open for 1% of the time, Pallas kernels for 48%

profile of v5, /device:TPU:0, one launch (start us, length us, event | category | flops | bytes accessed | tf_op | source)
XLA Modules:
  0.0 148.7 jit_solution(18407941896737646586)
XLA Ops:
  0.0 1.6 %copy-done = bf16[128,8192]{1,0:T(8,128)(2,1)S(1)} copy-done((bf16[128,8192]{1,0:T(8,128)(2,1)S(1)}, bf16[128,8192]{1,0:T(8,128)(2,1)}, u32[]{:S(2)}) %copy-start) | copy-done | bytes 2097176
  2.3 1.9 %pack.1 = (bf16[2064,128]{1,0:T(8,128)(2,1)S(1)}, bf16[2064,128]{1,0:T(8,128)(2,1)S(1)}) custom-call(s32[4,32]{1,0:T(4,128)S(1)} %copy-done.14, bf16[128,8192]{1,0:T(8,128)(2,1)S(1)} %copy-done), custom_call_target="tpu_custom_call" | custom-call | tf_op jit(solution)/shard_map/pack/pallas_call | solution.py:85
  4.2 3.1 %collective-permute-start = (bf16[2064,128]{1,0:T(8,128)(2,1)S(1)}, bf16[2064,128]{1,0:T(8,128)(2,1)S(1)}, u32[]{:S(2)}, u32[]{:S(2)}) collective-permute-start(bf16[2064,128]{1,0:T(8,128)(2,1)S(1)} %get-tuple-element.58.rest_0_), channel_id=1, source_target_pairs={{0,8},{8,16},{16,24},{24,28},{28,20},{20,12},{12,4},{4,0},{1,9},{9... | collective-permute-start | bytes 1585160 | tf_op jit(solution)/shard_map/ppermute | solution.py:431
  8.0 2.8 %tile_list.1.list_ref = s32[397]{0:T(512)} custom-call(s32[1]{0:T(128)} %bitcast.half_ref, s32[8,32]{1,0:T(8,128)} %mask_ref.3), custom_call_target="tpu_custom_call" | custom-call | tf_op jit(solution)/shard_map/tile_list/pallas_call | solution.py:146
  10.9 8.3 %collective-permute-done.rest_2_ = bf16[2064,128]{1,0:T(8,128)(2,1)S(1)} collective-permute-done((bf16[2064,128]{1,0:T(8,128)(2,1)S(1)}, bf16[2064,128]{1,0:T(8,128)(2,1)S(1)}, u32[]{:S(2)}, u32[]{:S(2)}) %collective-permute-start) | collective-permute-done | bytes 528416 | tf_op jit(solution)/shard_map/ppermute | solution.py:431
  19.2 1.5 %collective-permute-done.1.rest_3_ = bf16[2064,128]{1,0:T(8,128)(2,1)S(1)} collective-permute-done((bf16[2064,128]{1,0:T(8,128)(2,1)S(1)}, bf16[2064,128]{1,0:T(8,128)(2,1)S(1)}, u32[]{:S(2)}, u32[]{:S(2)}) %collective-permute-start.1) | collective-permute-done | bytes 528416 | tf_op jit(solution)/shard_map/ppermute | solution.py:431
  20.7 1.6 %collective-permute-start.3 = (bf16[2064,128]{1,0:T(8,128)(2,1)S(1)}, bf16[2064,128]{1,0:T(8,128)(2,1)S(1)}, u32[]{:S(2)}, u32[]{:S(2)}) collective-permute-start(bf16[2064,128]{1,0:T(8,128)(2,1)S(1)} %collective-permute-done.rest_2_), channel_id=1, source_target_pairs={{0,8},{8,16},{16,24},{24,28},{28,20},{20,12},{12,4},{4,0},{1,9},{9... | collective-permute-start | bytes 1585160 | tf_op jit(solution)/shard_map/ppermute | solution.py:431
  23.4 7.2 %ladder.7 = f32[256,1024]{1,0:T(8,128)S(1)} custom-call(s32[397]{0:T(512)S(1)} %copy-done.13, bf16[2048,8192]{1,0:T(8,128)(2,1)} %int_ref.13, bf16[2064,128]{1,0:T(8,128)(2,1)S(1)} %get-tuple-element.58.rest_0_, bf16[2064,128]{1,0:T(8,128)(2,1)S(1)} %get-tuple-element.59.rest_1_, bf16[2064,128]{1,0:T(8,128)(2,1)S(1)} %collective-permute-done.rest_2_, ...), custom_call_target="tpu_custom_call" | custom-call | flops 4294967296 | bytes 8388608 | tf_op jit(solution)/shard_map/ladder/pallas_call | solution.py:259
  30.6 2.7 %collective-permute-done.3.rest_0_ = bf16[2064,128]{1,0:T(8,128)(2,1)S(1)} collective-permute-done((bf16[2064,128]{1,0:T(8,128)(2,1)S(1)}, bf16[2064,128]{1,0:T(8,128)(2,1)S(1)}, u32[]{:S(2)}, u32[]{:S(2)}) %collective-permute-start.3) | collective-permute-done | bytes 528416 | tf_op jit(solution)/shard_map/ppermute | solution.py:431
  33.3 1.3 collective-permute-done.4.rest_1_
  34.6 1.6 %collective-permute-start.5 = (bf16[2064,128]{1,0:T(8,128)(2,1)S(1)}, bf16[2064,128]{1,0:T(8,128)(2,1)S(1)}, u32[]{:S(2)}, u32[]{:S(2)}) collective-permute-start(bf16[2064,128]{1,0:T(8,128)(2,1)S(1)} %collective-permute-done.3.rest_0_), channel_id=1, source_target_pairs={{0,8},{8,16},{16,24},{24,28},{28,20},{20,12},{12,4},{4,0},{1,9},{9... | collective-permute-start | bytes 1585160 | tf_op jit(solution)/shard_map/ppermute | solution.py:431
  36.6 7.2 %ladder.8.mine_ref = f32[256,1024]{1,0:T(8,128)S(1)} custom-call(s32[397]{0:T(512)S(1)} %copy-done.13, bf16[2048,8192]{1,0:T(8,128)(2,1)} %int_ref.13, bf16[2064,128]{1,0:T(8,128)(2,1)S(1)} %get-tuple-element.58.rest_0_, bf16[2064,128]{1,0:T(8,128)(2,1)S(1)} %get-tuple-element.59.rest_1_, bf16[2064,128]{1,0:T(8,128)(2,1)S(1)} %collective-permute-done.rest_2_, ...), custom_call_target="tpu_custom_call" | custom-call | flops 4294967296 | bytes 8388608 | tf_op jit(solution)/shard_map/ladder/pallas_call | solution.py:259
  43.8 1.0 code.5
  44.8 1.6 %collective-permute-start.10 = (s16[256,1152]{1,0:T(8,128)(2,1)S(1)}, s16[256,1152]{1,0:T(8,128)(2,1)S(1)}, u32[]{:S(2)}, u32[]{:S(2)}) collective-permute-start(s16[256,1152]{1,0:T(8,128)(2,1)S(1)} %get-tuple-element.73), channel_id=1, source_target_pairs={{0,2},{1,3},{2,0},{3,1},{4,6},{5,7},{6,4},{7,5},{8,10},{9,11},{10,... | collective-permute-start | bytes 1769480 | tf_op jit(solution)/shard_map/ppermute | solution.py:408
  46.4 2.6 %collective-permute-done.5.rest_2_ = bf16[2064,128]{1,0:T(8,128)(2,1)S(1)} collective-permute-done((bf16[2064,128]{1,0:T(8,128)(2,1)S(1)}, bf16[2064,128]{1,0:T(8,128)(2,1)S(1)}, u32[]{:S(2)}, u32[]{:S(2)}) %collective-permute-start.5) | collective-permute-done | bytes 528416 | tf_op jit(solution)/shard_map/ppermute | solution.py:431
  49.0 1.3 collective-permute-done.6.rest_3_
  50.3 1.5 %collective-permute-start.8 = (bf16[2064,128]{1,0:T(8,128)(2,1)S(1)}, bf16[2064,128]{1,0:T(8,128)(2,1)S(1)}, u32[]{:S(2)}, u32[]{:S(2)}) collective-permute-start(bf16[2064,128]{1,0:T(8,128)(2,1)S(1)} %collective-permute-done.5.rest_2_), channel_id=1, source_target_pairs={{0,8},{8,16},{16,24},{24,28},{28,20},{20,12},{12,4},{4,0},{1,9},{9... | collective-permute-start | bytes 1585160 | tf_op jit(solution)/shard_map/ppermute | solution.py:431
  52.3 7.2 %ladder.9 = f32[256,1024]{1,0:T(8,128)S(1)} custom-call(s32[397]{0:T(512)S(1)} %copy-done.13, bf16[2048,8192]{1,0:T(8,128)(2,1)} %int_ref.13, bf16[2064,128]{1,0:T(8,128)(2,1)S(1)} %collective-permute-done.3.rest_0_, bf16[2064,128]{1,0:T(8,128)(2,1)S(1)} %collective-permute-done.4.rest_1_, bf16[2064,128]{1,0:T(8,128)(2,1)S(1)} %collective-permute-done.5.rest_2_, ...), custom_call_target="tpu_custom_call" | custom-call | flops 4294967296 | bytes 8388608 | tf_op jit(solution)/shard_map/ladder/pallas_call | solution.py:259
  60.9 2.8 %collective-permute-done.8.rest_0_ = bf16[2064,128]{1,0:T(8,128)(2,1)S(1)} collective-permute-done((bf16[2064,128]{1,0:T(8,128)(2,1)S(1)}, bf16[2064,128]{1,0:T(8,128)(2,1)S(1)}, u32[]{:S(2)}, u32[]{:S(2)}) %collective-permute-start.8) | collective-permute-done | bytes 528416 | tf_op jit(solution)/shard_map/ppermute | solution.py:431
  63.6 1.2 collective-permute-done.9.rest_1_
  65.5 1.4 collective-permute-start.12
  66.9 7.4 %ladder.10.mine_ref = f32[256,1024]{1,0:T(8,128)S(1)} custom-call(s32[397]{0:T(512)S(1)} %copy-done.13, bf16[2048,8192]{1,0:T(8,128)(2,1)} %int_ref.13, bf16[2064,128]{1,0:T(8,128)(2,1)S(1)} %collective-permute-done.3.rest_0_, bf16[2064,128]{1,0:T(8,128)(2,1)S(1)} %collective-permute-done.4.rest_1_, bf16[2064,128]{1,0:T(8,128)(2,1)S(1)} %collective-permute-done.5.rest_2_, ...), custom_call_target="tpu_custom_call" | custom-call | flops 4294967296 | bytes 8388608 | tf_op jit(solution)/shard_map/ladder/pallas_call | solution.py:259
  74.3 1.0 code.6
  75.3 4.0 %collective-permute-done.11.rest_2_ = bf16[2064,128]{1,0:T(8,128)(2,1)S(1)} collective-permute-done((bf16[2064,128]{1,0:T(8,128)(2,1)S(1)}, bf16[2064,128]{1,0:T(8,128)(2,1)S(1)}, u32[]{:S(2)}, u32[]{:S(2)}) %collective-permute-start.11) | collective-permute-done | bytes 528416 | tf_op jit(solution)/shard_map/ppermute | solution.py:431
  79.6 1.5 %collective-permute-start.16 = (s16[256,1152]{1,0:T(8,128)(2,1)S(1)}, s16[256,1152]{1,0:T(8,128)(2,1)S(1)}, u32[]{:S(2)}, u32[]{:S(2)}) collective-permute-start(s16[256,1152]{1,0:T(8,128)(2,1)S(1)} %get-tuple-element.83), channel_id=1, source_target_pairs={{0,2},{1,3},{2,0},{3,1},{4,6},{5,7},{6,4},{7,5},{8,10},{9,11},{10,... | collective-permute-start | bytes 1769480 | tf_op jit(solution)/shard_map/ppermute | solution.py:408
  81.7 1.4 collective-permute-start.15
  83.1 11.6 %ladder.11 = (f32[256,1024]{1,0:T(8,128)S(1)}, f32[256,1024]{1,0:T(8,128)S(1)}) custom-call(s32[397]{0:T(512)S(1)} %copy-done.13, bf16[2048,8192]{1,0:T(8,128)(2,1)} %int_ref.13, bf16[2064,128]{1,0:T(8,128)(2,1)S(1)} %collective-permute-done.8.rest_0_, bf16[2064,128]{1,0:T(8,128)(2,1)S(1)} %collective-permute-done.9.rest_1_, ...), custom_call_target="tpu_custom_call" | custom-call | flops 8589934592 | bytes 16777216 | tf_op jit(solution)/shard_map/ladder/pallas_call | solution.py:259
  94.9 2.6 %collective-permute-done.19.got_ref = f32[256,1024]{1,0:T(8,128)S(1)} collective-permute-done((f32[256,1024]{1,0:T(8,128)S(1)}, f32[256,1024]{1,0:T(8,128)S(1)}, u32[]{:S(2)}, u32[]{:S(2)}) %collective-permute-start.19) | collective-permute-done | bytes 1048608 | tf_op jit(solution)/shard_map/ppermute | solution.py:441
  97.6 0.9 code.7
  98.5 1.0 collective-permute-start.20
  100.1 1.4 collective-permute-start.18
  101.5 11.4 %ladder.12 = (f32[128,1024]{1,0:T(8,128)S(1)}, f32[128,1024]{1,0:T(8,128)S(1)}) custom-call(s32[397]{0:T(512)S(1)} %copy-done.13, bf16[2048,8192]{1,0:T(8,128)(2,1)} %int_ref.13, bf16[2064,128]{1,0:T(8,128)(2,1)S(1)} %collective-permute-done.14.rest_0_, bf16[2064,128]{1,0:T(8,128)(2,1)S(1)} %collective-permute-done.15.rest_1_), custom_call_target="tpu_custom_call" | custom-call | flops 4294967296 | bytes 16777216 | tf_op jit(solution)/shard_map/ladder/pallas_call | solution.py:259
  113.0 1.0 collective-permute-done.20.rest_6_
  114.0 1.9 %collective-permute-done.21.got_ref = f32[128,1024]{1,0:T(8,128)S(1)} collective-permute-done((f32[128,1024]{1,0:T(8,128)S(1)}, f32[128,1024]{1,0:T(8,128)S(1)}, u32[]{:S(2)}, u32[]{:S(2)}) %collective-permute-start.21) | collective-permute-done | bytes 524320 | tf_op jit(solution)/shard_map/ppermute | solution.py:447
  117.2 0.9 collective-permute-start.22
  118.2 11.7 %ladder.13 = (f32[128,1024]{1,0:T(8,128)S(1)}, f32[128,1024]{1,0:T(8,128)S(1)}) custom-call(s32[397]{0:T(512)S(1)} %copy-done.13, bf16[2048,8192]{1,0:T(8,128)(2,1)} %int_ref.13, bf16[2064,128]{1,0:T(8,128)(2,1)S(1)} %collective-permute-done.17.rest_0_, bf16[2064,128]{1,0:T(8,128)(2,1)S(1)} %collective-permute-done.18.rest_1_), custom_call_target="tpu_custom_call" | custom-call | flops 4294967296 | bytes 16777216 | tf_op jit(solution)/shard_map/ladder/pallas_call | solution.py:259
  130.7 1.5 %collective-permute-done.23.got_ref = f32[128,1024]{1,0:T(8,128)S(1)} collective-permute-done((f32[128,1024]{1,0:T(8,128)S(1)}, f32[128,1024]{1,0:T(8,128)S(1)}, u32[]{:S(2)}, u32[]{:S(2)}) %collective-permute-start.23) | collective-permute-done | bytes 524320 | tf_op jit(solution)/shard_map/ppermute | solution.py:467
  132.3 1.2 code.9
  135.1 1.1 copy-done.2
  136.2 1.1 copy-done.4
  137.2 1.1 copy-done.6
  138.3 1.0 copy-done.8
  139.4 1.0 copy-done.12
  140.3 2.3 %final.2.rest_2_ = bf16[2,256,1024]{2,1,0:T(8,128)(2,1)S(1)} custom-call(s32[15]{0:T(128)S(1)} %dynamic-slice_bitcast_fusion.src_ref, s32[2]{0:T(128)S(1)} %pad_add_fusion.place_ref, f32[2,256,1]{2,1,0:T(8,128)S(1)} %copy.10.occ_ref, f32[1,1024]{1,0:T(1,128)S(1)} %bitcast.13, f32[256,1024]{1,0:T(8,128)S(1)} %get-tuple-element.103.rest_0_, ...), custom_call_target="tpu_custom_call" | custom-call | tf_op jit(solution)/shard_map/final/pallas_call | solution.py:361
  142.6 1.3 collective-permute-done.24.rest_1_
  143.9 1.4 final.3
  145.5 1.9 %collective-permute-done.25 = bf16[256,1024]{1,0:T(8,128)(2,1)S(1)} collective-permute-done((bf16[256,1024]{1,0:T(8,128)(2,1)S(1)}, bf16[256,1024]{1,0:T(8,128)(2,1)S(1)}, u32[]{:S(2)}, u32[]{:S(2)}) %collective-permute-start.25) | collective-permute-done | bytes 524320 | tf_op jit(solution)/shard_map/ppermute | solution.py:470
  147.4 1.4 maximum_select_fusion
  (61 shorter events, 11.1 us)
Async XLA Ops:
  0.0 1.6 %copy-start = (bf16[128,8192]{1,0:T(8,128)(2,1)S(1)}, bf16[128,8192]{1,0:T(8,128)(2,1)}, u32[]{:S(2)}) copy-start(bf16[128,8192]{1,0:T(8,128)(2,1)} %amp_ref.1) | copy-start | bytes 6291460
  1.6 0.7 copy-start.14
  2.3 5.0 %copy-start.16 = (f32[256]{0:T(256)S(1)}, f32[256]{0:T(256)}, u32[]{:S(2)}) copy-start(f32[256]{0:T(256)} %param.11) | copy-start | bytes 3076
  2.3 8.6 %copy-start.15 = (f32[2048]{0:T(1024)S(1)}, f32[2048]{0:T(1024)}, u32[]{:S(2)}) copy-start(f32[2048]{0:T(1024)} %param.12) | copy-start | bytes 24580
  4.2 15.0 %collective-permute-start = (bf16[2064,128]{1,0:T(8,128)(2,1)S(1)}, bf16[2064,128]{1,0:T(8,128)(2,1)S(1)}, u32[]{:S(2)}, u32[]{:S(2)}) collective-permute-start(bf16[2064,128]{1,0:T(8,128)(2,1)S(1)} %get-tuple-element.58.rest_0_), channel_id=1, source_target_pairs={{0,8},{8,16},{16,24},{24,28},{28,20},{20,12},{12,4},{4,0},{1,9},{9... | collective-permute-start | bytes 1585160 | tf_op jit(solution)/shard_map/ppermute | solution.py:431
  7.2 13.5 %collective-permute-start.1 = (bf16[2064,128]{1,0:T(8,128)(2,1)S(1)}, bf16[2064,128]{1,0:T(8,128)(2,1)S(1)}, u32[]{:S(2)}, u32[]{:S(2)}) collective-permute-start(bf16[2064,128]{1,0:T(8,128)(2,1)S(1)} %get-tuple-element.59.rest_1_), channel_id=1, source_target_pairs={{8,0},{16,8},{24,16},{28,24},{20,28},{12,20},{4,12},{0,4},{9,1},{1... | collective-permute-start | bytes 1585160 | tf_op jit(solution)/shard_map/ppermute | solution.py:431
  7.3 3.6 %collective-permute-start.2 = (f32[256]{0:T(256)S(1)}, f32[256]{0:T(256)S(1)}, u32[]{:S(2)}, u32[]{:S(2)}) collective-permute-start(f32[256]{0:T(256)S(1)} %copy-done.16), channel_id=1, source_target_pairs={{0,1},{1,0},{2,3},{3,2},{4,5},{5,4},{6,7},{7,6},{8,9},{9,8},{10,11... | collective-permute-start | bytes 3080 | tf_op jit(solution)/shard_map/ppermute | solution.py:392
  20.7 12.6 %collective-permute-start.3 = (bf16[2064,128]{1,0:T(8,128)(2,1)S(1)}, bf16[2064,128]{1,0:T(8,128)(2,1)S(1)}, u32[]{:S(2)}, u32[]{:S(2)}) collective-permute-start(bf16[2064,128]{1,0:T(8,128)(2,1)S(1)} %collective-permute-done.rest_2_), channel_id=1, source_target_pairs={{0,8},{8,16},{16,24},{24,28},{28,20},{20,12},{12,4},{4,0},{1,9},{9... | collective-permute-start | bytes 1585160 | tf_op jit(solution)/shard_map/ppermute | solution.py:431
  22.3 12.3 %collective-permute-start.4 = (bf16[2064,128]{1,0:T(8,128)(2,1)S(1)}, bf16[2064,128]{1,0:T(8,128)(2,1)S(1)}, u32[]{:S(2)}, u32[]{:S(2)}) collective-permute-start(bf16[2064,128]{1,0:T(8,128)(2,1)S(1)} %collective-permute-done.1.rest_3_), channel_id=1, source_target_pairs={{8,0},{16,8},{24,16},{28,24},{20,28},{12,20},{4,12},{0,4},{9,1},{1... | collective-permute-start | bytes 1585160 | tf_op jit(solution)/shard_map/ppermute | solution.py:431
  22.7 0.7 copy-start.13
  34.6 9.2 %collective-permute-start.7 = (f32[256,1024]{1,0:T(8,128)S(1)}, f32[256,1024]{1,0:T(8,128)S(1)}, u32[]{:S(2)}, u32[]{:S(2)}) collective-permute-start(f32[256,1024]{1,0:T(8,128)S(1)} %ladder.7), channel_id=1, source_target_pairs={{0,1},{1,0},{2,3},{3,2},{4,5},{5,4},{6,7},{7,6},{8,9},{9,8},{10,11... | collective-permute-start | bytes 3145736 | tf_op jit(solution)/shard_map/ppermute | solution.py:452
  34.6 14.4 %collective-permute-start.5 = (bf16[2064,128]{1,0:T(8,128)(2,1)S(1)}, bf16[2064,128]{1,0:T(8,128)(2,1)S(1)}, u32[]{:S(2)}, u32[]{:S(2)}) collective-permute-start(bf16[2064,128]{1,0:T(8,128)(2,1)S(1)} %collective-permute-done.3.rest_0_), channel_id=1, source_target_pairs={{0,8},{8,16},{16,24},{24,28},{28,20},{20,12},{12,4},{4,0},{1,9},{9... | collective-permute-start | bytes 1585160 | tf_op jit(solution)/shard_map/ppermute | solution.py:431
  36.2 14.1 %collective-permute-start.6 = (bf16[2064,128]{1,0:T(8,128)(2,1)S(1)}, bf16[2064,128]{1,0:T(8,128)(2,1)S(1)}, u32[]{:S(2)}, u32[]{:S(2)}) collective-permute-start(bf16[2064,128]{1,0:T(8,128)(2,1)S(1)} %collective-permute-done.4.rest_1_), channel_id=1, source_target_pairs={{8,0},{16,8},{24,16},{28,24},{20,28},{12,20},{4,12},{0,4},{9,1},{1... | collective-permute-start | bytes 1585160 | tf_op jit(solution)/shard_map/ppermute | solution.py:431
  44.8 15.2 %collective-permute-start.10 = (s16[256,1152]{1,0:T(8,128)(2,1)S(1)}, s16[256,1152]{1,0:T(8,128)(2,1)S(1)}, u32[]{:S(2)}, u32[]{:S(2)}) collective-permute-start(s16[256,1152]{1,0:T(8,128)(2,1)S(1)} %get-tuple-element.73), channel_id=1, source_target_pairs={{0,2},{1,3},{2,0},{3,1},{4,6},{5,7},{6,4},{7,5},{8,10},{9,11},{10,... | collective-permute-start | bytes 1769480 | tf_op jit(solution)/shard_map/ppermute | solution.py:408
  50.3 13.3 %collective-permute-start.8 = (bf16[2064,128]{1,0:T(8,128)(2,1)S(1)}, bf16[2064,128]{1,0:T(8,128)(2,1)S(1)}, u32[]{:S(2)}, u32[]{:S(2)}) collective-permute-start(bf16[2064,128]{1,0:T(8,128)(2,1)S(1)} %collective-permute-done.5.rest_2_), channel_id=1, source_target_pairs={{0,8},{8,16},{16,24},{24,28},{28,20},{20,12},{12,4},{4,0},{1,9},{9... | collective-permute-start | bytes 1585160 | tf_op jit(solution)/shard_map/ppermute | solution.py:431
  51.8 13.0 %collective-permute-start.9 = (bf16[2064,128]{1,0:T(8,128)(2,1)S(1)}, bf16[2064,128]{1,0:T(8,128)(2,1)S(1)}, u32[]{:S(2)}, u32[]{:S(2)}) collective-permute-start(bf16[2064,128]{1,0:T(8,128)(2,1)S(1)} %collective-permute-done.6.rest_3_), channel_id=1, source_target_pairs={{8,0},{16,8},{24,16},{28,24},{20,28},{12,20},{4,12},{0,4},{9,1},{1... | collective-permute-start | bytes 1585160 | tf_op jit(solution)/shard_map/ppermute | solution.py:431
  60.0 0.8 copy-start.1
  64.9 9.4 %collective-permute-start.13 = (f32[256,1024]{1,0:T(8,128)S(1)}, f32[256,1024]{1,0:T(8,128)S(1)}, u32[]{:S(2)}, u32[]{:S(2)}) collective-permute-start(f32[256,1024]{1,0:T(8,128)S(1)} %ladder.9), channel_id=1, source_target_pairs={{0,1},{1,0},{2,3},{3,2},{4,5},{5,4},{6,7},{7,6},{8,9},{9,8},{10,11... | collective-permute-start | bytes 3145736 | tf_op jit(solution)/shard_map/ppermute | solution.py:452
  64.9 14.4 %collective-permute-start.11 = (bf16[2064,128]{1,0:T(8,128)(2,1)S(1)}, bf16[2064,128]{1,0:T(8,128)(2,1)S(1)}, u32[]{:S(2)}, u32[]{:S(2)}) collective-permute-start(bf16[2064,128]{1,0:T(8,128)(2,1)S(1)} %collective-permute-done.8.rest_0_), channel_id=1, source_target_pairs={{0,8},{8,16},{16,24},{24,28},{28,20},{20,12},{12,4},{4,0},{1,9},{9... | collective-permute-start | bytes 1585160 | tf_op jit(solution)/shard_map/ppermute | solution.py:431
  65.5 14.1 %collective-permute-start.12 = (bf16[2064,128]{1,0:T(8,128)(2,1)S(1)}, bf16[2064,128]{1,0:T(8,128)(2,1)S(1)}, u32[]{:S(2)}, u32[]{:S(2)}) collective-permute-start(bf16[2064,128]{1,0:T(8,128)(2,1)S(1)} %collective-permute-done.9.rest_1_), channel_id=1, source_target_pairs={{8,0},{16,8},{24,16},{28,24},{20,28},{12,20},{4,12},{0,4},{9,1},{1... | collective-permute-start | bytes 1585160 | tf_op jit(solution)/shard_map/ppermute | solution.py:431
  79.6 15.2 %collective-permute-start.16 = (s16[256,1152]{1,0:T(8,128)(2,1)S(1)}, s16[256,1152]{1,0:T(8,128)(2,1)S(1)}, u32[]{:S(2)}, u32[]{:S(2)}) collective-permute-start(s16[256,1152]{1,0:T(8,128)(2,1)S(1)} %get-tuple-element.83), channel_id=1, source_target_pairs={{0,2},{1,3},{2,0},{3,1},{4,6},{5,7},{6,4},{7,5},{8,10},{9,11},{10,... | collective-permute-start | bytes 1769480 | tf_op jit(solution)/shard_map/ppermute | solution.py:408
  81.1 13.7 %collective-permute-start.14 = (bf16[2064,128]{1,0:T(8,128)(2,1)S(1)}, bf16[2064,128]{1,0:T(8,128)(2,1)S(1)}, u32[]{:S(2)}, u32[]{:S(2)}) collective-permute-start(bf16[2064,128]{1,0:T(8,128)(2,1)S(1)} %collective-permute-done.11.rest_2_), channel_id=1, source_target_pairs={{0,8},{8,16},{16,24},{24,28},{28,20},{20,12},{12,4},{4,0},{1,9},{9... | collective-permute-start | bytes 1585160 | tf_op jit(solution)/shard_map/ppermute | solution.py:431
  81.7 13.1 %collective-permute-start.15 = (bf16[2064,128]{1,0:T(8,128)(2,1)S(1)}, bf16[2064,128]{1,0:T(8,128)(2,1)S(1)}, u32[]{:S(2)}, u32[]{:S(2)}) collective-permute-start(bf16[2064,128]{1,0:T(8,128)(2,1)S(1)} %collective-permute-done.12.rest_3_), channel_id=1, source_target_pairs={{8,0},{16,8},{24,16},{28,24},{20,28},{12,20},{4,12},{0,4},{9,1},{1... | collective-permute-start | bytes 1585160 | tf_op jit(solution)/shard_map/ppermute | solution.py:431
  94.8 18.2 %copy-start.3 = (s16[256,1152]{1,0:T(8,128)(2,1)}, s16[256,1152]{1,0:T(8,128)(2,1)S(1)}, u32[]{:S(2)}) copy-start(s16[256,1152]{1,0:T(8,128)(2,1)S(1)} %collective-permute-done.16.rest_5_) | copy-start | bytes 1769476
  94.8 2.7 %collective-permute-start.19 = (f32[256,1024]{1,0:T(8,128)S(1)}, f32[256,1024]{1,0:T(8,128)S(1)}, u32[]{:S(2)}, u32[]{:S(2)}) collective-permute-start(f32[256,1024]{1,0:T(8,128)S(1)} %get-tuple-element.90), channel_id=1, source_target_pairs={{0,1},{1,0},{2,3},{3,2},{4,5},{5,4},{6,7},{7,6},{8,9},{9,8},{10,11... | collective-permute-start | bytes 3145736 | tf_op jit(solution)/shard_map/ppermute | solution.py:441
  98.5 15.4 %collective-permute-start.20 = (s16[256,1152]{1,0:T(8,128)(2,1)S(1)}, s16[256,1152]{1,0:T(8,128)(2,1)S(1)}, u32[]{:S(2)}, u32[]{:S(2)}) collective-permute-start(s16[256,1152]{1,0:T(8,128)(2,1)S(1)} %get-tuple-element.91), channel_id=1, source_target_pairs={{0,2},{1,3},{2,0},{3,1},{4,6},{5,7},{6,4},{7,5},{8,10},{9,11},{10,... | collective-permute-start | bytes 1769480 | tf_op jit(solution)/shard_map/ppermute | solution.py:408
  99.5 14.4 %collective-permute-start.17 = (bf16[2064,128]{1,0:T(8,128)(2,1)S(1)}, bf16[2064,128]{1,0:T(8,128)(2,1)S(1)}, u32[]{:S(2)}, u32[]{:S(2)}) collective-permute-start(bf16[2064,128]{1,0:T(8,128)(2,1)S(1)} %collective-permute-done.14.rest_0_), channel_id=1, source_target_pairs={{0,8},{8,16},{16,24},{24,28},{28,20},{20,12},{12,4},{4,0},{1,9},{9... | collective-permute-start | bytes 1585160 | tf_op jit(solution)/shard_map/ppermute | solution.py:431
  100.1 13.8 %collective-permute-start.18 = (bf16[2064,128]{1,0:T(8,128)(2,1)S(1)}, bf16[2064,128]{1,0:T(8,128)(2,1)S(1)}, u32[]{:S(2)}, u32[]{:S(2)}) collective-permute-start(bf16[2064,128]{1,0:T(8,128)(2,1)S(1)} %collective-permute-done.15.rest_1_), channel_id=1, source_target_pairs={{8,0},{16,8},{24,16},{28,24},{20,28},{12,20},{4,12},{0,4},{9,1},{1... | collective-permute-start | bytes 1585160 | tf_op jit(solution)/shard_map/ppermute | solution.py:431
  113.9 15.9 %copy-start.5 = (s16[256,1152]{1,0:T(8,128)(2,1)}, s16[256,1152]{1,0:T(8,128)(2,1)S(1)}, u32[]{:S(2)}) copy-start(s16[256,1152]{1,0:T(8,128)(2,1)S(1)} %collective-permute-done.20.rest_6_) | copy-start | bytes 1769476
  114.0 2.0 %collective-permute-start.21 = (f32[128,1024]{1,0:T(8,128)S(1)}, f32[128,1024]{1,0:T(8,128)S(1)}, u32[]{:S(2)}, u32[]{:S(2)}) collective-permute-start(f32[128,1024]{1,0:T(8,128)S(1)} %get-tuple-element.98), channel_id=1, source_target_pairs={{0,1},{1,0},{2,3},{3,2},{4,5},{5,4},{6,7},{7,6},{8,9},{9,8},{10,11... | collective-permute-start | bytes 1572872 | tf_op jit(solution)/shard_map/ppermute | solution.py:447
  116.4 0.8 copy-start.7
  117.2 12.6 %collective-permute-start.22 = (s16[128,1152]{1,0:T(8,128)(2,1)S(1)}, s16[128,1152]{1,0:T(8,128)(2,1)S(1)}, u32[]{:S(2)}, u32[]{:S(2)}) collective-permute-start(s16[128,1152]{1,0:T(8,128)(2,1)S(1)} %get-tuple-element.99), channel_id=1, source_target_pairs={{0,2},{1,3},{2,0},{3,1},{4,6},{5,7},{6,4},{7,5},{8,10},{9,11},{10,... | collective-permute-start | bytes 884744 | tf_op jit(solution)/shard_map/ppermute | solution.py:408
  129.9 4.4 %copy-start.11 = (s16[128,1152]{1,0:T(8,128)(2,1)}, s16[128,1152]{1,0:T(8,128)(2,1)S(1)}, u32[]{:S(2)}) copy-start(s16[128,1152]{1,0:T(8,128)(2,1)S(1)} %collective-permute-done.22.rest_7_) | copy-start | bytes 884740
  129.9 2.4 %collective-permute-start.23 = (f32[128,1024]{1,0:T(8,128)S(1)}, f32[128,1024]{1,0:T(8,128)S(1)}, u32[]{:S(2)}, u32[]{:S(2)}) collective-permute-start(f32[128,1024]{1,0:T(8,128)S(1)} %get-tuple-element.100), channel_id=1, source_target_pairs={{0,1},{1,0},{2,3},{3,2},{4,5},{5,4},{6,7},{7,6},{8,9},{9,8},{10,11... | collective-permute-start | bytes 1572872 | tf_op jit(solution)/shard_map/ppermute | solution.py:467
  133.5 0.8 copy-start.9
  134.3 9.6 %collective-permute-start.24 = (s16[128,1152]{1,0:T(8,128)(2,1)}, s16[128,1152]{1,0:T(8,128)(2,1)}, u32[]{:S(2)}, u32[]{:S(2)}) collective-permute-start(s16[128,1152]{1,0:T(8,128)(2,1)} %get-tuple-element.102), channel_id=1, source_target_pairs={{0,2},{1,3},{2,0},{3,1},{4,6},{5,7},{6,4},{7,5},{8,10},{9,11},{10,... | collective-permute-start | bytes 884744 | tf_op jit(solution)/shard_map/ppermute | solution.py:408
  135.1 1.1 copy-start.2
  136.2 1.1 copy-start.4
  137.2 1.1 copy-start.6
  138.3 1.0 copy-start.8
  139.4 1.0 copy-start.12
  140.3 3.6 %copy-start.10 = (f32[128,1024]{1,0:T(8,128)S(1)}, f32[128,1024]{1,0:T(8,128)}, u32[]{:S(2)}) copy-start(f32[128,1024]{1,0:T(8,128)} %copy-done.9) | copy-start | bytes 1572868
  145.4 2.0 %collective-permute-start.25 = (bf16[256,1024]{1,0:T(8,128)(2,1)S(1)}, bf16[256,1024]{1,0:T(8,128)(2,1)S(1)}, u32[]{:S(2)}, u32[]{:S(2)}) collective-permute-start(bf16[256,1024]{1,0:T(8,128)(2,1)S(1)} %get-tuple-element.112), channel_id=1, source_target_pairs={{0,1},{1,0},{2,3},{3,2},{4,5},{5,4},{6,7},{7,6},{8,9},{9,8},{10,11... | collective-permute-start | bytes 1572872 | tf_op jit(solution)/shard_map/ppermute | solution.py:470
